TPU v7x, 512 devices: a whole 4x4x16 slice. The times are simulated.
512 devices in a mesh: gx: 16 (over x, z_hi), gy: 8 (over y, core), gz: 4 (over z_lo).
Axes of the slice: x: 4, y: 4, z: 16 (z_hi: 4, z_lo: 4; z = z_hi * 4 + z_lo), core: 2. Of those that a mesh axis runs over, the one named last changes fastest.
Arguments:
- velocity: float32 [3, 256, 128, 512], P(None, 'gx', 'gy', 'gz'), may hold values from -6 to 6
- stress: float32 [6, 256, 128, 512], P(None, 'gx', 'gy', 'gz'), may hold values from -6 to 6
- memory: float32 [6, 256, 128, 512], P(None, 'gx', 'gy', 'gz'), may hold values from -4 to 4
- lame_lambda: float32 [256, 128, 512], P('gx', 'gy', 'gz'), may hold values from 0.5 to 1.5
- shear_modulus: float32 [256, 128, 512], P('gx', 'gy', 'gz'), may hold values from 0.3 to 1
- buoyancy: float32 [256, 128, 512], P('gx', 'gy', 'gz'), may hold values from 0.5 to 1.5
- anelastic_weight: float32 [256, 128, 512], P('gx', 'gy', 'gz'), may hold values from 0.2 to 1
- decay_table: float32 [8], replicated, may hold values from 0.3 to 0.95
- mech_index: int32 [256, 128, 512], P('gx', 'gy', 'gz'), may hold values from 0 to 7
- surface_depth: int32 [256, 128], P('gx', 'gy'), may hold values from 0 to 3
Outputs:
- velocity_out: float32 [3, 256, 128, 512], P(None, 'gx', 'gy', 'gz')
- stress_out: float32 [6, 256, 128, 512], P(None, 'gx', 'gy', 'gz')
- memory_out: float32 [6, 256, 128, 512], P(None, 'gx', 'gy', 'gz')
All inputs are finite; a program needn't handle non-finite values.
Results may differ from a plain program's by a relative error of at most 0.0003.
Values sent between devices are 32-bit elements; how exact they have to be, the bound alone decides.
No kernel may reach another device: no remote copies, remote signals or barrier semaphores. Data moves between devices by JAX's collectives and lax.ppermute only.
A program may use at most 128 MiB of HBM per device.

v0:
```python
import jax
import jax.numpy as jnp
from jax import lax
from jax.sharding import PartitionSpec as P

STEPS = 2


COEF_NEAR = 9.0 / 8.0
COEF_FAR = -1.0 / 24.0
TIME_STEP = 0.2


def extended(value, sides, width):
    for axis, dim in sides:
        peers, length = (lax.axis_size(axis), value.shape[dim])
        up = [(i, (i + 1) % peers) for i in range(peers - 1)]
        down = [(j, i) for i, j in up]
        last = lax.slice_in_dim(value, length - width, length, axis=dim)
        leading = lax.slice_in_dim(value, 0, width, axis=dim)
        before = lax.ppermute(last, axis, up)
        after = lax.ppermute(leading, axis, down)
        value = jnp.concatenate([before, value, after], axis=dim)
    return value


def along(padded, axis, offset):
    count = padded.shape[axis] - 4
    return lax.slice_in_dim(padded, 2 + offset, 2 + offset + count, axis=axis)


def forward(padded, axis):
    return COEF_NEAR * (along(padded, axis, 1) - along(padded, axis, 0)) + COEF_FAR * (
        along(padded, axis, 2) - along(padded, axis, -1)
    )


def backward(padded, axis):
    return COEF_NEAR * (along(padded, axis, 0) - along(padded, axis, -1)) + COEF_FAR * (
        along(padded, axis, 1) - along(padded, axis, -2)
    )


def crop_other(padded, axis):
    for other in range(3):
        if other != axis:
            padded = lax.slice_in_dim(padded, 2, padded.shape[other] - 2, axis=other)
    return padded


def velocity_update(velocity, buoyancy, fetch):
    scale = TIME_STEP * buoyancy
    vel_x = velocity[0] + scale * (
        forward(fetch(0, 0), 0) + backward(fetch(3, 1), 1) + backward(fetch(4, 2), 2)
    )
    vel_y = velocity[1] + scale * (
        backward(fetch(3, 0), 0) + forward(fetch(1, 1), 1) + backward(fetch(5, 2), 2)
    )
    vel_z = velocity[2] + scale * (
        backward(fetch(4, 0), 0) + backward(fetch(5, 1), 1) + forward(fetch(2, 2), 2)
    )
    return jnp.stack([vel_x, vel_y, vel_z])


def stress_update(
    padded_vel,
    stress,
    memory,
    lame_lambda,
    shear_modulus,
    anelastic_weight,
    decay_cell,
    air,
    surface_cell,
):

    def fetch(comp, axis):
        return crop_other(padded_vel[comp], axis)

    strain_xx = backward(fetch(0, 0), 0)
    strain_yy = backward(fetch(1, 1), 1)
    strain_zz = backward(fetch(2, 2), 2)
    strain_xy = forward(fetch(0, 1), 1) + forward(fetch(1, 0), 0)
    strain_xz = forward(fetch(0, 2), 2) + forward(fetch(2, 0), 0)
    strain_yz = forward(fetch(1, 2), 2) + forward(fetch(2, 1), 1)
    volume = lame_lambda * (strain_xx + strain_yy + strain_zz)
    rates = jnp.stack(
        [
            volume + 2.0 * shear_modulus * strain_xx,
            volume + 2.0 * shear_modulus * strain_yy,
            volume + 2.0 * shear_modulus * strain_zz,
            shear_modulus * strain_xy,
            shear_modulus * strain_xz,
            shear_modulus * strain_yz,
        ]
    )
    memory_new = decay_cell * memory + (1.0 - decay_cell) * anelastic_weight * rates
    stress_new = stress + TIME_STEP * (rates - memory_new)
    keep_all = 1.0 - air
    keep_vertical = keep_all * (1.0 - surface_cell)
    factors = jnp.stack([keep_all, keep_all, keep_vertical, keep_all, keep_vertical, keep_vertical])
    return (stress_new * factors, memory_new)


def lookup_decay(mech_index, decay_table):
    levels = jnp.arange(decay_table.shape[0], dtype=jnp.int32)
    hits = mech_index[None] == levels[:, None, None, None]
    return jnp.sum(jnp.where(hits, decay_table[:, None, None, None], jnp.float32(0.0)), axis=0)


def shards(
    velocity,
    stress,
    memory,
    lame_lambda,
    shear_modulus,
    buoyancy,
    anelastic_weight,
    decay_table,
    mech_index,
    surface_depth,
):
    decay_cell = lookup_decay(mech_index, decay_table)
    depth_cells = lame_lambda.shape[2]
    depth_index = lax.axis_index("gz") * depth_cells + lax.broadcasted_iota(
        jnp.int32, (1, 1, depth_cells), 2
    )
    top = surface_depth[:, :, None]
    air = (depth_index < top).astype(jnp.float32)
    surface_cell = (depth_index == top).astype(jnp.float32)
    for step_index in range(STEPS):
        padded_stress = extended(stress, (("gx", 1), ("gy", 2), ("gz", 3)), 2)
        velocity = velocity_update(
            velocity, buoyancy, lambda comp, axis: crop_other(padded_stress[comp], axis)
        )
        padded_vel = extended(velocity, (("gx", 1), ("gy", 2), ("gz", 3)), 2)
        stress, memory = stress_update(
            padded_vel,
            stress,
            memory,
            lame_lambda,
            shear_modulus,
            anelastic_weight,
            decay_cell,
            air,
            surface_cell,
        )
    return (velocity, stress, memory)


def solution(mesh):
    placed = (
        P(None, "gx", "gy", "gz"),
        P(None, "gx", "gy", "gz"),
        P(None, "gx", "gy", "gz"),
        P("gx", "gy", "gz"),
        P("gx", "gy", "gz"),
        P("gx", "gy", "gz"),
        P("gx", "gy", "gz"),
        P(),
        P("gx", "gy", "gz"),
        P("gx", "gy"),
    )
    return jax.shard_map(
        shards,
        mesh=mesh,
        in_specs=placed,
        out_specs=(P(None, "gx", "gy", "gz"), P(None, "gx", "gy", "gz"), P(None, "gx", "gy", "gz")),
        check_vma=False,
    )
```

profile of v0, /device:TPU:1, one launch (start us, length us, event | category | flops | bytes accessed | tf_op | source)
XLA Modules:
  0.0 195.3 jit_solution(11114318099680005243)
XLA Ops:
  3.0 10.3 %collective-permute-start = (f32[6,2,16,128]{3,2,1,0:T(8,128)S(1)}, f32[6,2,16,128]{3,2,1,0:T(8,128)S(1)}, u32[]{:S(2)}, u32[]{:S(2)}) collective-permute-start(f32[6,2,16,128]{3,2,1,0:T(8,128)S(1)} %get-tuple-element.55), channel_id=1, source_target_pairs={{0,32},{32,64},{64,96},{96,128},{128,160},{160,192},{192,224},{224... | collective-permute-start | bytes 294920 | tf_op jit(solution)/shard_map/ppermute | solution.py:21
  15.6 9.0 %collective-permute-start.2 = (f32[6,20,2,128]{3,2,1,0:T(2,128)S(1)}, f32[6,20,2,128]{3,2,1,0:T(2,128)S(1)}, u32[]{:S(2)}, u32[]{:S(2)}) collective-permute-start(f32[6,20,2,128]{3,2,1,0:T(2,128)S(1)} %get-tuple-element.50), channel_id=1, source_target_pairs={{0,4},{4,8},{8,12},{12,16},{16,20},{20,24},{24,28},{1,5},{5,9},{9,... | collective-permute-start | bytes 368648 | tf_op jit(solution)/shard_map/ppermute | solution.py:21
  27.3 3.5 %collective-permute-done.3 = f32[6,20,2,128]{3,2,1,0:T(2,128)S(1)} collective-permute-done((f32[6,20,2,128]{3,2,1,0:T(2,128)S(1)}, f32[6,20,2,128]{3,2,1,0:T(2,128)S(1)}, u32[]{:S(2)}, u32[]{:S(2)}) %collective-permute-start.3) | collective-permute-done | bytes 122912 | tf_op jit(solution)/shard_map/ppermute | solution.py:22
  35.1 4.0 %collective-permute-start.4 = (f32[6,20,20,2]{2,3,1,0:T(2,128)S(1)}, f32[6,20,20,2]{2,3,1,0:T(2,128)S(1)}, u32[]{:S(2)}, u32[]{:S(2)}) collective-permute-start(f32[6,20,20,2]{2,3,1,0:T(2,128)S(1)} %copy-done.18), channel_id=1, source_target_pairs={{0,1},{1,2},{2,3},{4,5},{5,6},{6,7},{8,9},{9,10},{10,11},{12,13},{... | collective-permute-start | bytes 57608 | tf_op jit(solution)/shard_map/ppermute | solution.py:21
  43.6 2.9 %pad_maximum_fusion = f32[6,20,20,132]{3,2,1,0:T(8,128)S(1)} fusion(f32[6,20,20,2]{3,2,1,0:T(8,128)S(1)} %copy.64, f32[6,20,2,128]{3,2,1,0:T(2,128)S(1)} %collective-permute-done.3, f32[6,20,16,128]{3,2,1,0:T(8,128)} %copy-done.1, f32[6,20,2,128]{3,2,1,0:T(2,128)S(1)} %collective-permute-done.2, f32[6,20,20,2]{3,2,1,0:T(8,128)S(1)} %copy.63), kind=kLoop, calls=%fused_computation | loop fusion | flops 1267200 | bytes 2534400 | tf_op jit(solution)/shard_map/concatenate | solution.py:23
  49.1 9.9 %collective-permute-start.6 = (f32[3,2,16,128]{3,2,1,0:T(8,128)S(1)}, f32[3,2,16,128]{3,2,1,0:T(8,128)S(1)}, u32[]{:S(2)}, u32[]{:S(2)}) collective-permute-start(f32[3,2,16,128]{3,2,1,0:T(8,128)S(1)} %get-tuple-element.66), channel_id=1, source_target_pairs={{0,32},{32,64},{64,96},{96,128},{128,160},{160,192},{192,224},{224... | collective-permute-start | bytes 147464 | tf_op jit(solution)/shard_map/ppermute | solution.py:21
  60.4 11.2 %collective-permute-done.7 = f32[3,2,16,128]{3,2,1,0:T(8,128)S(1)} collective-permute-done((f32[3,2,16,128]{3,2,1,0:T(8,128)S(1)}, f32[3,2,16,128]{3,2,1,0:T(8,128)S(1)}, u32[]{:S(2)}, u32[]{:S(2)}) %collective-permute-start.7) | collective-permute-done | bytes 49184 | tf_op jit(solution)/shard_map/ppermute | solution.py:22
  73.6 2.4 %collective-permute-start.9 = (f32[3,20,2,128]{3,2,1,0:T(2,128)S(1)}, f32[3,20,2,128]{3,2,1,0:T(2,128)S(1)}, u32[]{:S(2)}, u32[]{:S(2)}) collective-permute-start(f32[3,20,2,128]{3,2,1,0:T(2,128)S(1)} %get-tuple-element.63), channel_id=1, source_target_pairs={{4,0},{8,4},{12,8},{16,12},{20,16},{24,20},{28,24},{5,1},{9,5},{13... | collective-permute-start | bytes 184328 | tf_op jit(solution)/shard_map/ppermute | solution.py:22
  76.1 3.0 %collective-permute-done.9 = f32[3,20,2,128]{3,2,1,0:T(2,128)S(1)} collective-permute-done((f32[3,20,2,128]{3,2,1,0:T(2,128)S(1)}, f32[3,20,2,128]{3,2,1,0:T(2,128)S(1)}, u32[]{:S(2)}, u32[]{:S(2)}) %collective-permute-start.9) | collective-permute-done | bytes 61472 | tf_op jit(solution)/shard_map/ppermute | solution.py:22
  81.7 6.0 %collective-permute-start.10 = (f32[3,20,20,2]{2,3,1,0:T(2,128)S(1)}, f32[3,20,20,2]{2,3,1,0:T(2,128)S(1)}, u32[]{:S(2)}, u32[]{:S(2)}) collective-permute-start(f32[3,20,20,2]{2,3,1,0:T(2,128)S(1)} %copy.79), channel_id=1, source_target_pairs={{0,1},{1,2},{2,3},{4,5},{5,6},{6,7},{8,9},{9,10},{10,11},{12,13},{... | collective-permute-start | bytes 28808 | tf_op jit(solution)/shard_map/ppermute | solution.py:21
  94.4 8.5 %collective-permute-start.12 = (f32[6,2,16,128]{3,2,1,0:T(8,128)S(1)}, f32[6,2,16,128]{3,2,1,0:T(8,128)S(1)}, u32[]{:S(2)}, u32[]{:S(2)}) collective-permute-start(f32[6,2,16,128]{3,2,1,0:T(8,128)S(1)} %get-tuple-element.52), channel_id=1, source_target_pairs={{0,32},{32,64},{64,96},{96,128},{128,160},{160,192},{192,224},{224... | collective-permute-start | bytes 294920 | tf_op jit(solution)/shard_map/ppermute | solution.py:21
  104.8 11.5 %collective-permute-done.13 = f32[6,2,16,128]{3,2,1,0:T(8,128)S(1)} collective-permute-done((f32[6,2,16,128]{3,2,1,0:T(8,128)S(1)}, f32[6,2,16,128]{3,2,1,0:T(8,128)S(1)}, u32[]{:S(2)}, u32[]{:S(2)}) %collective-permute-start.13) | collective-permute-done | bytes 98336 | tf_op jit(solution)/shard_map/ppermute | solution.py:22
  116.3 5.0 %collective-permute-start.14 = (f32[6,20,2,128]{3,2,1,0:T(2,128)S(1)}, f32[6,20,2,128]{3,2,1,0:T(2,128)S(1)}, u32[]{:S(2)}, u32[]{:S(2)}) collective-permute-start(f32[6,20,2,128]{3,2,1,0:T(2,128)S(1)} %get-tuple-element.48), channel_id=1, source_target_pairs={{0,4},{4,8},{8,12},{12,16},{16,20},{20,24},{24,28},{1,5},{5,9},{9,... | collective-permute-start | bytes 368648 | tf_op jit(solution)/shard_map/ppermute | solution.py:21
  123.5 4.1 %collective-permute-done.15 = f32[6,20,2,128]{3,2,1,0:T(2,128)S(1)} collective-permute-done((f32[6,20,2,128]{3,2,1,0:T(2,128)S(1)}, f32[6,20,2,128]{3,2,1,0:T(2,128)S(1)}, u32[]{:S(2)}, u32[]{:S(2)}) %collective-permute-start.15) | collective-permute-done | bytes 122912 | tf_op jit(solution)/shard_map/ppermute | solution.py:22
  130.1 3.0 %copy.81 = f32[6,20,20,2]{2,1,3,0:T(8,128)} copy(f32[6,20,20,2]{3,2,1,0:T(8,128)} %get-tuple-element.38) | data formatting | bytes 38400
  133.0 5.2 %collective-permute-start.16 = (f32[6,20,20,2]{2,1,3,0:T(8,128)}, f32[6,20,20,2]{2,1,3,0:T(8,128)}, u32[]{:S(2)}, u32[]{:S(2)}) collective-permute-start(f32[6,20,20,2]{2,1,3,0:T(8,128)} %copy.81), channel_id=1, source_target_pairs={{0,1},{1,2},{2,3},{4,5},{5,6},{6,7},{8,9},{9,10},{10,11},{12,13},{... | collective-permute-start | bytes 57608 | tf_op jit(solution)/shard_map/ppermute | solution.py:21
  142.9 3.1 %collective-permute-done.17 = f32[6,20,20,2]{2,1,3,0:T(8,128)} collective-permute-done((f32[6,20,20,2]{2,1,3,0:T(8,128)}, f32[6,20,20,2]{2,1,3,0:T(8,128)}, u32[]{:S(2)}, u32[]{:S(2)}) %collective-permute-start.17) | collective-permute-done | bytes 19232 | tf_op jit(solution)/shard_map/ppermute | solution.py:22
  146.0 2.9 %copy.72 = f32[6,20,20,2]{3,2,1,0:T(8,128)} copy(f32[6,20,20,2]{2,1,3,0:T(8,128)} %collective-permute-done.17) | data formatting | bytes 38400 | tf_op jit(solution)/shard_map/ppermute | solution.py:22
  148.9 3.2 %pad_maximum_fusion.1 = f32[6,20,20,132]{3,2,1,0:T(8,128)S(1)} fusion(f32[6,20,20,2]{3,2,1,0:T(8,128)} %copy.72, f32[6,20,2,128]{3,2,1,0:T(2,128)} %copy-done.15, f32[6,2,16,128]{3,2,1,0:T(8,128)S(1)} %collective-permute-done.13, f32[6,16,16,128]{3,2,1,0:T(8,128)S(1)} %add_multiply_fusion.1, f32[6,2,16,128]{3,2,1,0:T(8,128)S(1)} %collective-permute-done.12, ...), kind=kLoop, calls=%fused_computation.1 | loop fusion | flops 1900800 | bytes 2534400 | tf_op jit(solution)/shard_map/concatenate | solution.py:23
  153.9 7.5 %collective-permute-start.18 = (f32[3,2,16,128]{3,2,1,0:T(8,128)S(1)}, f32[3,2,16,128]{3,2,1,0:T(8,128)S(1)}, u32[]{:S(2)}, u32[]{:S(2)}) collective-permute-start(f32[3,2,16,128]{3,2,1,0:T(8,128)S(1)} %get-tuple-element.64), channel_id=1, source_target_pairs={{0,32},{32,64},{64,96},{96,128},{128,160},{160,192},{192,224},{224... | collective-permute-start | bytes 147464 | tf_op jit(solution)/shard_map/ppermute | solution.py:21
  162.8 7.7 %collective-permute-done.19 = f32[3,2,16,128]{3,2,1,0:T(8,128)S(1)} collective-permute-done((f32[3,2,16,128]{3,2,1,0:T(8,128)S(1)}, f32[3,2,16,128]{3,2,1,0:T(8,128)S(1)}, u32[]{:S(2)}, u32[]{:S(2)}) %collective-permute-start.19) | collective-permute-done | bytes 49184 | tf_op jit(solution)/shard_map/ppermute | solution.py:22
  170.5 4.8 %collective-permute-start.20 = (f32[3,20,2,128]{3,2,1,0:T(2,128)S(1)}, f32[3,20,2,128]{3,2,1,0:T(2,128)S(1)}, u32[]{:S(2)}, u32[]{:S(2)}) collective-permute-start(f32[3,20,2,128]{3,2,1,0:T(2,128)S(1)} %get-tuple-element.60), channel_id=1, source_target_pairs={{0,4},{4,8},{8,12},{12,16},{16,20},{20,24},{24,28},{1,5},{5,9},{9,... | collective-permute-start | bytes 184328 | tf_op jit(solution)/shard_map/ppermute | solution.py:21
  177.3 3.6 %collective-permute-done.21 = f32[3,20,2,128]{3,2,1,0:T(2,128)S(1)} collective-permute-done((f32[3,20,2,128]{3,2,1,0:T(2,128)S(1)}, f32[3,20,2,128]{3,2,1,0:T(2,128)S(1)}, u32[]{:S(2)}, u32[]{:S(2)}) %collective-permute-start.21) | collective-permute-done | bytes 61472 | tf_op jit(solution)/shard_map/ppermute | solution.py:22
  185.4 3.4 %collective-permute-done.23 = f32[3,20,20,2]{2,1,3,0:T(8,128)} collective-permute-done((f32[3,20,20,2]{2,1,3,0:T(8,128)S(1)}, f32[3,20,20,2]{2,1,3,0:T(8,128)}, u32[]{:S(2)}, u32[]{:S(2)}) %collective-permute-start.23) | collective-permute-done | bytes 9632 | tf_op jit(solution)/shard_map/ppermute | solution.py:22
  (138 shorter events, 58.3 us)
Async XLA Ops:
  1.7 13.8 %collective-permute-start.1 = (f32[6,2,16,128]{3,2,1,0:T(8,128)S(1)}, f32[6,2,16,128]{3,2,1,0:T(8,128)S(1)}, u32[]{:S(2)}, u32[]{:S(2)}) collective-permute-start(f32[6,2,16,128]{3,2,1,0:T(8,128)S(1)} %get-tuple-element.54), channel_id=1, source_target_pairs={{32,0},{64,32},{96,64},{128,96},{160,128},{192,160},{224,192},{256... | collective-permute-start | bytes 294920 | tf_op jit(solution)/shard_map/ppermute | solution.py:22
  3.0 12.4 %collective-permute-start = (f32[6,2,16,128]{3,2,1,0:T(8,128)S(1)}, f32[6,2,16,128]{3,2,1,0:T(8,128)S(1)}, u32[]{:S(2)}, u32[]{:S(2)}) collective-permute-start(f32[6,2,16,128]{3,2,1,0:T(8,128)S(1)} %get-tuple-element.55), channel_id=1, source_target_pairs={{0,32},{32,64},{64,96},{96,128},{128,160},{160,192},{192,224},{224... | collective-permute-start | bytes 294920 | tf_op jit(solution)/shard_map/ppermute | solution.py:21
  15.6 11.7 %collective-permute-start.2 = (f32[6,20,2,128]{3,2,1,0:T(2,128)S(1)}, f32[6,20,2,128]{3,2,1,0:T(2,128)S(1)}, u32[]{:S(2)}, u32[]{:S(2)}) collective-permute-start(f32[6,20,2,128]{3,2,1,0:T(2,128)S(1)} %get-tuple-element.50), channel_id=1, source_target_pairs={{0,4},{4,8},{8,12},{12,16},{16,20},{20,24},{24,28},{1,5},{5,9},{9,... | collective-permute-start | bytes 368648 | tf_op jit(solution)/shard_map/ppermute | solution.py:21
  24.6 6.2 %collective-permute-start.3 = (f32[6,20,2,128]{3,2,1,0:T(2,128)S(1)}, f32[6,20,2,128]{3,2,1,0:T(2,128)S(1)}, u32[]{:S(2)}, u32[]{:S(2)}) collective-permute-start(f32[6,20,2,128]{3,2,1,0:T(2,128)S(1)} %get-tuple-element.51), channel_id=1, source_target_pairs={{4,0},{8,4},{12,8},{16,12},{20,16},{24,20},{28,24},{5,1},{9,5},{13... | collective-permute-start | bytes 368648 | tf_op jit(solution)/shard_map/ppermute | solution.py:22
  33.8 8.0 %collective-permute-start.5 = (f32[6,20,20,2]{2,3,1,0:T(2,128)S(1)}, f32[6,20,20,2]{2,3,1,0:T(2,128)}, u32[]{:S(2)}, u32[]{:S(2)}) collective-permute-start(f32[6,20,20,2]{2,3,1,0:T(2,128)S(1)} %copy.78), channel_id=1, source_target_pairs={{1,0},{2,1},{3,2},{5,4},{6,5},{7,6},{9,8},{10,9},{11,10},{13,12},{... | collective-permute-start | bytes 57608 | tf_op jit(solution)/shard_map/ppermute | solution.py:22
  35.1 5.8 %collective-permute-start.4 = (f32[6,20,20,2]{2,3,1,0:T(2,128)S(1)}, f32[6,20,20,2]{2,3,1,0:T(2,128)S(1)}, u32[]{:S(2)}, u32[]{:S(2)}) collective-permute-start(f32[6,20,20,2]{2,3,1,0:T(2,128)S(1)} %copy-done.18), channel_id=1, source_target_pairs={{0,1},{1,2},{2,3},{4,5},{5,6},{6,7},{8,9},{9,10},{10,11},{12,13},{... | collective-permute-start | bytes 57608 | tf_op jit(solution)/shard_map/ppermute | solution.py:21
  49.1 11.3 %collective-permute-start.6 = (f32[3,2,16,128]{3,2,1,0:T(8,128)S(1)}, f32[3,2,16,128]{3,2,1,0:T(8,128)S(1)}, u32[]{:S(2)}, u32[]{:S(2)}) collective-permute-start(f32[3,2,16,128]{3,2,1,0:T(8,128)S(1)} %get-tuple-element.66), channel_id=1, source_target_pairs={{0,32},{32,64},{64,96},{96,128},{128,160},{160,192},{192,224},{224... | collective-permute-start | bytes 147464 | tf_op jit(solution)/shard_map/ppermute | solution.py:21
  59.0 12.6 %collective-permute-start.7 = (f32[3,2,16,128]{3,2,1,0:T(8,128)S(1)}, f32[3,2,16,128]{3,2,1,0:T(8,128)S(1)}, u32[]{:S(2)}, u32[]{:S(2)}) collective-permute-start(f32[3,2,16,128]{3,2,1,0:T(8,128)S(1)} %get-tuple-element.67), channel_id=1, source_target_pairs={{32,0},{64,32},{96,64},{128,96},{160,128},{192,160},{224,192},{256... | collective-permute-start | bytes 147464 | tf_op jit(solution)/shard_map/ppermute | solution.py:22
  71.6 4.5 %collective-permute-start.8 = (f32[3,20,2,128]{3,2,1,0:T(2,128)S(1)}, f32[3,20,2,128]{3,2,1,0:T(2,128)S(1)}, u32[]{:S(2)}, u32[]{:S(2)}) collective-permute-start(f32[3,20,2,128]{3,2,1,0:T(2,128)S(1)} %get-tuple-element.62), channel_id=1, source_target_pairs={{0,4},{4,8},{8,12},{12,16},{16,20},{20,24},{24,28},{1,5},{5,9},{9,... | collective-permute-start | bytes 184328 | tf_op jit(solution)/shard_map/ppermute | solution.py:21
  73.6 5.5 %collective-permute-start.9 = (f32[3,20,2,128]{3,2,1,0:T(2,128)S(1)}, f32[3,20,2,128]{3,2,1,0:T(2,128)S(1)}, u32[]{:S(2)}, u32[]{:S(2)}) collective-permute-start(f32[3,20,2,128]{3,2,1,0:T(2,128)S(1)} %get-tuple-element.63), channel_id=1, source_target_pairs={{4,0},{8,4},{12,8},{16,12},{20,16},{24,20},{28,24},{5,1},{9,5},{13... | collective-permute-start | bytes 184328 | tf_op jit(solution)/shard_map/ppermute | solution.py:22
  80.4 9.0 %collective-permute-start.11 = (f32[3,20,20,2]{2,3,1,0:T(2,128)S(1)}, f32[3,20,20,2]{2,3,1,0:T(2,128)S(1)}, u32[]{:S(2)}, u32[]{:S(2)}) collective-permute-start(f32[3,20,20,2]{2,3,1,0:T(2,128)S(1)} %copy.80), channel_id=1, source_target_pairs={{1,0},{2,1},{3,2},{5,4},{6,5},{7,6},{9,8},{10,9},{11,10},{13,12},{... | collective-permute-start | bytes 28808 | tf_op jit(solution)/shard_map/ppermute | solution.py:22
  81.7 7.3 %collective-permute-start.10 = (f32[3,20,20,2]{2,3,1,0:T(2,128)S(1)}, f32[3,20,20,2]{2,3,1,0:T(2,128)S(1)}, u32[]{:S(2)}, u32[]{:S(2)}) collective-permute-start(f32[3,20,20,2]{2,3,1,0:T(2,128)S(1)} %copy.79), channel_id=1, source_target_pairs={{0,1},{1,2},{2,3},{4,5},{5,6},{6,7},{8,9},{9,10},{10,11},{12,13},{... | collective-permute-start | bytes 28808 | tf_op jit(solution)/shard_map/ppermute | solution.py:21
  94.4 10.3 %collective-permute-start.12 = (f32[6,2,16,128]{3,2,1,0:T(8,128)S(1)}, f32[6,2,16,128]{3,2,1,0:T(8,128)S(1)}, u32[]{:S(2)}, u32[]{:S(2)}) collective-permute-start(f32[6,2,16,128]{3,2,1,0:T(8,128)S(1)} %get-tuple-element.52), channel_id=1, source_target_pairs={{0,32},{32,64},{64,96},{96,128},{128,160},{160,192},{192,224},{224... | collective-permute-start | bytes 294920 | tf_op jit(solution)/shard_map/ppermute | solution.py:21
  103.0 13.3 %collective-permute-start.13 = (f32[6,2,16,128]{3,2,1,0:T(8,128)S(1)}, f32[6,2,16,128]{3,2,1,0:T(8,128)S(1)}, u32[]{:S(2)}, u32[]{:S(2)}) collective-permute-start(f32[6,2,16,128]{3,2,1,0:T(8,128)S(1)} %get-tuple-element.53), channel_id=1, source_target_pairs={{32,0},{64,32},{96,64},{128,96},{160,128},{192,160},{224,192},{256... | collective-permute-start | bytes 294920 | tf_op jit(solution)/shard_map/ppermute | solution.py:22
  116.3 7.1 %collective-permute-start.14 = (f32[6,20,2,128]{3,2,1,0:T(2,128)S(1)}, f32[6,20,2,128]{3,2,1,0:T(2,128)S(1)}, u32[]{:S(2)}, u32[]{:S(2)}) collective-permute-start(f32[6,20,2,128]{3,2,1,0:T(2,128)S(1)} %get-tuple-element.48), channel_id=1, source_target_pairs={{0,4},{4,8},{8,12},{12,16},{16,20},{20,24},{24,28},{1,5},{5,9},{9,... | collective-permute-start | bytes 368648 | tf_op jit(solution)/shard_map/ppermute | solution.py:21
  121.4 6.2 %collective-permute-start.15 = (f32[6,20,2,128]{3,2,1,0:T(2,128)S(1)}, f32[6,20,2,128]{3,2,1,0:T(2,128)S(1)}, u32[]{:S(2)}, u32[]{:S(2)}) collective-permute-start(f32[6,20,2,128]{3,2,1,0:T(2,128)S(1)} %get-tuple-element.49), channel_id=1, source_target_pairs={{4,0},{8,4},{12,8},{16,12},{20,16},{24,20},{28,24},{5,1},{9,5},{13... | collective-permute-start | bytes 368648 | tf_op jit(solution)/shard_map/ppermute | solution.py:22
  133.0 8.1 %collective-permute-start.16 = (f32[6,20,20,2]{2,1,3,0:T(8,128)}, f32[6,20,20,2]{2,1,3,0:T(8,128)}, u32[]{:S(2)}, u32[]{:S(2)}) collective-permute-start(f32[6,20,20,2]{2,1,3,0:T(8,128)} %copy.81), channel_id=1, source_target_pairs={{0,1},{1,2},{2,3},{4,5},{5,6},{6,7},{8,9},{9,10},{10,11},{12,13},{... | collective-permute-start | bytes 57608 | tf_op jit(solution)/shard_map/ppermute | solution.py:21
  139.8 6.2 %collective-permute-start.17 = (f32[6,20,20,2]{2,1,3,0:T(8,128)}, f32[6,20,20,2]{2,1,3,0:T(8,128)}, u32[]{:S(2)}, u32[]{:S(2)}) collective-permute-start(f32[6,20,20,2]{2,1,3,0:T(8,128)} %copy.82), channel_id=1, source_target_pairs={{1,0},{2,1},{3,2},{5,4},{6,5},{7,6},{9,8},{10,9},{11,10},{13,12},{... | collective-permute-start | bytes 57608 | tf_op jit(solution)/shard_map/ppermute | solution.py:22
  153.9 8.9 %collective-permute-start.18 = (f32[3,2,16,128]{3,2,1,0:T(8,128)S(1)}, f32[3,2,16,128]{3,2,1,0:T(8,128)S(1)}, u32[]{:S(2)}, u32[]{:S(2)}) collective-permute-start(f32[3,2,16,128]{3,2,1,0:T(8,128)S(1)} %get-tuple-element.64), channel_id=1, source_target_pairs={{0,32},{32,64},{64,96},{96,128},{128,160},{160,192},{192,224},{224... | collective-permute-start | bytes 147464 | tf_op jit(solution)/shard_map/ppermute | solution.py:21
  161.4 9.1 %collective-permute-start.19 = (f32[3,2,16,128]{3,2,1,0:T(8,128)S(1)}, f32[3,2,16,128]{3,2,1,0:T(8,128)S(1)}, u32[]{:S(2)}, u32[]{:S(2)}) collective-permute-start(f32[3,2,16,128]{3,2,1,0:T(8,128)S(1)} %get-tuple-element.65), channel_id=1, source_target_pairs={{32,0},{64,32},{96,64},{128,96},{160,128},{192,160},{224,192},{256... | collective-permute-start | bytes 147464 | tf_op jit(solution)/shard_map/ppermute | solution.py:22
  170.5 6.7 %collective-permute-start.20 = (f32[3,20,2,128]{3,2,1,0:T(2,128)S(1)}, f32[3,20,2,128]{3,2,1,0:T(2,128)S(1)}, u32[]{:S(2)}, u32[]{:S(2)}) collective-permute-start(f32[3,20,2,128]{3,2,1,0:T(2,128)S(1)} %get-tuple-element.60), channel_id=1, source_target_pairs={{0,4},{4,8},{8,12},{12,16},{16,20},{20,24},{24,28},{1,5},{5,9},{9,... | collective-permute-start | bytes 184328 | tf_op jit(solution)/shard_map/ppermute | solution.py:21
  175.3 5.5 %collective-permute-start.21 = (f32[3,20,2,128]{3,2,1,0:T(2,128)S(1)}, f32[3,20,2,128]{3,2,1,0:T(2,128)S(1)}, u32[]{:S(2)}, u32[]{:S(2)}) collective-permute-start(f32[3,20,2,128]{3,2,1,0:T(2,128)S(1)} %get-tuple-element.61), channel_id=1, source_target_pairs={{4,0},{8,4},{12,8},{16,12},{20,16},{24,20},{28,24},{5,1},{9,5},{13... | collective-permute-start | bytes 184328 | tf_op jit(solution)/shard_map/ppermute | solution.py:22
  181.8 3.1 %collective-permute-start.22 = (f32[3,20,20,2]{2,1,3,0:T(8,128)S(1)}, f32[3,20,20,2]{2,1,3,0:T(8,128)S(1)}, u32[]{:S(2)}, u32[]{:S(2)}) collective-permute-start(f32[3,20,20,2]{2,1,3,0:T(8,128)S(1)} %copy.83), channel_id=1, source_target_pairs={{0,1},{1,2},{2,3},{4,5},{5,6},{6,7},{8,9},{9,10},{10,11},{12,13},{... | collective-permute-start | bytes 28808 | tf_op jit(solution)/shard_map/ppermute | solution.py:21
  183.6 5.2 %collective-permute-start.23 = (f32[3,20,20,2]{2,1,3,0:T(8,128)S(1)}, f32[3,20,20,2]{2,1,3,0:T(8,128)}, u32[]{:S(2)}, u32[]{:S(2)}) collective-permute-start(f32[3,20,20,2]{2,1,3,0:T(8,128)S(1)} %copy.84), channel_id=1, source_target_pairs={{1,0},{2,1},{3,2},{5,4},{6,5},{7,6},{9,8},{10,9},{11,10},{13,12},{... | collective-permute-start | bytes 28808 | tf_op jit(solution)/shard_map/ppermute | solution.py:22
  (19 other events, 133.1 us)
where the time goes:
time: 196 us; the launch traced here: 195 us
  starting transfers between devices  92 us (47%)
  waiting for transfers between devices  54 us (28%)
  local copies, waits for them, and re-layouts  27.5 us (14%)
  other arithmetic  20.3 us (10%)
    ppermute x12, starting transfers between devices, extended(): before = lax.ppermute(last, axis, up)  73.4 us
    ppermute x12, waiting for transfers between devices, extended(): after = lax.ppermute(leading, axis, down)  51.1 us
    ppermute x12, starting transfers between devices, extended(): after = lax.ppermute(leading, axis, down)  18.6 us
    unnamed x48, local copies, waits for them, and re-layouts  12.9 us
    concatenate x8, other arithmetic, extended(): value = jnp.concatenate([before, value, after], axis=dim)  8.59 us
    ppermute x4, local copies, waits for them, and re-layouts, extended(): after = lax.ppermute(leading, axis, down)  6.47 us
    unnamed x15, other arithmetic  4.21 us
  transfers between devices with their start and end apart: 24, of which 13 were waited for; matrix products, arithmetic and copies ran while one was open for 5% of the time, Pallas kernels for 0%

commit v1 on v0

v1 whole, which is shorter than its diff:
```python
import functools

import jax
import jax.numpy as jnp
from jax import lax
from jax.experimental import pallas as pl
from jax.experimental.pallas import tpu as pltpu
from jax.sharding import PartitionSpec as P

STEPS = 2
COEF_NEAR = 9.0 / 8.0
COEF_FAR = -1.0 / 24.0
TIME_STEP = 0.2
AXES = ("gx", "gy", "gz")

STRESS = (
    ((0, "f"), (3, "b"), (4, "b")),
    ((3, "b"), (1, "f"), (5, "b")),
    ((4, "b"), (5, "b"), (2, "f")),
)
VELOCITY = (
    ((0, "b"), (1, "f"), (2, "f")),
    ((1, "b"), (0, "f"), (2, "f")),
    ((2, "b"), (0, "f"), (1, "f")),
)
BEFORE = {"f": (-1,), "b": (-2, -1)}
AFTER = {"f": (0, 1), "b": (0,)}
TAPS = {
    "f": ((1, COEF_NEAR), (0, -COEF_NEAR), (2, COEF_FAR), (-1, -COEF_FAR)),
    "b": ((0, COEF_NEAR), (-1, -COEF_NEAR), (1, COEF_FAR), (-2, -COEF_FAR)),
}


def layers(spec, sides):
    return [(comp, off) for comp, kind in spec for off in sides[kind]]


def weighted(taps):
    a, b, c, d = taps
    return COEF_NEAR * (a - b) + COEF_FAR * (c - d)


class Faces:
    def __init__(self, spec, fields, halos, rows, edges):
        self.spec, self.fields, self.rows, self.edges = spec, fields, rows, edges
        self.xb, self.xa, self.yb, self.ya, self.zb, self.za = halos
        self.nx, self.ny, self.nz = fields.shape[1:]
        self.before = [{k: i for i, k in enumerate(layers(s, BEFORE))} for s in spec]
        self.after = [{k: i for i, k in enumerate(layers(s, AFTER))} for s in spec]

    def prepare(self):
        nx, ny, nz = self.nx, self.ny, self.nz
        for slot, (comp, kind) in enumerate(self.spec[1]):
            for x in range(nx):
                self.rows[slot, x, 8 : 8 + ny, :] = self.fields[comp, x]
                for off in BEFORE[kind]:
                    i = self.before[1][comp, off]
                    self.rows[slot, x, 8 + off : 9 + off, :] = self.yb[i, x : x + 1, :]
                for off in AFTER[kind]:
                    i = self.after[1][comp, off]
                    self.rows[slot, x, 8 + ny + off : 9 + ny + off, :] = self.ya[i, x : x + 1, :]
        got = jnp.concatenate([self.zb[...], self.za[...]], axis=0)
        row = lax.broadcasted_iota(jnp.int32, (16, nz), 0)
        lane = lax.broadcasted_iota(jnp.int32, (16, nz), 1)
        for slot, (comp, kind) in enumerate(self.spec[2]):
            weights = jnp.zeros((16, nz), jnp.float32)
            for shift, weight in TAPS[kind]:
                for off in BEFORE[kind]:
                    at = off - shift
                    if 0 <= at < nz:
                        hit = (row == self.before[2][comp, off]) & (lane == at)
                        weights = weights + jnp.where(hit, weight, 0.0)
                for off in AFTER[kind]:
                    at = nz + off - shift
                    if 0 <= at < nz:
                        hit = (row == 8 + self.after[2][comp, off]) & (lane == at)
                        weights = weights + jnp.where(hit, weight, 0.0)
            self.edges[slot] = lax.dot_general(
                got,
                weights,
                (((0,), (0,)), ((), ())),
                precision=lax.Precision.HIGHEST,
                preferred_element_type=jnp.float32,
            )

    def dx(self, comp, x):
        kind = dict(self.spec[0])[comp]

        def plane(at):
            if at < 0:
                return self.xb[self.before[0][comp, at]]
            if at >= self.nx:
                return self.xa[self.after[0][comp, at - self.nx]]
            return self.fields[comp, at]

        return weighted([plane(x + off) for off, _ in TAPS[kind]])

    def dy(self, comp, x):
        slot = [c for c, _ in self.spec[1]].index(comp)
        kind = self.spec[1][slot][1]
        return weighted(
            [self.rows[slot, x, 8 + off : 8 + off + self.ny, :] for off, _ in TAPS[kind]]
        )

    def dz(self, comp, x):
        slot = [c for c, _ in self.spec[2]].index(comp)
        kind = self.spec[2][slot][1]
        here = self.fields[comp, x]
        lane = lax.broadcasted_iota(jnp.int32, (1, self.nz), 1)
        total = self.edges[slot, x * self.ny : (x + 1) * self.ny, :]
        for off, weight in TAPS[kind]:
            if off == 0:
                total = total + weight * here
            else:
                inside = (lane + off >= 0) & (lane + off < self.nz)
                moved = pltpu.roll(here, (-off) % self.nz, 1)
                total = total + jnp.where(inside, weight, 0.0) * moved
        return total


def pack(spec, fields, up, down):
    nx, ny, nz = fields.shape[1:]
    xu, yu, zu = up
    xd, yd, zd = down
    for i, (comp, off) in enumerate(layers(spec[0], BEFORE)):
        xu[i] = fields[comp, nx + off]
    for i, (comp, off) in enumerate(layers(spec[0], AFTER)):
        xd[i] = fields[comp, off]
    for i, (comp, off) in enumerate(layers(spec[1], BEFORE)):
        yu[i] = fields[comp, :, ny + off, :]
    for i, (comp, off) in enumerate(layers(spec[1], AFTER)):
        yd[i] = fields[comp, :, off, :]
    row = lax.broadcasted_iota(jnp.int32, (16, nz), 0)
    lane = lax.broadcasted_iota(jnp.int32, (16, nz), 1)
    before, after = layers(spec[2], BEFORE), layers(spec[2], AFTER)
    total = None
    for comp, _ in spec[2]:
        pick = jnp.zeros((16, nz), jnp.float32)
        for i, (c, off) in enumerate(before):
            if c == comp:
                pick = jnp.where((row == i) & (lane == nz + off), 1.0, pick)
        for i, (c, off) in enumerate(after):
            if c == comp:
                pick = jnp.where((row == 8 + i) & (lane == off), 1.0, pick)
        part = lax.dot_general(
            pick,
            fields[comp].reshape(nx * ny, nz),
            (((1,), (1,)), ((), ())),
            precision=lax.Precision.HIGHEST,
            preferred_element_type=jnp.float32,
        )
        total = part if total is None else total + part
    zu[...] = total[:8]
    zd[...] = total[8:]


def first_kernel(stress, xu, xd, yu, yd, zu, zd):
    pack(STRESS, stress, (xu, yu, zu), (xd, yd, zd))


def velocity_kernel(send, *refs):
    stress, velocity, buoyancy = refs[:3]
    out = refs[9]
    faces = Faces(STRESS, stress, refs[3:9], refs[-2], refs[-1])
    faces.prepare()
    for x in range(velocity.shape[1]):
        scale = TIME_STEP * buoyancy[x]
        out[0, x] = velocity[0, x] + scale * (faces.dx(0, x) + faces.dy(3, x) + faces.dz(4, x))
        out[1, x] = velocity[1, x] + scale * (faces.dx(3, x) + faces.dy(1, x) + faces.dz(5, x))
        out[2, x] = velocity[2, x] + scale * (faces.dx(4, x) + faces.dy(5, x) + faces.dz(2, x))
    if send:
        xu, xd, yu, yd, zu, zd = refs[10:16]
        pack(VELOCITY, out, (xu, yu, zu), (xd, yd, zd))


def stress_kernel(send, *refs):
    velocity, stress, memory, lam, shear, weight, mech, top_ref, first, table = refs[:10]
    out, kept = refs[16:18]
    faces = Faces(VELOCITY, velocity, refs[10:16], refs[-2], refs[-1])
    faces.prepare()
    nx, ny, nz = lam.shape
    tops = top_ref[...].astype(jnp.float32).T
    depth = (first[0] + lax.broadcasted_iota(jnp.int32, (1, nz), 1)).astype(jnp.float32)
    for x in range(nx):
        decay = jnp.zeros((ny, nz), jnp.float32)
        for level in range(table.shape[0]):
            decay = jnp.where(mech[x] == level, table[level], decay)
        gain = (1.0 - decay) * weight[x]
        top = tops[:, x : x + 1]
        solid = depth >= top
        below = depth > top
        xx, yy, zz = faces.dx(0, x), faces.dy(1, x), faces.dz(2, x)
        volume = lam[x] * (xx + yy + zz)
        double = 2.0 * shear[x]
        rates = (
            volume + double * xx,
            volume + double * yy,
            volume + double * zz,
            shear[x] * (faces.dy(0, x) + faces.dx(1, x)),
            shear[x] * (faces.dz(0, x) + faces.dx(2, x)),
            shear[x] * (faces.dz(1, x) + faces.dy(2, x)),
        )
        for comp, rate in enumerate(rates):
            new = decay * memory[comp, x] + gain * rate
            kept[comp, x] = new
            keep = below if comp in (2, 4, 5) else solid
            out[comp, x] = jnp.where(keep, stress[comp, x] + TIME_STEP * (rate - new), 0.0)
    if send:
        xu, xd, yu, yd, zu, zd = refs[18:24]
        pack(STRESS, out, (xu, yu, zu), (xd, yd, zd))


def face_shapes(spec, nx, ny, nz):
    shapes = []
    for sides in (BEFORE, AFTER):
        shapes.append((len(layers(spec[0], sides)), ny, nz))
        shapes.append((len(layers(spec[1], sides)), nx, nz))
        shapes.append((8, nx * ny))
    xu, yu, zu, xd, yd, zd = [jax.ShapeDtypeStruct(s, jnp.float32) for s in shapes]
    return [xu, xd, yu, yd, zu, zd]


def call(body, outs, operands, scalars=(), scratch=()):
    vmem = pl.BlockSpec(memory_space=pltpu.VMEM)
    smem = pl.BlockSpec(memory_space=pltpu.SMEM)
    return pl.pallas_call(
        body,
        out_shape=outs,
        in_specs=[smem if i in scalars else vmem for i in range(len(operands))],
        out_specs=[vmem] * len(outs),
        scratch_shapes=list(scratch),
        compiler_params=pltpu.CompilerParams(vmem_limit_bytes=24 * 1024 * 1024),
    )(*operands)


def exchange(faces):
    got = []
    for i, face in enumerate(faces):
        axis = AXES[i // 2]
        peers = lax.axis_size(axis)
        pairs = [(j, j + 1) for j in range(peers - 1)]
        if i % 2:
            pairs = [(b, a) for a, b in pairs]
        got.append(lax.ppermute(face, axis, pairs))
    return got


def shards(
    velocity,
    stress,
    memory,
    lame_lambda,
    shear_modulus,
    buoyancy,
    anelastic_weight,
    decay_table,
    mech_index,
    surface_depth,
):
    nx, ny, nz = lame_lambda.shape
    first = (lax.axis_index("gz") * nz).astype(jnp.int32).reshape(1)
    like = lambda a: jax.ShapeDtypeStruct(a.shape, a.dtype)
    scratch = (
        pltpu.VMEM((3, nx, ny + 16, nz), jnp.float32),
        pltpu.VMEM((3, nx * ny, nz), jnp.float32),
    )
    stress_faces = face_shapes(STRESS, nx, ny, nz)
    velocity_faces = face_shapes(VELOCITY, nx, ny, nz)
    faces = call(first_kernel, stress_faces, [stress])
    for step in range(STEPS):
        halos = exchange(faces)
        velocity, *faces = call(
            functools.partial(velocity_kernel, True),
            [like(velocity)] + velocity_faces,
            [stress, velocity, buoyancy, *halos],
            scratch=scratch,
        )
        halos = exchange(faces)
        send = step < STEPS - 1
        stress, memory, *faces = call(
            functools.partial(stress_kernel, send),
            [like(stress), like(memory)] + (stress_faces if send else []),
            [
                velocity,
                stress,
                memory,
                lame_lambda,
                shear_modulus,
                anelastic_weight,
                mech_index,
                surface_depth,
                first,
                decay_table,
                *halos,
            ],
            scalars=(8, 9),
            scratch=scratch,
        )
    return (velocity, stress, memory)


def solution(mesh):
    fields = P(None, *AXES)
    cells = P(*AXES)
    return jax.shard_map(
        shards,
        mesh=mesh,
        in_specs=(fields,) * 3 + (cells,) * 4 + (P(), cells, P("gx", "gy")),
        out_specs=(fields,) * 3,
        check_vma=False,
    )
```

time: 196 us -> 123 us (0.63)
  the two profiles are of different devices: /device:TPU:1 before, /device:TPU:15 now
where the time goes in v1:
time: 123 us; the launch traced here: 122 us
  starting transfers between devices  90.3 us (73%)
  waiting for transfers between devices  17.5 us (14%)
  Pallas kernels  8.47 us (7%)
  local copies, waits for them, and re-layouts  4.63 us (4%)
    ppermute x24, starting transfers between devices, exchange(): got.append(lax.ppermute(face, axis, pairs))  90.3 us
    ppermute x24, waiting for transfers between devices, exchange(): got.append(lax.ppermute(face, axis, pairs))  17.5 us
    pallas_call x5, Pallas kernels, call(): pl.pallas_call(body, out_shape=outs, in_specs=[smem if i in scalars else...  8.47 us
    unnamed x26, local copies, waits for them, and re-layouts  4.63 us
  transfers between devices with their start and end apart: 24, of which 8 were waited for; matrix products, arithmetic and copies ran while one was open for 0% of the time, Pallas kernels for 0%

profile of v1, /device:TPU:15, one launch (start us, length us, event | category | flops | bytes accessed | tf_op | source)
XLA Modules:
  0.0 121.8 jit_solution(17561286076802179905)
XLA Ops:
  2.2 9.0 %collective-permute-start = (f32[5,16,128]{2,1,0:T(8,128)S(1)}, f32[5,16,128]{2,1,0:T(8,128)S(1)}, u32[]{:S(2)}, u32[]{:S(2)}) collective-permute-start(f32[5,16,128]{2,1,0:T(8,128)S(1)} %get-tuple-element.33), channel_id=1, source_target_pairs={{0,32},{32,64},{64,96},{96,128},{128,160},{160,192},{192,224},{224... | collective-permute-start | bytes 122888 | tf_op jit(solution)/shard_map/ppermute | solution.py:244
  11.2 4.0 %collective-permute-start.2 = (f32[5,16,128]{2,1,0:T(8,128)S(1)}, f32[5,16,128]{2,1,0:T(8,128)S(1)}, u32[]{:S(2)}, u32[]{:S(2)}) collective-permute-start(f32[5,16,128]{2,1,0:T(8,128)S(1)} %get-tuple-element.35), channel_id=1, source_target_pairs={{0,4},{4,8},{8,12},{12,16},{16,20},{20,24},{24,28},{1,5},{5,9},{9,... | collective-permute-start | bytes 122888 | tf_op jit(solution)/shard_map/ppermute | solution.py:244
  15.2 5.5 %collective-permute-start.1 = (f32[4,16,128]{2,1,0:T(8,128)S(1)}, f32[4,16,128]{2,1,0:T(8,128)S(1)}, u32[]{:S(2)}, u32[]{:S(2)}) collective-permute-start(f32[4,16,128]{2,1,0:T(8,128)S(1)} %get-tuple-element.34), channel_id=1, source_target_pairs={{32,0},{64,32},{96,64},{128,96},{160,128},{192,160},{224,192},{256... | collective-permute-start | bytes 98312 | tf_op jit(solution)/shard_map/ppermute | solution.py:244
  20.8 1.9 %collective-permute-start.3 = (f32[4,16,128]{2,1,0:T(8,128)S(1)}, f32[4,16,128]{2,1,0:T(8,128)S(1)}, u32[]{:S(2)}, u32[]{:S(2)}) collective-permute-start(f32[4,16,128]{2,1,0:T(8,128)S(1)} %get-tuple-element.36), channel_id=1, source_target_pairs={{4,0},{8,4},{12,8},{16,12},{20,16},{24,20},{28,24},{5,1},{9,5},{13... | collective-permute-start | bytes 98312 | tf_op jit(solution)/shard_map/ppermute | solution.py:244
  22.7 2.6 %collective-permute-start.4 = (f32[8,256]{1,0:T(8,128)S(1)}, f32[8,256]{1,0:T(8,128)S(1)}, u32[]{:S(2)}, u32[]{:S(2)}) collective-permute-start(f32[8,256]{1,0:T(8,128)S(1)} %get-tuple-element.37), channel_id=1, source_target_pairs={{0,1},{1,2},{2,3},{4,5},{5,6},{6,7},{8,9},{9,10},{10,11},{12,13},{... | collective-permute-start | bytes 24584 | tf_op jit(solution)/shard_map/ppermute | solution.py:244
  27.4 3.4 %collective-permute-done.5.refs_8_ = f32[8,256]{1,0:T(8,128)S(1)} collective-permute-done((f32[8,256]{1,0:T(8,128)S(1)}, f32[8,256]{1,0:T(8,128)S(1)}, u32[]{:S(2)}, u32[]{:S(2)}) %collective-permute-start.5) | collective-permute-done | bytes 8224 | tf_op jit(solution)/shard_map/ppermute | solution.py:244
  34.2 7.6 %collective-permute-start.7 = (f32[5,16,128]{2,1,0:T(8,128)S(1)}, f32[5,16,128]{2,1,0:T(8,128)S(1)}, u32[]{:S(2)}, u32[]{:S(2)}) collective-permute-start(f32[5,16,128]{2,1,0:T(8,128)S(1)} %get-tuple-element.41), channel_id=1, source_target_pairs={{32,0},{64,32},{96,64},{128,96},{160,128},{192,160},{224,192},{256... | collective-permute-start | bytes 122888 | tf_op jit(solution)/shard_map/ppermute | solution.py:244
  41.7 4.8 %collective-permute-start.9 = (f32[5,16,128]{2,1,0:T(8,128)S(1)}, f32[5,16,128]{2,1,0:T(8,128)S(1)}, u32[]{:S(2)}, u32[]{:S(2)}) collective-permute-start(f32[5,16,128]{2,1,0:T(8,128)S(1)} %get-tuple-element.43), channel_id=1, source_target_pairs={{4,0},{8,4},{12,8},{16,12},{20,16},{24,20},{28,24},{5,1},{9,5},{13... | collective-permute-start | bytes 122888 | tf_op jit(solution)/shard_map/ppermute | solution.py:244
  48.5 3.1 %collective-permute-start.8 = (f32[4,16,128]{2,1,0:T(8,128)S(1)}, f32[4,16,128]{2,1,0:T(8,128)S(1)}, u32[]{:S(2)}, u32[]{:S(2)}) collective-permute-start(f32[4,16,128]{2,1,0:T(8,128)S(1)} %get-tuple-element.42), channel_id=1, source_target_pairs={{0,4},{4,8},{8,12},{12,16},{16,20},{20,24},{24,28},{1,5},{5,9},{9,... | collective-permute-start | bytes 98312 | tf_op jit(solution)/shard_map/ppermute | solution.py:244
  51.6 3.6 %collective-permute-start.10 = (f32[8,256]{1,0:T(8,128)S(1)}, f32[8,256]{1,0:T(8,128)S(1)}, u32[]{:S(2)}, u32[]{:S(2)}) collective-permute-start(f32[8,256]{1,0:T(8,128)S(1)} %get-tuple-element.44), channel_id=1, source_target_pairs={{0,1},{1,2},{2,3},{4,5},{5,6},{6,7},{8,9},{9,10},{10,11},{12,13},{... | collective-permute-start | bytes 24584 | tf_op jit(solution)/shard_map/ppermute | solution.py:244
  57.3 3.6 %collective-permute-done.11.refs_15_ = f32[8,256]{1,0:T(8,128)S(1)} collective-permute-done((f32[8,256]{1,0:T(8,128)S(1)}, f32[8,256]{1,0:T(8,128)S(1)}, u32[]{:S(2)}, u32[]{:S(2)}) %collective-permute-start.11) | collective-permute-done | bytes 8224 | tf_op jit(solution)/shard_map/ppermute | solution.py:244
  61.6 2.3 %shard_map.123 = (f32[6,16,16,128]{3,2,1,0:T(8,128)S(1)}, f32[6,16,16,128]{3,2,1,0:T(8,128)S(1)}, f32[5,16,128]{2,1,0:T(8,128)S(1)}, f32[4,16,128]{2,1,0:T(8,128...) custom-call(f32[3,16,16,128]{3,2,1,0:T(8,128)S(1)} %get-tuple-elemen, ...), custom_call_target="tpu_custom_call" | custom-call | tf_op jit(solution)/shard_map/pallas_call | solution.py:226
  63.9 4.9 %collective-permute-start.12 = (f32[5,16,128]{2,1,0:T(8,128)S(1)}, f32[5,16,128]{2,1,0:T(8,128)S(1)}, u32[]{:S(2)}, u32[]{:S(2)}) collective-permute-start(f32[5,16,128]{2,1,0:T(8,128)S(1)} %get-tuple-element.47), channel_id=1, source_target_pairs={{0,32},{32,64},{64,96},{96,128},{128,160},{160,192},{192,224},{224... | collective-permute-start | bytes 122888 | tf_op jit(solution)/shard_map/ppermute | solution.py:244
  68.8 4.4 %collective-permute-start.14 = (f32[5,16,128]{2,1,0:T(8,128)S(1)}, f32[5,16,128]{2,1,0:T(8,128)S(1)}, u32[]{:S(2)}, u32[]{:S(2)}) collective-permute-start(f32[5,16,128]{2,1,0:T(8,128)S(1)} %get-tuple-element.49), channel_id=1, source_target_pairs={{0,4},{4,8},{8,12},{12,16},{16,20},{20,24},{24,28},{1,5},{5,9},{9,... | collective-permute-start | bytes 122888 | tf_op jit(solution)/shard_map/ppermute | solution.py:244
  73.3 5.2 %collective-permute-start.13 = (f32[4,16,128]{2,1,0:T(8,128)S(1)}, f32[4,16,128]{2,1,0:T(8,128)S(1)}, u32[]{:S(2)}, u32[]{:S(2)}) collective-permute-start(f32[4,16,128]{2,1,0:T(8,128)S(1)} %get-tuple-element.48), channel_id=1, source_target_pairs={{32,0},{64,32},{96,64},{128,96},{160,128},{192,160},{224,192},{256... | collective-permute-start | bytes 98312 | tf_op jit(solution)/shard_map/ppermute | solution.py:244
  78.5 1.9 %collective-permute-start.15 = (f32[4,16,128]{2,1,0:T(8,128)S(1)}, f32[4,16,128]{2,1,0:T(8,128)S(1)}, u32[]{:S(2)}, u32[]{:S(2)}) collective-permute-start(f32[4,16,128]{2,1,0:T(8,128)S(1)} %get-tuple-element.50), channel_id=1, source_target_pairs={{4,0},{8,4},{12,8},{16,12},{20,16},{24,20},{28,24},{5,1},{9,5},{13... | collective-permute-start | bytes 98312 | tf_op jit(solution)/shard_map/ppermute | solution.py:244
  80.4 3.6 %collective-permute-start.16 = (f32[8,256]{1,0:T(8,128)S(1)}, f32[8,256]{1,0:T(8,128)S(1)}, u32[]{:S(2)}, u32[]{:S(2)}) collective-permute-start(f32[8,256]{1,0:T(8,128)S(1)} %get-tuple-element.51), channel_id=1, source_target_pairs={{0,1},{1,2},{2,3},{4,5},{5,6},{6,7},{8,9},{9,10},{10,11},{12,13},{... | collective-permute-start | bytes 24584 | tf_op jit(solution)/shard_map/ppermute | solution.py:244
  86.1 3.4 %collective-permute-done.17.refs_8_ = f32[8,256]{1,0:T(8,128)S(1)} collective-permute-done((f32[8,256]{1,0:T(8,128)S(1)}, f32[8,256]{1,0:T(8,128)S(1)}, u32[]{:S(2)}, u32[]{:S(2)}) %collective-permute-start.17) | collective-permute-done | bytes 8224 | tf_op jit(solution)/shard_map/ppermute | solution.py:244
  91.2 7.2 %collective-permute-start.19 = (f32[5,16,128]{2,1,0:T(8,128)S(1)}, f32[5,16,128]{2,1,0:T(8,128)S(1)}, u32[]{:S(2)}, u32[]{:S(2)}) collective-permute-start(f32[5,16,128]{2,1,0:T(8,128)S(1)} %get-tuple-element.56), channel_id=1, source_target_pairs={{32,0},{64,32},{96,64},{128,96},{160,128},{192,160},{224,192},{256... | collective-permute-start | bytes 122888 | tf_op jit(solution)/shard_map/ppermute | solution.py:244
  98.4 4.8 %collective-permute-start.21 = (f32[5,16,128]{2,1,0:T(8,128)S(1)}, f32[5,16,128]{2,1,0:T(8,128)S(1)}, u32[]{:S(2)}, u32[]{:S(2)}) collective-permute-start(f32[5,16,128]{2,1,0:T(8,128)S(1)} %get-tuple-element.58), channel_id=1, source_target_pairs={{4,0},{8,4},{12,8},{16,12},{20,16},{24,20},{28,24},{5,1},{9,5},{13... | collective-permute-start | bytes 122888 | tf_op jit(solution)/shard_map/ppermute | solution.py:244
  105.1 3.4 %collective-permute-start.20 = (f32[4,16,128]{2,1,0:T(8,128)S(1)}, f32[4,16,128]{2,1,0:T(8,128)S(1)}, u32[]{:S(2)}, u32[]{:S(2)}) collective-permute-start(f32[4,16,128]{2,1,0:T(8,128)S(1)} %get-tuple-element.57), channel_id=1, source_target_pairs={{0,4},{4,8},{8,12},{12,16},{16,20},{20,24},{24,28},{1,5},{5,9},{9,... | collective-permute-start | bytes 98312 | tf_op jit(solution)/shard_map/ppermute | solution.py:244
  108.5 3.6 %collective-permute-start.22 = (f32[8,256]{1,0:T(8,128)S(1)}, f32[8,256]{1,0:T(8,128)S(1)}, u32[]{:S(2)}, u32[]{:S(2)}) collective-permute-start(f32[8,256]{1,0:T(8,128)S(1)} %get-tuple-element.59), channel_id=1, source_target_pairs={{0,1},{1,2},{2,3},{4,5},{5,6},{6,7},{8,9},{9,10},{10,11},{12,13},{... | collective-permute-start | bytes 24584 | tf_op jit(solution)/shard_map/ppermute | solution.py:244
  114.2 4.0 %collective-permute-done.23.refs_15_ = f32[8,256]{1,0:T(8,128)S(1)} collective-permute-done((f32[8,256]{1,0:T(8,128)S(1)}, f32[8,256]{1,0:T(8,128)S(1)}, u32[]{:S(2)}, u32[]{:S(2)}) %collective-permute-start.23) | collective-permute-done | bytes 8224 | tf_op jit(solution)/shard_map/ppermute | solution.py:244
  119.2 2.6 %shard_map.125 = (f32[6,16,16,128]{3,2,1,0:T(8,128)}, f32[6,16,16,128]{3,2,1,0:T(8,128)}) custom-call(f32[3,16,16,128]{3,2,1,0:T(8,128)S(1)} %copy-done.9, f32[6,16,16,128]{3,2,1,0:T(8,128)S(1)} %get-tuple-element.46.refs_0_.refs_1_, f32[6,16,16,128]{3,2,1,0:T(8,128)S(1)} %get-tuple-element.54.refs_2_, f32[16,16,128]{2,1,0:T(8,128)S(1)} %copy-done.5, ...), custom_call_target="tpu_custom_call" | custom-call | tf_op jit(solution)/shard_map/pallas_call | solution.py:226
  (55 shorter events, 20.3 us)
Async XLA Ops:
  2.2 28.6 %collective-permute-start = (f32[5,16,128]{2,1,0:T(8,128)S(1)}, f32[5,16,128]{2,1,0:T(8,128)S(1)}, u32[]{:S(2)}, u32[]{:S(2)}) collective-permute-start(f32[5,16,128]{2,1,0:T(8,128)S(1)} %get-tuple-element.33), channel_id=1, source_target_pairs={{0,32},{32,64},{64,96},{96,128},{128,160},{160,192},{192,224},{224... | collective-permute-start | bytes 122888 | tf_op jit(solution)/shard_map/ppermute | solution.py:244
  11.2 19.6 %collective-permute-start.2 = (f32[5,16,128]{2,1,0:T(8,128)S(1)}, f32[5,16,128]{2,1,0:T(8,128)S(1)}, u32[]{:S(2)}, u32[]{:S(2)}) collective-permute-start(f32[5,16,128]{2,1,0:T(8,128)S(1)} %get-tuple-element.35), channel_id=1, source_target_pairs={{0,4},{4,8},{8,12},{12,16},{16,20},{20,24},{24,28},{1,5},{5,9},{9,... | collective-permute-start | bytes 122888 | tf_op jit(solution)/shard_map/ppermute | solution.py:244
  15.2 15.5 %collective-permute-start.1 = (f32[4,16,128]{2,1,0:T(8,128)S(1)}, f32[4,16,128]{2,1,0:T(8,128)S(1)}, u32[]{:S(2)}, u32[]{:S(2)}) collective-permute-start(f32[4,16,128]{2,1,0:T(8,128)S(1)} %get-tuple-element.34), channel_id=1, source_target_pairs={{32,0},{64,32},{96,64},{128,96},{160,128},{192,160},{224,192},{256... | collective-permute-start | bytes 98312 | tf_op jit(solution)/shard_map/ppermute | solution.py:244
  20.8 10.0 %collective-permute-start.3 = (f32[4,16,128]{2,1,0:T(8,128)S(1)}, f32[4,16,128]{2,1,0:T(8,128)S(1)}, u32[]{:S(2)}, u32[]{:S(2)}) collective-permute-start(f32[4,16,128]{2,1,0:T(8,128)S(1)} %get-tuple-element.36), channel_id=1, source_target_pairs={{4,0},{8,4},{12,8},{16,12},{20,16},{24,20},{28,24},{5,1},{9,5},{13... | collective-permute-start | bytes 98312 | tf_op jit(solution)/shard_map/ppermute | solution.py:244
  22.7 3.4 %collective-permute-start.4 = (f32[8,256]{1,0:T(8,128)S(1)}, f32[8,256]{1,0:T(8,128)S(1)}, u32[]{:S(2)}, u32[]{:S(2)}) collective-permute-start(f32[8,256]{1,0:T(8,128)S(1)} %get-tuple-element.37), channel_id=1, source_target_pairs={{0,1},{1,2},{2,3},{4,5},{5,6},{6,7},{8,9},{9,10},{10,11},{12,13},{... | collective-permute-start | bytes 24584 | tf_op jit(solution)/shard_map/ppermute | solution.py:244
  26.1 4.6 %collective-permute-start.5 = (f32[8,256]{1,0:T(8,128)S(1)}, f32[8,256]{1,0:T(8,128)S(1)}, u32[]{:S(2)}, u32[]{:S(2)}) collective-permute-start(f32[8,256]{1,0:T(8,128)S(1)} %get-tuple-element.38), channel_id=1, source_target_pairs={{1,0},{2,1},{3,2},{5,4},{6,5},{7,6},{9,8},{10,9},{11,10},{13,12},{... | collective-permute-start | bytes 24584 | tf_op jit(solution)/shard_map/ppermute | solution.py:244
  34.2 26.8 %collective-permute-start.7 = (f32[5,16,128]{2,1,0:T(8,128)S(1)}, f32[5,16,128]{2,1,0:T(8,128)S(1)}, u32[]{:S(2)}, u32[]{:S(2)}) collective-permute-start(f32[5,16,128]{2,1,0:T(8,128)S(1)} %get-tuple-element.41), channel_id=1, source_target_pairs={{32,0},{64,32},{96,64},{128,96},{160,128},{192,160},{224,192},{256... | collective-permute-start | bytes 122888 | tf_op jit(solution)/shard_map/ppermute | solution.py:244
  41.7 19.2 %collective-permute-start.9 = (f32[5,16,128]{2,1,0:T(8,128)S(1)}, f32[5,16,128]{2,1,0:T(8,128)S(1)}, u32[]{:S(2)}, u32[]{:S(2)}) collective-permute-start(f32[5,16,128]{2,1,0:T(8,128)S(1)} %get-tuple-element.43), channel_id=1, source_target_pairs={{4,0},{8,4},{12,8},{16,12},{20,16},{24,20},{28,24},{5,1},{9,5},{13... | collective-permute-start | bytes 122888 | tf_op jit(solution)/shard_map/ppermute | solution.py:244
  46.5 14.4 %collective-permute-start.6 = (f32[4,16,128]{2,1,0:T(8,128)S(1)}, f32[4,16,128]{2,1,0:T(8,128)S(1)}, u32[]{:S(2)}, u32[]{:S(2)}) collective-permute-start(f32[4,16,128]{2,1,0:T(8,128)S(1)} %get-tuple-element.40), channel_id=1, source_target_pairs={{0,32},{32,64},{64,96},{96,128},{128,160},{160,192},{192,224},{224... | collective-permute-start | bytes 98312 | tf_op jit(solution)/shard_map/ppermute | solution.py:244
  48.5 12.5 %collective-permute-start.8 = (f32[4,16,128]{2,1,0:T(8,128)S(1)}, f32[4,16,128]{2,1,0:T(8,128)S(1)}, u32[]{:S(2)}, u32[]{:S(2)}) collective-permute-start(f32[4,16,128]{2,1,0:T(8,128)S(1)} %get-tuple-element.42), channel_id=1, source_target_pairs={{0,4},{4,8},{8,12},{12,16},{16,20},{20,24},{24,28},{1,5},{5,9},{9,... | collective-permute-start | bytes 98312 | tf_op jit(solution)/shard_map/ppermute | solution.py:244
  51.6 4.4 %collective-permute-start.10 = (f32[8,256]{1,0:T(8,128)S(1)}, f32[8,256]{1,0:T(8,128)S(1)}, u32[]{:S(2)}, u32[]{:S(2)}) collective-permute-start(f32[8,256]{1,0:T(8,128)S(1)} %get-tuple-element.44), channel_id=1, source_target_pairs={{0,1},{1,2},{2,3},{4,5},{5,6},{6,7},{8,9},{9,10},{10,11},{12,13},{... | collective-permute-start | bytes 24584 | tf_op jit(solution)/shard_map/ppermute | solution.py:244
  56.0 4.9 %collective-permute-start.11 = (f32[8,256]{1,0:T(8,128)S(1)}, f32[8,256]{1,0:T(8,128)S(1)}, u32[]{:S(2)}, u32[]{:S(2)}) collective-permute-start(f32[8,256]{1,0:T(8,128)S(1)} %get-tuple-element.45), channel_id=1, source_target_pairs={{1,0},{2,1},{3,2},{5,4},{6,5},{7,6},{9,8},{10,9},{11,10},{13,12},{... | collective-permute-start | bytes 24584 | tf_op jit(solution)/shard_map/ppermute | solution.py:244
  63.9 25.6 %collective-permute-start.12 = (f32[5,16,128]{2,1,0:T(8,128)S(1)}, f32[5,16,128]{2,1,0:T(8,128)S(1)}, u32[]{:S(2)}, u32[]{:S(2)}) collective-permute-start(f32[5,16,128]{2,1,0:T(8,128)S(1)} %get-tuple-element.47), channel_id=1, source_target_pairs={{0,32},{32,64},{64,96},{96,128},{128,160},{160,192},{192,224},{224... | collective-permute-start | bytes 122888 | tf_op jit(solution)/shard_map/ppermute | solution.py:244
  68.8 20.6 %collective-permute-start.14 = (f32[5,16,128]{2,1,0:T(8,128)S(1)}, f32[5,16,128]{2,1,0:T(8,128)S(1)}, u32[]{:S(2)}, u32[]{:S(2)}) collective-permute-start(f32[5,16,128]{2,1,0:T(8,128)S(1)} %get-tuple-element.49), channel_id=1, source_target_pairs={{0,4},{4,8},{8,12},{12,16},{16,20},{20,24},{24,28},{1,5},{5,9},{9,... | collective-permute-start | bytes 122888 | tf_op jit(solution)/shard_map/ppermute | solution.py:244
  73.3 16.2 %collective-permute-start.13 = (f32[4,16,128]{2,1,0:T(8,128)S(1)}, f32[4,16,128]{2,1,0:T(8,128)S(1)}, u32[]{:S(2)}, u32[]{:S(2)}) collective-permute-start(f32[4,16,128]{2,1,0:T(8,128)S(1)} %get-tuple-element.48), channel_id=1, source_target_pairs={{32,0},{64,32},{96,64},{128,96},{160,128},{192,160},{224,192},{256... | collective-permute-start | bytes 98312 | tf_op jit(solution)/shard_map/ppermute | solution.py:244
  78.5 11.0 %collective-permute-start.15 = (f32[4,16,128]{2,1,0:T(8,128)S(1)}, f32[4,16,128]{2,1,0:T(8,128)S(1)}, u32[]{:S(2)}, u32[]{:S(2)}) collective-permute-start(f32[4,16,128]{2,1,0:T(8,128)S(1)} %get-tuple-element.50), channel_id=1, source_target_pairs={{4,0},{8,4},{12,8},{16,12},{20,16},{24,20},{28,24},{5,1},{9,5},{13... | collective-permute-start | bytes 98312 | tf_op jit(solution)/shard_map/ppermute | solution.py:244
  80.4 4.4 %collective-permute-start.16 = (f32[8,256]{1,0:T(8,128)S(1)}, f32[8,256]{1,0:T(8,128)S(1)}, u32[]{:S(2)}, u32[]{:S(2)}) collective-permute-start(f32[8,256]{1,0:T(8,128)S(1)} %get-tuple-element.51), channel_id=1, source_target_pairs={{0,1},{1,2},{2,3},{4,5},{5,6},{6,7},{8,9},{9,10},{10,11},{12,13},{... | collective-permute-start | bytes 24584 | tf_op jit(solution)/shard_map/ppermute | solution.py:244
  84.8 4.6 %collective-permute-start.17 = (f32[8,256]{1,0:T(8,128)S(1)}, f32[8,256]{1,0:T(8,128)S(1)}, u32[]{:S(2)}, u32[]{:S(2)}) collective-permute-start(f32[8,256]{1,0:T(8,128)S(1)} %get-tuple-element.52), channel_id=1, source_target_pairs={{1,0},{2,1},{3,2},{5,4},{6,5},{7,6},{9,8},{10,9},{11,10},{13,12},{... | collective-permute-start | bytes 24584 | tf_op jit(solution)/shard_map/ppermute | solution.py:244
  91.2 27.0 %collective-permute-start.19 = (f32[5,16,128]{2,1,0:T(8,128)S(1)}, f32[5,16,128]{2,1,0:T(8,128)S(1)}, u32[]{:S(2)}, u32[]{:S(2)}) collective-permute-start(f32[5,16,128]{2,1,0:T(8,128)S(1)} %get-tuple-element.56), channel_id=1, source_target_pairs={{32,0},{64,32},{96,64},{128,96},{160,128},{192,160},{224,192},{256... | collective-permute-start | bytes 122888 | tf_op jit(solution)/shard_map/ppermute | solution.py:244
  98.4 19.8 %collective-permute-start.21 = (f32[5,16,128]{2,1,0:T(8,128)S(1)}, f32[5,16,128]{2,1,0:T(8,128)S(1)}, u32[]{:S(2)}, u32[]{:S(2)}) collective-permute-start(f32[5,16,128]{2,1,0:T(8,128)S(1)} %get-tuple-element.58), channel_id=1, source_target_pairs={{4,0},{8,4},{12,8},{16,12},{20,16},{24,20},{28,24},{5,1},{9,5},{13... | collective-permute-start | bytes 122888 | tf_op jit(solution)/shard_map/ppermute | solution.py:244
  103.2 15.0 %collective-permute-start.18 = (f32[4,16,128]{2,1,0:T(8,128)S(1)}, f32[4,16,128]{2,1,0:T(8,128)S(1)}, u32[]{:S(2)}, u32[]{:S(2)}) collective-permute-start(f32[4,16,128]{2,1,0:T(8,128)S(1)} %get-tuple-element.55), channel_id=1, source_target_pairs={{0,32},{32,64},{64,96},{96,128},{128,160},{160,192},{192,224},{224... | collective-permute-start | bytes 98312 | tf_op jit(solution)/shard_map/ppermute | solution.py:244
  105.1 13.1 %collective-permute-start.20 = (f32[4,16,128]{2,1,0:T(8,128)S(1)}, f32[4,16,128]{2,1,0:T(8,128)S(1)}, u32[]{:S(2)}, u32[]{:S(2)}) collective-permute-start(f32[4,16,128]{2,1,0:T(8,128)S(1)} %get-tuple-element.57), channel_id=1, source_target_pairs={{0,4},{4,8},{8,12},{12,16},{16,20},{20,24},{24,28},{1,5},{5,9},{9,... | collective-permute-start | bytes 98312 | tf_op jit(solution)/shard_map/ppermute | solution.py:244
  108.5 4.4 %collective-permute-start.22 = (f32[8,256]{1,0:T(8,128)S(1)}, f32[8,256]{1,0:T(8,128)S(1)}, u32[]{:S(2)}, u32[]{:S(2)}) collective-permute-start(f32[8,256]{1,0:T(8,128)S(1)} %get-tuple-element.59), channel_id=1, source_target_pairs={{0,1},{1,2},{2,3},{4,5},{5,6},{6,7},{8,9},{9,10},{10,11},{12,13},{... | collective-permute-start | bytes 24584 | tf_op jit(solution)/shard_map/ppermute | solution.py:244
  113.0 5.3 %collective-permute-start.23 = (f32[8,256]{1,0:T(8,128)S(1)}, f32[8,256]{1,0:T(8,128)S(1)}, u32[]{:S(2)}, u32[]{:S(2)}) collective-permute-start(f32[8,256]{1,0:T(8,128)S(1)} %get-tuple-element.60), channel_id=1, source_target_pairs={{1,0},{2,1},{3,2},{5,4},{6,5},{7,6},{9,8},{10,9},{11,10},{13,12},{... | collective-permute-start | bytes 24584 | tf_op jit(solution)/shard_map/ppermute | solution.py:244
  (13 other events, 276.2 us)

commit v2 on v1

--- a/solution.py
+++ b/solution.py
@@ -30,6 +30,11 @@
     "b": ((0, COEF_NEAR), (-1, -COEF_NEAR), (1, COEF_FAR), (-2, -COEF_FAR)),
 }
 
+FACE = 5
+INNER = FACE + 1
+GIVEN = INNER + FACE
+TAKEN = 2 * FACE + 2
+
 
 def layers(spec, sides):
     return [(comp, off) for comp, kind in spec for off in sides[kind]]
@@ -41,9 +46,9 @@
 
 
 class Faces:
-    def __init__(self, spec, fields, halos, rows, edges):
+    def __init__(self, spec, fields, core, pair, spread, outer, rows, edges):
         self.spec, self.fields, self.rows, self.edges = spec, fields, rows, edges
-        self.xb, self.xa, self.yb, self.ya, self.zb, self.za = halos
+        self.core, self.pair, self.spread, self.outer = core, pair, spread, outer
         self.nx, self.ny, self.nz = fields.shape[1:]
         self.before = [{k: i for i, k in enumerate(layers(s, BEFORE))} for s in spec]
         self.after = [{k: i for i, k in enumerate(layers(s, AFTER))} for s in spec]
@@ -53,13 +58,29 @@
         for slot, (comp, kind) in enumerate(self.spec[1]):
             for x in range(nx):
                 self.rows[slot, x, 8 : 8 + ny, :] = self.fields[comp, x]
-                for off in BEFORE[kind]:
-                    i = self.before[1][comp, off]
-                    self.rows[slot, x, 8 + off : 9 + off, :] = self.yb[i, x : x + 1, :]
-                for off in AFTER[kind]:
-                    i = self.after[1][comp, off]
-                    self.rows[slot, x, 8 + ny + off : 9 + ny + off, :] = self.ya[i, x : x + 1, :]
-        got = jnp.concatenate([self.zb[...], self.za[...]], axis=0)
+
+        def beside(before, after):
+            for slot, (comp, kind) in enumerate(self.spec[1]):
+                for x in range(nx):
+                    for off in BEFORE[kind]:
+                        i = self.before[1][comp, off]
+                        self.rows[slot, x, 8 + off : 9 + off, :] = before(i, x)
+                    for off in AFTER[kind]:
+                        i = self.after[1][comp, off]
+                        self.rows[slot, x, 8 + ny + off : 9 + ny + off, :] = after(i, x)
+
+        outer = lambda i, x: self.outer[i, x : x + 1, :]
+
+        @pl.when(self.core == 0)
+        def _():
+            beside(outer, lambda i, x: self.pair[GIVEN + INNER + i, x : x + 1, :])
+
+        @pl.when(self.core == 1)
+        def _():
+            beside(lambda i, x: self.pair[INNER + i, x : x + 1, :], outer)
+
+        ends = [self.spread[side * TAKEN + 2 * FACE + self.core] for side in (0, 1)]
+        got = jnp.concatenate([jnp.concatenate([e[:8], e[8:]], axis=1) for e in ends], axis=0)
         row = lax.broadcasted_iota(jnp.int32, (16, nz), 0)
         lane = lax.broadcasted_iota(jnp.int32, (16, nz), 1)
         for slot, (comp, kind) in enumerate(self.spec[2]):
@@ -88,9 +109,9 @@
 
         def plane(at):
             if at < 0:
-                return self.xb[self.before[0][comp, at]]
+                return self.spread[self.core * FACE + self.before[0][comp, at]]
             if at >= self.nx:
-                return self.xa[self.after[0][comp, at - self.nx]]
+                return self.spread[TAKEN + self.core * FACE + self.after[0][comp, at - self.nx]]
             return self.fields[comp, at]
 
         return weighted([plane(x + off) for off, _ in TAPS[kind]])
@@ -118,18 +139,8 @@
         return total
 
 
-def pack(spec, fields, up, down):
+def pack(spec, fields, core, own, given):
     nx, ny, nz = fields.shape[1:]
-    xu, yu, zu = up
-    xd, yd, zd = down
-    for i, (comp, off) in enumerate(layers(spec[0], BEFORE)):
-        xu[i] = fields[comp, nx + off]
-    for i, (comp, off) in enumerate(layers(spec[0], AFTER)):
-        xd[i] = fields[comp, off]
-    for i, (comp, off) in enumerate(layers(spec[1], BEFORE)):
-        yu[i] = fields[comp, :, ny + off, :]
-    for i, (comp, off) in enumerate(layers(spec[1], AFTER)):
-        yd[i] = fields[comp, :, off, :]
     row = lax.broadcasted_iota(jnp.int32, (16, nz), 0)
     lane = lax.broadcasted_iota(jnp.int32, (16, nz), 1)
     before, after = layers(spec[2], BEFORE), layers(spec[2], AFTER)
@@ -150,33 +161,65 @@
             preferred_element_type=jnp.float32,
         )
         total = part if total is None else total + part
-    zu[...] = total[:8]
-    zd[...] = total[8:]
-
-
-def first_kernel(stress, xu, xd, yu, yd, zu, zd):
-    pack(STRESS, stress, (xu, yu, zu), (xd, yd, zd))
-
-
-def velocity_kernel(send, *refs):
-    stress, velocity, buoyancy = refs[:3]
-    out = refs[9]
-    faces = Faces(STRESS, stress, refs[3:9], refs[-2], refs[-1])
+    half = nx * ny // 2
+    ends = [jnp.concatenate([t[:, :half], t[:, half:]], axis=0) for t in (total[:8], total[8:])]
+
+    def write(up, down, inner_up):
+        for ref, sides in ((up, BEFORE), (down, AFTER)):
+            for i, (comp, off) in enumerate(layers(spec[0], sides)):
+                ref[i] = fields[comp, nx + off if sides is BEFORE else off]
+        up[FACE] = ends[0]
+        down[FACE] = ends[1]
+        inner, outer = (BEFORE, AFTER) if inner_up else (AFTER, BEFORE)
+        for ref, sides in ((given, inner), (own, outer)):
+            for i, (comp, off) in enumerate(layers(spec[1], sides)):
+                ref[INNER + i] = fields[comp, :, ny + off if sides is BEFORE else off, :]
+
+    @pl.when(core == 0)
+    def _():
+        write(own, given, True)
+
+    @pl.when(core == 1)
+    def _():
+        write(given, own, False)
+
+
+def first_kernel(core, stress, own, given):
+    pack(STRESS, stress, core[0], own, given)
+
+
+def gather_kernel(core, own, pair, along_x, along_y, along_z):
+    here = core[0]
+    there = 1 - here
+    other = there * GIVEN
+    along_x[pl.ds(here * FACE, FACE)] = own[:FACE]
+    along_x[pl.ds(there * FACE, FACE)] = pair[pl.ds(other, FACE)]
+    along_z[here] = own[FACE]
+    along_z[there] = pair[other + FACE]
+    along_y[...] = own[INNER:]
+
+
+def join_kernel(along_x, along_z, taken):
+    taken[: 2 * FACE] = along_x[...]
+    taken[2 * FACE :] = along_z[...]
+
+
+def velocity_kernel(*refs):
+    core, stress, velocity, buoyancy, pair, spread, outer, out = refs[:8]
+    faces = Faces(STRESS, stress, core[0], pair, spread, outer, refs[-2], refs[-1])
     faces.prepare()
     for x in range(velocity.shape[1]):
         scale = TIME_STEP * buoyancy[x]
         out[0, x] = velocity[0, x] + scale * (faces.dx(0, x) + faces.dy(3, x) + faces.dz(4, x))
         out[1, x] = velocity[1, x] + scale * (faces.dx(3, x) + faces.dy(1, x) + faces.dz(5, x))
         out[2, x] = velocity[2, x] + scale * (faces.dx(4, x) + faces.dy(5, x) + faces.dz(2, x))
-    if send:
-        xu, xd, yu, yd, zu, zd = refs[10:16]
-        pack(VELOCITY, out, (xu, yu, zu), (xd, yd, zd))
+    pack(VELOCITY, out, core[0], *refs[8:10])
 
 
 def stress_kernel(send, *refs):
-    velocity, stress, memory, lam, shear, weight, mech, top_ref, first, table = refs[:10]
-    out, kept = refs[16:18]
-    faces = Faces(VELOCITY, velocity, refs[10:16], refs[-2], refs[-1])
+    core, first, table, velocity, stress, memory, lam, shear, weight, mech, top_ref = refs[:11]
+    pair, spread, outer, out, kept = refs[11:16]
+    faces = Faces(VELOCITY, velocity, core[0], pair, spread, outer, refs[-2], refs[-1])
     faces.prepare()
     nx, ny, nz = lam.shape
     tops = top_ref[...].astype(jnp.float32).T
@@ -206,43 +249,43 @@
             keep = below if comp in (2, 4, 5) else solid
             out[comp, x] = jnp.where(keep, stress[comp, x] + TIME_STEP * (rate - new), 0.0)
     if send:
-        xu, xd, yu, yd, zu, zd = refs[18:24]
-        pack(STRESS, out, (xu, yu, zu), (xd, yd, zd))
-
-
-def face_shapes(spec, nx, ny, nz):
-    shapes = []
-    for sides in (BEFORE, AFTER):
-        shapes.append((len(layers(spec[0], sides)), ny, nz))
-        shapes.append((len(layers(spec[1], sides)), nx, nz))
-        shapes.append((8, nx * ny))
-    xu, yu, zu, xd, yd, zd = [jax.ShapeDtypeStruct(s, jnp.float32) for s in shapes]
-    return [xu, xd, yu, yd, zu, zd]
-
-
-def call(body, outs, operands, scalars=(), scratch=()):
+        pack(STRESS, out, core[0], *refs[16:18])
+
+
+def call(body, outs, operands, scalars=1, scratch=()):
     vmem = pl.BlockSpec(memory_space=pltpu.VMEM)
     smem = pl.BlockSpec(memory_space=pltpu.SMEM)
     return pl.pallas_call(
         body,
         out_shape=outs,
-        in_specs=[smem if i in scalars else vmem for i in range(len(operands))],
+        in_specs=[smem if i < scalars else vmem for i in range(len(operands))],
         out_specs=[vmem] * len(outs),
         scratch_shapes=list(scratch),
         compiler_params=pltpu.CompilerParams(vmem_limit_bytes=24 * 1024 * 1024),
     )(*operands)
 
 
-def exchange(faces):
-    got = []
-    for i, face in enumerate(faces):
-        axis = AXES[i // 2]
-        peers = lax.axis_size(axis)
-        pairs = [(j, j + 1) for j in range(peers - 1)]
-        if i % 2:
-            pairs = [(b, a) for a, b in pairs]
-        got.append(lax.ppermute(face, axis, pairs))
-    return got
+def exchange(core, own, given):
+    plane = own.shape[1:]
+    planes = lambda n: jax.ShapeDtypeStruct((n,) + plane, own.dtype)
+    gx, gy, gz = [lax.axis_size(axis) for axis in AXES]
+    cores = [[j, j + 1] for j in range(0, gy, 2)]
+    pair = lax.all_gather(given, "gy", axis=0, tiled=True, axis_index_groups=cores)
+    along_x, along_y, along_z = call(
+        gather_kernel, [planes(2 * FACE), planes(FACE), planes(2)], [core, own, pair]
+    )
+    to_x, to_z = [], []
+    for j in range(gy):
+        step = 1 - 2 * (j % 2)
+        to_x += [(i * gy + j, (i + step) * gy + j) for i in range(gx) if 0 <= i + step < gx]
+        to_z += [(j * gz + k, j * gz + k + step) for k in range(gz) if 0 <= k + step < gz]
+    to_y = [(j, j + 1) for j in range(1, gy - 1, 2)] + [(j + 1, j) for j in range(1, gy - 1, 2)]
+    got_x = lax.ppermute(along_x, ("gx", "gy"), to_x)
+    got_z = lax.ppermute(along_z, ("gy", "gz"), to_z)
+    outer = lax.ppermute(along_y, "gy", to_y)
+    (taken,) = call(join_kernel, [planes(TAKEN)], [got_x, got_z], scalars=0)
+    spread = lax.all_gather(taken, "gy", axis=0, tiled=True, axis_index_groups=cores)
+    return pair, spread, outer
 
 
 def shards(
@@ -258,29 +301,30 @@
     surface_depth,
 ):
     nx, ny, nz = lame_lambda.shape
+    core = (lax.axis_index("gy") % 2).astype(jnp.int32).reshape(1)
     first = (lax.axis_index("gz") * nz).astype(jnp.int32).reshape(1)
     like = lambda a: jax.ShapeDtypeStruct(a.shape, a.dtype)
+    packed = [jax.ShapeDtypeStruct((GIVEN, ny, nz), jnp.float32)] * 2
     scratch = (
         pltpu.VMEM((3, nx, ny + 16, nz), jnp.float32),
         pltpu.VMEM((3, nx * ny, nz), jnp.float32),
     )
-    stress_faces = face_shapes(STRESS, nx, ny, nz)
-    velocity_faces = face_shapes(VELOCITY, nx, ny, nz)
-    faces = call(first_kernel, stress_faces, [stress])
+    own, given = call(first_kernel, packed, [core, stress])
     for step in range(STEPS):
-        halos = exchange(faces)
-        velocity, *faces = call(
-            functools.partial(velocity_kernel, True),
-            [like(velocity)] + velocity_faces,
-            [stress, velocity, buoyancy, *halos],
+        velocity, own, given = call(
+            velocity_kernel,
+            [like(velocity)] + packed,
+            [core, stress, velocity, buoyancy, *exchange(core, own, given)],
             scratch=scratch,
         )
-        halos = exchange(faces)
         send = step < STEPS - 1
-        stress, memory, *faces = call(
+        stress, memory, *rest = call(
             functools.partial(stress_kernel, send),
-            [like(stress), like(memory)] + (stress_faces if send else []),
+            [like(stress), like(memory)] + (packed if send else []),
             [
+                core,
+                first,
+                decay_table,
                 velocity,
                 stress,
                 memory,
@@ -289,13 +333,13 @@
                 anelastic_weight,
                 mech_index,
                 surface_depth,
-                first,
-                decay_table,
-                *halos,
+                *exchange(core, own, given),
             ],
-            scalars=(8, 9),
+            scalars=3,
             scratch=scratch,
         )
+        if send:
+            own, given = rest
     return (velocity, stress, memory)
 
 

time: 123 us -> 85.8 us (0.70)
  the two profiles are of different devices: /device:TPU:15 before, /device:TPU:1 now
where the time goes in v2:
time: 85.8 us; the launch traced here: 84.5 us
  starting transfers between devices  49.4 us (58%)
  blocking collectives  22.4 us (26%)
  Pallas kernels  9.48 us (11%)
  local copies, waits for them, and re-layouts  1.78 us (2%)
  between operations  0.99 us (1%)
    ppermute x4, starting transfers between devices, exchange(): outer = lax.ppermute(along_y, 'gy', to_y)  38.8 us
    all_gather x4, blocking collectives, exchange(): lax.all_gather(given, 'gy', axis=0, tiled=True, axis_index_groups=cores)  14.4 us
    pallas_call x13, Pallas kernels, call(): pl.pallas_call(body, out_shape=outs, in_specs=[smem if i < scalars else v...  9.48 us
    all_gather x4, blocking collectives, exchange(): lax.all_gather(taken, 'gy', axis=0, tiled=True, axis_index_groups=cores)  8.05 us
    ppermute x4, starting transfers between devices, exchange(): got_x = lax.ppermute(along_x, ('gx', 'gy'), to_x)  5.43 us
    ppermute x4, starting transfers between devices, exchange(): got_z = lax.ppermute(along_z, ('gy', 'gz'), to_z)  5.17 us
    unnamed x24, local copies, waits for them, and re-layouts  1.78 us
  transfers between devices with their start and end apart: 12, of which 1 were waited for; matrix products, arithmetic and copies ran while one was open for 0% of the time, Pallas kernels for 0%

profile of v2, /device:TPU:1, one launch (start us, length us, event | category | flops | bytes accessed | tf_op | source)
XLA Modules:
  0.0 84.5 jit_solution(13004158427537809123)
XLA Ops:
  2.3 8.4 %all_gather.24.pair.refs_4_ = f32[22,16,128]{2,1,0:T(8,128)S(1)} all-gather(f32[11,16,128]{2,1,0:T(8,128)S(1)} %get-tuple-element.29), channel_id=1, replica_groups={{0,4},{8,12},{16,20},{24,28},{1,5},{9,13},{17,21},{25,29},{2,6},{10,14}..., dimensions={0}, use_global_device_ids=true | all-gather | bytes 270336 | tf_op jit(solution)/shard_map/all_gather | solution.py:273
  10.7 1.4 %collective-permute-start = (f32[10,16,128]{2,1,0:T(8,128)S(1)}, f32[10,16,128]{2,1,0:T(8,128)S(1)}, u32[]{:S(2)}, u32[]{:S(2)}) collective-permute-start(f32[10,16,128]{2,1,0:T(8,128)S(1)} %get-tuple-element.31), channel_id=1, source_target_pairs={{0,32},{32,64},{64,96},{96,128},{128,160},{160,192},{192,224},{224... | collective-permute-start | bytes 245768 | tf_op jit(solution)/shard_map/ppermute | solution.py:283
  12.2 1.3 %collective-permute-start.1 = (f32[2,16,128]{2,1,0:T(8,128)S(1)}, f32[2,16,128]{2,1,0:T(8,128)S(1)}, u32[]{:S(2)}, u32[]{:S(2)}) collective-permute-start(f32[2,16,128]{2,1,0:T(8,128)S(1)} %get-tuple-element.32), channel_id=1, source_target_pairs={{0,1},{1,2},{2,3},{5,4},{6,5},{7,6},{8,9},{9,10},{10,11},{13,12},{... | collective-permute-start | bytes 49160 | tf_op jit(solution)/shard_map/ppermute | solution.py:284
  13.5 8.4 %collective-permute-start.2 = (f32[5,16,128]{2,1,0:T(8,128)S(1)}, f32[5,16,128]{2,1,0:T(8,128)S(1)}, u32[]{:S(2)}, u32[]{:S(2)}) collective-permute-start(f32[5,16,128]{2,1,0:T(8,128)S(1)} %get-tuple-element.33), channel_id=1, source_target_pairs={{4,8},{12,16},{20,24},{8,4},{16,12},{24,20},{5,9},{13,17},{21,25},... | collective-permute-start | bytes 122888 | tf_op jit(solution)/shard_map/ppermute | solution.py:285
  21.9 2.1 %all_gather.25.refs_5_ = f32[24,16,128]{2,1,0:T(8,128)S(1)} all-gather(f32[12,16,128]{2,1,0:T(8,128)S(1)} %shard_map.123), channel_id=1, replica_groups={{0,4},{8,12},{16,20},{24,28},{1,5},{9,13},{17,21},{25,29},{2,6},{10,14}..., dimensions={0}, use_global_device_ids=true | all-gather | bytes 294912 | tf_op jit(solution)/shard_map/all_gather | solution.py:287
  24.1 1.5 %shard_map.124 = (f32[3,16,16,128]{3,2,1,0:T(8,128)S(1)}, f32[11,16,128]{2,1,0:T(8,128)S(1)}, f32[11,16,128]{2,1,0:T(8,128)S(1)}) custom-call(s32[1]{0:T(128)} %bitcast.core.refs_0_, f32[6,16,16,128]{3,2,1,0:T(8,128)S(1)} %copy-done.1, f32[3,16,16,128]{3,2,1,0:T(8,128)S(1)} %copy-done.8, f32[16,16,128]{2,1,0:T(8,128)S(1)} %copy-done.3, ...), custom_call_target="tpu_custom_call" | custom-call | tf_op jit(solution)/shard_map/pallas_call | solution.py:258
  25.6 2.1 %all_gather.26.pair.refs_11_ = f32[22,16,128]{2,1,0:T(8,128)S(1)} all-gather(f32[11,16,128]{2,1,0:T(8,128)S(1)} %get-tuple-element.35), channel_id=1, replica_groups={{0,4},{8,12},{16,20},{24,28},{1,5},{9,13},{17,21},{25,29},{2,6},{10,14}..., dimensions={0}, use_global_device_ids=true | all-gather | bytes 270336 | tf_op jit(solution)/shard_map/all_gather | solution.py:273
  27.7 1.3 %collective-permute-start.3 = (f32[10,16,128]{2,1,0:T(8,128)S(1)}, f32[10,16,128]{2,1,0:T(8,128)S(1)}, u32[]{:S(2)}, u32[]{:S(2)}) collective-permute-start(f32[10,16,128]{2,1,0:T(8,128)S(1)} %get-tuple-element.37), channel_id=1, source_target_pairs={{0,32},{32,64},{64,96},{96,128},{128,160},{160,192},{192,224},{224... | collective-permute-start | bytes 245768 | tf_op jit(solution)/shard_map/ppermute | solution.py:283
  29.0 1.3 %collective-permute-start.4 = (f32[2,16,128]{2,1,0:T(8,128)S(1)}, f32[2,16,128]{2,1,0:T(8,128)S(1)}, u32[]{:S(2)}, u32[]{:S(2)}) collective-permute-start(f32[2,16,128]{2,1,0:T(8,128)S(1)} %get-tuple-element.38), channel_id=1, source_target_pairs={{0,1},{1,2},{2,3},{5,4},{6,5},{7,6},{8,9},{9,10},{10,11},{13,12},{... | collective-permute-start | bytes 49160 | tf_op jit(solution)/shard_map/ppermute | solution.py:284
  30.3 11.8 %collective-permute-start.5 = (f32[5,16,128]{2,1,0:T(8,128)S(1)}, f32[5,16,128]{2,1,0:T(8,128)S(1)}, u32[]{:S(2)}, u32[]{:S(2)}) collective-permute-start(f32[5,16,128]{2,1,0:T(8,128)S(1)} %get-tuple-element.39), channel_id=1, source_target_pairs={{4,8},{12,16},{20,24},{8,4},{16,12},{24,20},{5,9},{13,17},{21,25},... | collective-permute-start | bytes 122888 | tf_op jit(solution)/shard_map/ppermute | solution.py:285
  42.2 2.1 %all_gather.27.refs_12_ = f32[24,16,128]{2,1,0:T(8,128)S(1)} all-gather(f32[12,16,128]{2,1,0:T(8,128)S(1)} %shard_map.126), channel_id=1, replica_groups={{0,4},{8,12},{16,20},{24,28},{1,5},{9,13},{17,21},{25,29},{2,6},{10,14}..., dimensions={0}, use_global_device_ids=true | all-gather | bytes 294912 | tf_op jit(solution)/shard_map/all_gather | solution.py:287
  44.9 2.3 %shard_map.127 = (f32[6,16,16,128]{3,2,1,0:T(8,128)S(1)}, f32[6,16,16,128]{3,2,1,0:T(8,128)S(1)}, f32[11,16,128]{2,1,0:T(8,128)S(1)}, f32[11,16,128]{2,1,0:T(8,128)S(1)}) custom-call(s32[1]{0:T(128)} %bitcast.core.refs_0_, s32[1]{0:T(128)} %bitcast.1.refs_1_, f32[8]{0:T(128)S(1)} %copy-done.11, f32[3,16,16,128]{3,2,1,0:T(8,128)S(1)} %get-tuple-element.34.refs_3_.refs_2_, ...), custom_call_target="tpu_custom_call" | custom-call | tf_op jit(solution)/shard_map/pallas_call | solution.py:258
  47.2 1.9 %all_gather.28.pair.refs_4_ = f32[22,16,128]{2,1,0:T(8,128)S(1)} all-gather(f32[11,16,128]{2,1,0:T(8,128)S(1)} %get-tuple-element.41), channel_id=1, replica_groups={{0,4},{8,12},{16,20},{24,28},{1,5},{9,13},{17,21},{25,29},{2,6},{10,14}..., dimensions={0}, use_global_device_ids=true | all-gather | bytes 270336 | tf_op jit(solution)/shard_map/all_gather | solution.py:273
  49.2 1.3 %collective-permute-start.6 = (f32[10,16,128]{2,1,0:T(8,128)S(1)}, f32[10,16,128]{2,1,0:T(8,128)S(1)}, u32[]{:S(2)}, u32[]{:S(2)}) collective-permute-start(f32[10,16,128]{2,1,0:T(8,128)S(1)} %get-tuple-element.43), channel_id=1, source_target_pairs={{0,32},{32,64},{64,96},{96,128},{128,160},{160,192},{192,224},{224... | collective-permute-start | bytes 245768 | tf_op jit(solution)/shard_map/ppermute | solution.py:283
  50.5 1.3 %collective-permute-start.7 = (f32[2,16,128]{2,1,0:T(8,128)S(1)}, f32[2,16,128]{2,1,0:T(8,128)S(1)}, u32[]{:S(2)}, u32[]{:S(2)}) collective-permute-start(f32[2,16,128]{2,1,0:T(8,128)S(1)} %get-tuple-element.44), channel_id=1, source_target_pairs={{0,1},{1,2},{2,3},{5,4},{6,5},{7,6},{8,9},{9,10},{10,11},{13,12},{... | collective-permute-start | bytes 49160 | tf_op jit(solution)/shard_map/ppermute | solution.py:284
  51.8 9.9 %collective-permute-start.8 = (f32[5,16,128]{2,1,0:T(8,128)S(1)}, f32[5,16,128]{2,1,0:T(8,128)S(1)}, u32[]{:S(2)}, u32[]{:S(2)}) collective-permute-start(f32[5,16,128]{2,1,0:T(8,128)S(1)} %get-tuple-element.45), channel_id=1, source_target_pairs={{4,8},{12,16},{20,24},{8,4},{16,12},{24,20},{5,9},{13,17},{21,25},... | collective-permute-start | bytes 122888 | tf_op jit(solution)/shard_map/ppermute | solution.py:285
  61.7 1.9 %all_gather.29.refs_5_ = f32[24,16,128]{2,1,0:T(8,128)S(1)} all-gather(f32[12,16,128]{2,1,0:T(8,128)S(1)} %shard_map.129), channel_id=1, replica_groups={{0,4},{8,12},{16,20},{24,28},{1,5},{9,13},{17,21},{25,29},{2,6},{10,14}..., dimensions={0}, use_global_device_ids=true | all-gather | bytes 294912 | tf_op jit(solution)/shard_map/all_gather | solution.py:287
  63.7 2.3 %shard_map.130 = (f32[3,16,16,128]{3,2,1,0:T(8,128)}, f32[11,16,128]{2,1,0:T(8,128)S(1)}, f32[11,16,128]{2,1,0:T(8,128)S(1)}) custom-call(s32[1]{0:T(128)} %bitcast.core.refs_0_, f32[6,16,16,128]{3,2,1,0:T(8,128)S(1)} %get-tuple-element.40.refs_1_.refs_4_, f32[3,16,16,128]{3,2,1,0:T(8,128)S(1)} %get-tuple-element.34.refs_3_.refs_2_, ...), custom_call_target="tpu_custom_call" | custom-call | tf_op jit(solution)/shard_map/pallas_call | solution.py:258
  66.0 1.9 %all_gather.30.pair.refs_11_ = f32[22,16,128]{2,1,0:T(8,128)S(1)} all-gather(f32[11,16,128]{2,1,0:T(8,128)S(1)} %get-tuple-element.48), channel_id=1, replica_groups={{0,4},{8,12},{16,20},{24,28},{1,5},{9,13},{17,21},{25,29},{2,6},{10,14}..., dimensions={0}, use_global_device_ids=true | all-gather | bytes 270336 | tf_op jit(solution)/shard_map/all_gather | solution.py:273
  68.0 1.4 %collective-permute-start.9 = (f32[10,16,128]{2,1,0:T(8,128)S(1)}, f32[10,16,128]{2,1,0:T(8,128)S(1)}, u32[]{:S(2)}, u32[]{:S(2)}) collective-permute-start(f32[10,16,128]{2,1,0:T(8,128)S(1)} %get-tuple-element.50), channel_id=1, source_target_pairs={{0,32},{32,64},{64,96},{96,128},{128,160},{160,192},{192,224},{224... | collective-permute-start | bytes 245768 | tf_op jit(solution)/shard_map/ppermute | solution.py:283
  69.4 1.3 %collective-permute-start.10 = (f32[2,16,128]{2,1,0:T(8,128)S(1)}, f32[2,16,128]{2,1,0:T(8,128)S(1)}, u32[]{:S(2)}, u32[]{:S(2)}) collective-permute-start(f32[2,16,128]{2,1,0:T(8,128)S(1)} %get-tuple-element.51), channel_id=1, source_target_pairs={{0,1},{1,2},{2,3},{5,4},{6,5},{7,6},{8,9},{9,10},{10,11},{13,12},{... | collective-permute-start | bytes 49160 | tf_op jit(solution)/shard_map/ppermute | solution.py:284
  70.7 8.7 %collective-permute-start.11 = (f32[5,16,128]{2,1,0:T(8,128)S(1)}, f32[5,16,128]{2,1,0:T(8,128)S(1)}, u32[]{:S(2)}, u32[]{:S(2)}) collective-permute-start(f32[5,16,128]{2,1,0:T(8,128)S(1)} %get-tuple-element.52), channel_id=1, source_target_pairs={{4,8},{12,16},{20,24},{8,4},{16,12},{24,20},{5,9},{13,17},{21,25},... | collective-permute-start | bytes 122888 | tf_op jit(solution)/shard_map/ppermute | solution.py:285
  79.8 1.9 %all_gather.31.refs_12_ = f32[24,16,128]{2,1,0:T(8,128)S(1)} all-gather(f32[12,16,128]{2,1,0:T(8,128)S(1)} %shard_map.132), channel_id=1, replica_groups={{0,4},{8,12},{16,20},{24,28},{1,5},{9,13},{17,21},{25,29},{2,6},{10,14}..., dimensions={0}, use_global_device_ids=true | all-gather | bytes 294912 | tf_op jit(solution)/shard_map/all_gather | solution.py:287
  81.8 2.7 %shard_map.133 = (f32[6,16,16,128]{3,2,1,0:T(8,128)}, f32[6,16,16,128]{3,2,1,0:T(8,128)}) custom-call(s32[1]{0:T(128)} %bitcast.core.refs_0_, s32[1]{0:T(128)} %bitcast.1.refs_1_, f32[8]{0:T(128)S(1)} %copy-done.11, f32[3,16,16,128]{3,2,1,0:T(8,128)S(1)} %copy-done.9, f32[6,16,16,128]{3,2,1,0:T(8,128)S(1)} %get-tuple-element.40.refs_1_.refs_4_, ...), custom_call_target="tpu_custom_call" | custom-call | tf_op jit(solution)/shard_map/pallas_call | solution.py:258
  (45 shorter events, 2.7 us)
Async XLA Ops:
  0.6 1.1 %copy-start = (f32[6,16,16,128]{3,2,1,0:T(8,128)S(1)}, f32[6,16,16,128]{3,2,1,0:T(8,128)}, u32[]{:S(2)}) copy-start(f32[6,16,16,128]{3,2,1,0:T(8,128)} %refs_4_.1) | copy-start | bytes 2359300
  1.8 22.2 %copy-start.1 = (f32[6,16,16,128]{3,2,1,0:T(8,128)S(1)}, f32[6,16,16,128]{3,2,1,0:T(8,128)}, u32[]{:S(2)}) copy-start(f32[6,16,16,128]{3,2,1,0:T(8,128)} %refs_4_.1) | copy-start | bytes 2359300
  10.7 13.3 %copy-start.8 = (f32[3,16,16,128]{3,2,1,0:T(8,128)S(1)}, f32[3,16,16,128]{3,2,1,0:T(8,128)}, u32[]{:S(2)}) copy-start(f32[3,16,16,128]{3,2,1,0:T(8,128)} %refs_2_.3) | copy-start | bytes 1179652
  10.7 11.2 %collective-permute-start = (f32[10,16,128]{2,1,0:T(8,128)S(1)}, f32[10,16,128]{2,1,0:T(8,128)S(1)}, u32[]{:S(2)}, u32[]{:S(2)}) collective-permute-start(f32[10,16,128]{2,1,0:T(8,128)S(1)} %get-tuple-element.31), channel_id=1, source_target_pairs={{0,32},{32,64},{64,96},{96,128},{128,160},{160,192},{192,224},{224... | collective-permute-start | bytes 245768 | tf_op jit(solution)/shard_map/ppermute | solution.py:283
  12.2 9.7 %collective-permute-start.1 = (f32[2,16,128]{2,1,0:T(8,128)S(1)}, f32[2,16,128]{2,1,0:T(8,128)S(1)}, u32[]{:S(2)}, u32[]{:S(2)}) collective-permute-start(f32[2,16,128]{2,1,0:T(8,128)S(1)} %get-tuple-element.32), channel_id=1, source_target_pairs={{0,1},{1,2},{2,3},{5,4},{6,5},{7,6},{8,9},{9,10},{10,11},{13,12},{... | collective-permute-start | bytes 49160 | tf_op jit(solution)/shard_map/ppermute | solution.py:284
  13.5 10.5 %collective-permute-start.2 = (f32[5,16,128]{2,1,0:T(8,128)S(1)}, f32[5,16,128]{2,1,0:T(8,128)S(1)}, u32[]{:S(2)}, u32[]{:S(2)}) collective-permute-start(f32[5,16,128]{2,1,0:T(8,128)S(1)} %get-tuple-element.33), channel_id=1, source_target_pairs={{4,8},{12,16},{20,24},{8,4},{16,12},{24,20},{5,9},{13,17},{21,25},... | collective-permute-start | bytes 122888 | tf_op jit(solution)/shard_map/ppermute | solution.py:285
  21.9 2.1 %copy-start.3 = (f32[16,16,128]{2,1,0:T(8,128)S(1)}, f32[16,16,128]{2,1,0:T(8,128)}, u32[]{:S(2)}) copy-start(f32[16,16,128]{2,1,0:T(8,128)} %refs_3_.3) | copy-start | bytes 393220
  24.0 20.2 %copy-start.6 = (f32[16,16,128]{2,1,0:T(8,128)S(1)}, f32[16,16,128]{2,1,0:T(8,128)}, u32[]{:S(2)}) copy-start(f32[16,16,128]{2,1,0:T(8,128)} %refs_8_.3) | copy-start | bytes 393220
  24.0 20.2 %copy-start.7 = (s32[16,16,128]{2,1,0:T(8,128)S(1)}, s32[16,16,128]{2,1,0:T(8,128)}, u32[]{:S(2)}) copy-start(s32[16,16,128]{2,1,0:T(8,128)} %refs_9_.3) | copy-start | bytes 393220
  24.0 20.2 %copy-start.10 = (s32[16,16]{1,0:T(8,128)S(1)}, s32[16,16]{1,0:T(8,128)}, u32[]{:S(2)}) copy-start(s32[16,16]{1,0:T(8,128)} %refs_10_.3) | copy-start | bytes 3076
  25.6 18.7 %copy-start.2 = (f32[6,16,16,128]{3,2,1,0:T(8,128)S(1)}, f32[6,16,16,128]{3,2,1,0:T(8,128)}, u32[]{:S(2)}) copy-start(f32[6,16,16,128]{3,2,1,0:T(8,128)} %refs_5_.1) | copy-start | bytes 2359300
  27.7 14.4 %collective-permute-start.3 = (f32[10,16,128]{2,1,0:T(8,128)S(1)}, f32[10,16,128]{2,1,0:T(8,128)S(1)}, u32[]{:S(2)}, u32[]{:S(2)}) collective-permute-start(f32[10,16,128]{2,1,0:T(8,128)S(1)} %get-tuple-element.37), channel_id=1, source_target_pairs={{0,32},{32,64},{64,96},{96,128},{128,160},{160,192},{192,224},{224... | collective-permute-start | bytes 245768 | tf_op jit(solution)/shard_map/ppermute | solution.py:283
  29.0 13.1 %collective-permute-start.4 = (f32[2,16,128]{2,1,0:T(8,128)S(1)}, f32[2,16,128]{2,1,0:T(8,128)S(1)}, u32[]{:S(2)}, u32[]{:S(2)}) collective-permute-start(f32[2,16,128]{2,1,0:T(8,128)S(1)} %get-tuple-element.38), channel_id=1, source_target_pairs={{0,1},{1,2},{2,3},{5,4},{6,5},{7,6},{8,9},{9,10},{10,11},{13,12},{... | collective-permute-start | bytes 49160 | tf_op jit(solution)/shard_map/ppermute | solution.py:284
  30.3 13.9 %collective-permute-start.5 = (f32[5,16,128]{2,1,0:T(8,128)S(1)}, f32[5,16,128]{2,1,0:T(8,128)S(1)}, u32[]{:S(2)}, u32[]{:S(2)}) collective-permute-start(f32[5,16,128]{2,1,0:T(8,128)S(1)} %get-tuple-element.39), channel_id=1, source_target_pairs={{4,8},{12,16},{20,24},{8,4},{16,12},{24,20},{5,9},{13,17},{21,25},... | collective-permute-start | bytes 122888 | tf_op jit(solution)/shard_map/ppermute | solution.py:285
  42.1 2.1 %copy-start.4 = (f32[16,16,128]{2,1,0:T(8,128)S(1)}, f32[16,16,128]{2,1,0:T(8,128)}, u32[]{:S(2)}) copy-start(f32[16,16,128]{2,1,0:T(8,128)} %refs_6_.3) | copy-start | bytes 393220
  42.2 2.1 %copy-start.5 = (f32[16,16,128]{2,1,0:T(8,128)S(1)}, f32[16,16,128]{2,1,0:T(8,128)}, u32[]{:S(2)}) copy-start(f32[16,16,128]{2,1,0:T(8,128)} %refs_7_.3) | copy-start | bytes 393220
  44.2 0.7 copy-start.11
  49.2 12.5 %collective-permute-start.6 = (f32[10,16,128]{2,1,0:T(8,128)S(1)}, f32[10,16,128]{2,1,0:T(8,128)S(1)}, u32[]{:S(2)}, u32[]{:S(2)}) collective-permute-start(f32[10,16,128]{2,1,0:T(8,128)S(1)} %get-tuple-element.43), channel_id=1, source_target_pairs={{0,32},{32,64},{64,96},{96,128},{128,160},{160,192},{192,224},{224... | collective-permute-start | bytes 245768 | tf_op jit(solution)/shard_map/ppermute | solution.py:283
  50.5 11.2 %collective-permute-start.7 = (f32[2,16,128]{2,1,0:T(8,128)S(1)}, f32[2,16,128]{2,1,0:T(8,128)S(1)}, u32[]{:S(2)}, u32[]{:S(2)}) collective-permute-start(f32[2,16,128]{2,1,0:T(8,128)S(1)} %get-tuple-element.44), channel_id=1, source_target_pairs={{0,1},{1,2},{2,3},{5,4},{6,5},{7,6},{8,9},{9,10},{10,11},{13,12},{... | collective-permute-start | bytes 49160 | tf_op jit(solution)/shard_map/ppermute | solution.py:284
  51.8 11.9 %collective-permute-start.8 = (f32[5,16,128]{2,1,0:T(8,128)S(1)}, f32[5,16,128]{2,1,0:T(8,128)S(1)}, u32[]{:S(2)}, u32[]{:S(2)}) collective-permute-start(f32[5,16,128]{2,1,0:T(8,128)S(1)} %get-tuple-element.45), channel_id=1, source_target_pairs={{4,8},{12,16},{20,24},{8,4},{16,12},{24,20},{5,9},{13,17},{21,25},... | collective-permute-start | bytes 122888 | tf_op jit(solution)/shard_map/ppermute | solution.py:285
  67.9 13.8 %copy-start.9 = (f32[3,16,16,128]{3,2,1,0:T(8,128)S(1)}, f32[3,16,16,128]{3,2,1,0:T(8,128)}, u32[]{:S(2)}) copy-start(f32[3,16,16,128]{3,2,1,0:T(8,128)} %get-tuple-element.26.refs_3_) | copy-start | bytes 1179652
  68.0 11.9 %collective-permute-start.9 = (f32[10,16,128]{2,1,0:T(8,128)S(1)}, f32[10,16,128]{2,1,0:T(8,128)S(1)}, u32[]{:S(2)}, u32[]{:S(2)}) collective-permute-start(f32[10,16,128]{2,1,0:T(8,128)S(1)} %get-tuple-element.50), channel_id=1, source_target_pairs={{0,32},{32,64},{64,96},{96,128},{128,160},{160,192},{192,224},{224... | collective-permute-start | bytes 245768 | tf_op jit(solution)/shard_map/ppermute | solution.py:283
  69.4 10.0 %collective-permute-start.10 = (f32[2,16,128]{2,1,0:T(8,128)S(1)}, f32[2,16,128]{2,1,0:T(8,128)S(1)}, u32[]{:S(2)}, u32[]{:S(2)}) collective-permute-start(f32[2,16,128]{2,1,0:T(8,128)S(1)} %get-tuple-element.51), channel_id=1, source_target_pairs={{0,1},{1,2},{2,3},{5,4},{6,5},{7,6},{8,9},{9,10},{10,11},{13,12},{... | collective-permute-start | bytes 49160 | tf_op jit(solution)/shard_map/ppermute | solution.py:284
  70.7 11.1 %collective-permute-start.11 = (f32[5,16,128]{2,1,0:T(8,128)S(1)}, f32[5,16,128]{2,1,0:T(8,128)S(1)}, u32[]{:S(2)}, u32[]{:S(2)}) collective-permute-start(f32[5,16,128]{2,1,0:T(8,128)S(1)} %get-tuple-element.52), channel_id=1, source_target_pairs={{4,8},{12,16},{20,24},{8,4},{16,12},{24,20},{5,9},{13,17},{21,25},... | collective-permute-start | bytes 122888 | tf_op jit(solution)/shard_map/ppermute | solution.py:285

commit v3 on v2

v3 whole, which is shorter than its diff:
```python
import jax
import jax.numpy as jnp
from jax import lax
from jax.experimental import pallas as pl
from jax.experimental.pallas import tpu as pltpu
from jax.sharding import PartitionSpec as P

STEPS = 2
COEF_NEAR = 9.0 / 8.0
COEF_FAR = -1.0 / 24.0
TIME_STEP = 0.2
AXES = ("gx", "gy", "gz")

STRESS = (
    ((0, "f"), (3, "b"), (4, "b")),
    ((3, "b"), (1, "f"), (5, "b")),
    ((4, "b"), (5, "b"), (2, "f")),
)
VELOCITY = (
    ((0, "b"), (1, "f"), (2, "f")),
    ((1, "b"), (0, "f"), (2, "f")),
    ((2, "b"), (0, "f"), (1, "f")),
)
BEFORE = {"f": (-1,), "b": (-2, -1)}
AFTER = {"f": (0, 1), "b": (0,)}
TAPS = {
    "f": ((1, COEF_NEAR), (0, -COEF_NEAR), (2, COEF_FAR), (-1, -COEF_FAR)),
    "b": ((0, COEF_NEAR), (-1, -COEF_NEAR), (1, COEF_FAR), (-2, -COEF_FAR)),
}

FACE = 5
GIVEN = 1 + FACE
TAKEN = 2 * FACE + 2


def edge_planes(nx):
    return {0: 0, 1: 1, nx - 2: 2, nx - 1: 3}


def layers(spec, sides):
    return [(comp, off) for comp, kind in spec for off in sides[kind]]


def weighted(taps):
    a, b, c, d = taps
    return COEF_NEAR * (a - b) + COEF_FAR * (c - d)


class Faces:
    def __init__(self, spec, fields, planes, core, pair, spread, outer, rows, edges):
        self.spec, self.fields, self.rows, self.edges = spec, fields, rows, edges
        self.planes = planes
        self.core, self.pair, self.spread, self.outer = core, pair, spread, outer
        self.nx, self.ny, self.nz = fields.shape[1:]
        self.before = [{k: i for i, k in enumerate(layers(s, BEFORE))} for s in spec]
        self.after = [{k: i for i, k in enumerate(layers(s, AFTER))} for s in spec]

    def prepare(self):
        nx, ny, nz = self.nx, self.ny, self.nz
        for slot, (comp, kind) in enumerate(self.spec[1]):
            for x in self.planes:
                self.rows[slot, x, 8 : 8 + ny, :] = self.fields[comp, x]

        def beside(before, after):
            for slot, (comp, kind) in enumerate(self.spec[1]):
                for x in self.planes:
                    for off in BEFORE[kind]:
                        i = self.before[1][comp, off]
                        self.rows[slot, x, 8 + off : 9 + off, :] = before(i, x)
                    for off in AFTER[kind]:
                        i = self.after[1][comp, off]
                        self.rows[slot, x, 8 + ny + off : 9 + ny + off, :] = after(i, x)

        outer = lambda i, x: self.outer[i, x : x + 1, :]

        @pl.when(self.core == 0)
        def _():
            beside(outer, lambda i, x: self.pair[GIVEN + 1 + i, x : x + 1, :])

        @pl.when(self.core == 1)
        def _():
            beside(lambda i, x: self.pair[1 + i, x : x + 1, :], outer)

        ends = [self.spread[side * TAKEN + 2 * FACE + self.core] for side in (0, 1)]
        got = jnp.concatenate([jnp.concatenate([e[:8], e[8:]], axis=1) for e in ends], axis=0)
        row = lax.broadcasted_iota(jnp.int32, (16, nz), 0)
        lane = lax.broadcasted_iota(jnp.int32, (16, nz), 1)
        for slot, (comp, kind) in enumerate(self.spec[2]):
            weights = jnp.zeros((16, nz), jnp.float32)
            for shift, weight in TAPS[kind]:
                for off in BEFORE[kind]:
                    at = off - shift
                    if 0 <= at < nz:
                        hit = (row == self.before[2][comp, off]) & (lane == at)
                        weights = weights + jnp.where(hit, weight, 0.0)
                for off in AFTER[kind]:
                    at = nz + off - shift
                    if 0 <= at < nz:
                        hit = (row == 8 + self.after[2][comp, off]) & (lane == at)
                        weights = weights + jnp.where(hit, weight, 0.0)
            for start, stop in self.columns():
                self.edges[slot, start:stop, :] = lax.dot_general(
                    got[:, start:stop],
                    weights,
                    (((0,), (0,)), ((), ())),
                    precision=lax.Precision.HIGHEST,
                    preferred_element_type=jnp.float32,
                )

    def columns(self):
        if len(self.planes) > 4:
            return [(0, self.nx * self.ny)]
        return [(0, 2 * self.ny), ((self.nx - 2) * self.ny, self.nx * self.ny)]

    def dx(self, comp, x):
        kind = dict(self.spec[0])[comp]

        def plane(at):
            if at < 0:
                return self.spread[self.core * FACE + self.before[0][comp, at]]
            if at >= self.nx:
                return self.spread[TAKEN + self.core * FACE + self.after[0][comp, at - self.nx]]
            return self.fields[comp, at]

        return weighted([plane(x + off) for off, _ in TAPS[kind]])

    def dy(self, comp, x):
        slot = [c for c, _ in self.spec[1]].index(comp)
        kind = self.spec[1][slot][1]
        return weighted(
            [self.rows[slot, x, 8 + off : 8 + off + self.ny, :] for off, _ in TAPS[kind]]
        )

    def dz(self, comp, x):
        slot = [c for c, _ in self.spec[2]].index(comp)
        kind = self.spec[2][slot][1]
        here = self.fields[comp, x]
        lane = lax.broadcasted_iota(jnp.int32, (1, self.nz), 1)
        total = self.edges[slot, x * self.ny : (x + 1) * self.ny, :]
        for off, weight in TAPS[kind]:
            if off == 0:
                total = total + weight * here
            else:
                inside = (lane + off >= 0) & (lane + off < self.nz)
                moved = pltpu.roll(here, (-off) % self.nz, 1)
                total = total + jnp.where(inside, weight, 0.0) * moved
        return total


def pack_x(spec, fields, place, nx, core, own, given):
    def write(up, down):
        for i, (comp, off) in enumerate(layers(spec[0], BEFORE)):
            up[i] = fields[comp, place[nx + off]]
        for i, (comp, off) in enumerate(layers(spec[0], AFTER)):
            down[i] = fields[comp, place[off]]

    @pl.when(core == 0)
    def _():
        write(own, given)

    @pl.when(core == 1)
    def _():
        write(given, own)


def pack_yz(spec, fields, core, own, given):
    nx, ny, nz = fields.shape[1:]
    row = lax.broadcasted_iota(jnp.int32, (16, nz), 0)
    lane = lax.broadcasted_iota(jnp.int32, (16, nz), 1)
    before, after = layers(spec[2], BEFORE), layers(spec[2], AFTER)
    total = None
    for comp, _ in spec[2]:
        pick = jnp.zeros((16, nz), jnp.float32)
        for i, (c, off) in enumerate(before):
            if c == comp:
                pick = jnp.where((row == i) & (lane == nz + off), 1.0, pick)
        for i, (c, off) in enumerate(after):
            if c == comp:
                pick = jnp.where((row == 8 + i) & (lane == off), 1.0, pick)
        part = lax.dot_general(
            pick,
            fields[comp].reshape(nx * ny, nz),
            (((1,), (1,)), ((), ())),
            precision=lax.Precision.HIGHEST,
            preferred_element_type=jnp.float32,
        )
        total = part if total is None else total + part
    half = nx * ny // 2
    ends = [jnp.concatenate([t[:, :half], t[:, half:]], axis=0) for t in (total[:8], total[8:])]

    def write(up, down, inner, outer):
        up[0] = ends[0]
        down[0] = ends[1]
        for ref, sides in ((given, inner), (own, outer)):
            for i, (comp, off) in enumerate(layers(spec[1], sides)):
                ref[1 + i] = fields[comp, :, ny + off if sides is BEFORE else off, :]

    @pl.when(core == 0)
    def _():
        write(own, given, BEFORE, AFTER)

    @pl.when(core == 1)
    def _():
        write(given, own, AFTER, BEFORE)


def first_x_kernel(core, stress, own, given):
    nx = stress.shape[1]
    pack_x(STRESS, stress, {x: x for x in range(nx)}, nx, core[0], own, given)


def first_yz_kernel(core, stress, behind, own, given):
    pack_yz(STRESS, stress, core[0], own, given)


def gather_x_kernel(core, own, pair, along_x):
    here = core[0]
    there = 1 - here
    along_x[pl.ds(here * FACE, FACE)] = own[...]
    along_x[pl.ds(there * FACE, FACE)] = pair[pl.ds(there * FACE, FACE)]


def gather_yz_kernel(core, own, pair, along_y, along_z):
    here = core[0]
    there = 1 - here
    along_z[here] = own[0]
    along_z[there] = pair[there * GIVEN]
    along_y[...] = own[1:]


def join_kernel(along_x, along_z, taken):
    taken[: 2 * FACE] = along_x[...]
    taken[2 * FACE :] = along_z[...]


def velocity_planes(faces, velocity, buoyancy, write):
    for x in faces.planes:
        scale = TIME_STEP * buoyancy[x]
        write(0, x, velocity[0, x] + scale * (faces.dx(0, x) + faces.dy(3, x) + faces.dz(4, x)))
        write(1, x, velocity[1, x] + scale * (faces.dx(3, x) + faces.dy(1, x) + faces.dz(5, x)))
        write(2, x, velocity[2, x] + scale * (faces.dx(4, x) + faces.dy(5, x) + faces.dz(2, x)))


def velocity_edge_kernel(core, stress, velocity, buoyancy, pair, spread, outer, *refs):
    out, own, given, rows, edges = refs
    nx = stress.shape[1]
    place = edge_planes(nx)
    faces = Faces(STRESS, stress, list(place), core[0], pair, spread, outer, rows, edges)
    faces.prepare()

    def write(comp, x, value):
        out[comp, place[x]] = value

    velocity_planes(faces, velocity, buoyancy, write)
    pack_x(VELOCITY, out, place, nx, core[0], own, given)


def velocity_rest_kernel(core, stress, velocity, buoyancy, pair, spread, outer, *refs):
    edge, behind, out, own, given, rows, edges = refs
    nx = stress.shape[1]
    place = edge_planes(nx)
    for x, at in place.items():
        for comp in range(3):
            out[comp, x] = edge[comp, at]
    inner = [x for x in range(nx) if x not in place]
    faces = Faces(STRESS, stress, inner, core[0], pair, spread, outer, rows, edges)
    faces.prepare()

    def write(comp, x, value):
        out[comp, x] = value

    velocity_planes(faces, velocity, buoyancy, write)
    pack_yz(VELOCITY, out, core[0], own, given)


def stress_planes(faces, first, table, stress, memory, cells, write):
    lam, shear, weight, mech, top_ref = cells
    nx, ny, nz = lam.shape
    tops = top_ref[...].astype(jnp.float32).T
    depth = (first[0] + lax.broadcasted_iota(jnp.int32, (1, nz), 1)).astype(jnp.float32)
    for x in faces.planes:
        decay = jnp.zeros((ny, nz), jnp.float32)
        for level in range(table.shape[0]):
            decay = jnp.where(mech[x] == level, table[level], decay)
        gain = (1.0 - decay) * weight[x]
        top = tops[:, x : x + 1]
        solid = depth >= top
        below = depth > top
        xx, yy, zz = faces.dx(0, x), faces.dy(1, x), faces.dz(2, x)
        volume = lam[x] * (xx + yy + zz)
        double = 2.0 * shear[x]
        rates = (
            volume + double * xx,
            volume + double * yy,
            volume + double * zz,
            shear[x] * (faces.dy(0, x) + faces.dx(1, x)),
            shear[x] * (faces.dz(0, x) + faces.dx(2, x)),
            shear[x] * (faces.dz(1, x) + faces.dy(2, x)),
        )
        for comp, rate in enumerate(rates):
            new = decay * memory[comp, x] + gain * rate
            keep = below if comp in (2, 4, 5) else solid
            moved = jnp.where(keep, stress[comp, x] + TIME_STEP * (rate - new), 0.0)
            write(comp, x, moved, new)


def stress_edge_kernel(core, first, table, velocity, stress, memory, *refs):
    cells, (pair, spread, outer, out, kept, own, given, rows, edges) = refs[:5], refs[5:]
    nx = stress.shape[1]
    place = edge_planes(nx)
    faces = Faces(VELOCITY, velocity, list(place), core[0], pair, spread, outer, rows, edges)
    faces.prepare()

    def write(comp, x, moved, new):
        out[comp, place[x]] = moved
        kept[comp, place[x]] = new

    stress_planes(faces, first, table, stress, memory, cells, write)
    pack_x(STRESS, out, place, nx, core[0], own, given)


def stress_rest_kernel(core, first, table, velocity, stress, memory, *refs):
    cells, (pair, spread, outer) = refs[:5], refs[5:8]
    edge, edge_kept, behind, out, kept, own, given, rows, edges = refs[8:]
    nx = stress.shape[1]
    place = edge_planes(nx)
    for x, at in place.items():
        for comp in range(6):
            out[comp, x] = edge[comp, at]
            kept[comp, x] = edge_kept[comp, at]
    inner = [x for x in range(nx) if x not in place]
    faces = Faces(VELOCITY, velocity, inner, core[0], pair, spread, outer, rows, edges)
    faces.prepare()

    def write(comp, x, moved, new):
        out[comp, x] = moved
        kept[comp, x] = new

    stress_planes(faces, first, table, stress, memory, cells, write)
    pack_yz(STRESS, out, core[0], own, given)


def last_kernel(core, first, table, velocity, stress, memory, *refs):
    cells, (pair, spread, outer, out, kept, rows, edges) = refs[:5], refs[5:]
    planes = list(range(stress.shape[1]))
    faces = Faces(VELOCITY, velocity, planes, core[0], pair, spread, outer, rows, edges)
    faces.prepare()

    def write(comp, x, moved, new):
        out[comp, x] = moved
        kept[comp, x] = new

    stress_planes(faces, first, table, stress, memory, cells, write)


def call(body, outs, operands, scalars=1, scratch=(), hold=False, cost=None):
    vmem = pl.BlockSpec(memory_space=pltpu.VMEM)
    specs = [pl.BlockSpec(memory_space=pltpu.SMEM)] * scalars
    specs += [vmem] * (len(operands) - scalars)
    if hold:
        specs[-1] = pl.BlockSpec(memory_space=pl.ANY)
    return pl.pallas_call(
        body,
        out_shape=outs,
        in_specs=specs,
        out_specs=[vmem] * len(outs),
        scratch_shapes=list(scratch),
        cost_estimate=cost,
        compiler_params=pltpu.CompilerParams(vmem_limit_bytes=24 * 1024 * 1024),
    )(*operands)


def float32(*shape):
    return jax.ShapeDtypeStruct(shape, jnp.float32)


def core_pairs(gy):
    return [[j, j + 1] for j in range(0, gy, 2)]


def send_x(core, own, given):
    gx, gy = lax.axis_size("gx"), lax.axis_size("gy")
    pair = lax.all_gather(given, "gy", axis=0, tiled=True, axis_index_groups=core_pairs(gy))
    (along,) = call(gather_x_kernel, [float32(2 * FACE, *own.shape[1:])], [core, own, pair])
    pairs = []
    for j in range(gy):
        step = 1 - 2 * (j % 2)
        pairs += [(i * gy + j, (i + step) * gy + j) for i in range(gx) if 0 <= i + step < gx]
    return along, lax.ppermute(along, ("gx", "gy"), pairs)


def send_yz(core, own, given, got_x):
    gy, gz = lax.axis_size("gy"), lax.axis_size("gz")
    plane = own.shape[1:]
    pair = lax.all_gather(given, "gy", axis=0, tiled=True, axis_index_groups=core_pairs(gy))
    along_y, along_z = call(
        gather_yz_kernel, [float32(FACE, *plane), float32(2, *plane)], [core, own, pair]
    )
    pairs = []
    for j in range(gy):
        step = 1 - 2 * (j % 2)
        pairs += [(j * gz + k, j * gz + k + step) for k in range(gz) if 0 <= k + step < gz]
    got_z = lax.ppermute(along_z, ("gy", "gz"), pairs)
    chips = [(j, j + 1) for j in range(1, gy - 1, 2)]
    outer = lax.ppermute(along_y, "gy", chips + [(k, j) for j, k in chips])
    (taken,) = call(join_kernel, [float32(TAKEN, *plane)], [got_x, got_z], scalars=0)
    spread = lax.all_gather(taken, "gy", axis=0, tiled=True, axis_index_groups=core_pairs(gy))
    return pair, spread, outer


def shards(
    velocity,
    stress,
    memory,
    lame_lambda,
    shear_modulus,
    buoyancy,
    anelastic_weight,
    decay_table,
    mech_index,
    surface_depth,
):
    nx, ny, nz = lame_lambda.shape
    core = (lax.axis_index("gy") % 2).astype(jnp.int32).reshape(1)
    first = (lax.axis_index("gz") * nz).astype(jnp.int32).reshape(1)
    like = lambda a: float32(*a.shape)
    scratch = (
        pltpu.VMEM((3, nx, ny + 16, nz), jnp.float32),
        pltpu.VMEM((3, nx * ny, nz), jnp.float32),
    )
    cost = pl.CostEstimate(flops=2**22, bytes_accessed=2**22, transcendentals=0)
    face_x = [float32(FACE, ny, nz)] * 2
    face_yz = [float32(GIVEN, ny, nz)] * 2
    cells = [lame_lambda, shear_modulus, anelastic_weight, mech_index, surface_depth]
    along, got_x = send_x(core, *call(first_x_kernel, face_x, [core, stress]))
    own, given = call(first_yz_kernel, face_yz, [core, stress, along], hold=True, cost=cost)
    for step in range(STEPS):
        halos = send_yz(core, own, given, got_x)
        operands = [core, stress, velocity, buoyancy, *halos]
        edge, own, given = call(
            velocity_edge_kernel, [float32(3, 4, ny, nz)] + face_x, operands, scratch=scratch
        )
        along, got_x = send_x(core, own, given)
        velocity, own, given = call(
            velocity_rest_kernel,
            [like(velocity)] + face_yz,
            operands + [edge, along],
            scratch=scratch,
            hold=True,
            cost=cost,
        )
        halos = send_yz(core, own, given, got_x)
        operands = [core, first, decay_table, velocity, stress, memory, *cells, *halos]
        if step == STEPS - 1:
            stress, memory = call(
                last_kernel, [like(stress), like(memory)], operands, scalars=3, scratch=scratch
            )
            break
        edge, edge_kept, own, given = call(
            stress_edge_kernel,
            [float32(6, 4, ny, nz)] * 2 + face_x,
            operands,
            scalars=3,
            scratch=scratch,
        )
        along, got_x = send_x(core, own, given)
        stress, memory, own, given = call(
            stress_rest_kernel,
            [like(stress), like(memory)] + face_yz,
            operands + [edge, edge_kept, along],
            scalars=3,
            scratch=scratch,
            hold=True,
            cost=cost,
        )
    return (velocity, stress, memory)


def solution(mesh):
    fields = P(None, *AXES)
    cells = P(*AXES)
    return jax.shard_map(
        shards,
        mesh=mesh,
        in_specs=(fields,) * 3 + (cells,) * 4 + (P(), cells, P("gx", "gy")),
        out_specs=(fields,) * 3,
        check_vma=False,
    )
```

time: 85.8 us -> 91.6 us (1.068)
  blocking collectives: 22.4 us -> 45.6 us
  starting transfers between devices: 49.4 us -> 31.3 us
  Pallas kernels: 9.48 us -> 11.2 us
    all_gather x8 -> x12, blocking collectives: 22.4 us -> 45.6 us  [the longest x4 23.5 us: send_yz(): lax.all_gather(given, 'gy', axis=0, tiled=True, axis_index_groups=core_pa...]
    ppermute x12, starting transfers between devices: 49.4 us -> 31.3 us  [the longest x4 21 us: send_yz(): outer = lax.ppermute(along_y, 'gy', chips + [(k, j) for j, k in chips])]
    pallas_call x13 -> x21, Pallas kernels: 9.48 us -> 11.2 us  [call(): pl.pallas_call(body, out_shape=outs, in_specs=specs, out_specs=[vmem] * l...]
  transfers between devices with their start and end apart: 12 -> 12, of which waited for: 1 -> 0; matrix products, arithmetic and copies ran while one was open for 0% -> 0% of each run, Pallas kernels for 0% -> 7%
where the time goes in v3:
time: 91.6 us; the launch traced here: 91 us
  blocking collectives  45.6 us (50%)
  starting transfers between devices  31.3 us (34%)
  Pallas kernels  11.2 us (12%)
  local copies, waits for them, and re-layouts  1.79 us (2%)
  between operations  1.03 us (1%)
    all_gather x4, blocking collectives, send_yz(): lax.all_gather(given, 'gy', axis=0, tiled=True, axis_index_groups=core_pa...  23.5 us
    ppermute x4, starting transfers between devices, send_yz(): outer = lax.ppermute(along_y, 'gy', chips + [(k, j) for j, k in chips])  21 us
    all_gather x4, blocking collectives, send_x(): lax.all_gather(given, 'gy', axis=0, tiled=True, axis_index_groups=core_pa...  14.1 us
    pallas_call x21, Pallas kernels, call(): pl.pallas_call(body, out_shape=outs, in_specs=specs, out_specs=[vmem] * l...  11.2 us
    all_gather x4, blocking collectives, send_yz(): lax.all_gather(taken, 'gy', axis=0, tiled=True, axis_index_groups=core_pa...  7.92 us
    ppermute x4, starting transfers between devices, send_x(): return (along, lax.ppermute(along, ('gx', 'gy'), pairs))  5.16 us
    ppermute x4, starting transfers between devices, send_yz(): got_z = lax.ppermute(along_z, ('gy', 'gz'), pairs)  5.12 us
  transfers between devices with their start and end apart: 12, of which 0 were waited for; matrix products, arithmetic and copies ran while one was open for 0% of the time, Pallas kernels for 7%

profile of v3, /device:TPU:1, one launch (start us, length us, event | category | flops | bytes accessed | tf_op | source)
XLA Modules:
  0.0 91.0 jit_solution(3402412823915771964)
XLA Ops:
  1.8 8.5 %all_gather.36.pair = f32[10,16,128]{2,1,0:T(8,128)S(1)} all-gather(f32[5,16,128]{2,1,0:T(8,128)S(1)} %get-tuple-element.38), channel_id=1, replica_groups={{0,4},{8,12},{16,20},{24,28},{1,5},{9,13},{17,21},{25,29},{2,6},{10,14}..., dimensions={0}, use_global_device_ids=true | all-gather | bytes 122880 | tf_op jit(solution)/shard_map/all_gather | solution.py:383
  10.3 1.3 %collective-permute-start = (f32[10,16,128]{2,1,0:T(8,128)S(1)}, f32[10,16,128]{2,1,0:T(8,128)S(1)}, u32[]{:S(2)}, u32[]{:S(2)}) collective-permute-start(f32[10,16,128]{2,1,0:T(8,128)S(1)} %shard_map.122.behind), channel_id=1, source_target_pairs={{0,32},{32,64},{64,96},{96,128},{128,160},{160,192},{192,224},{224... | collective-permute-start | bytes 245768 | tf_op jit(solution)/shard_map/ppermute | solution.py:389
  12.1 4.4 %all_gather.37.pair = f32[12,16,128]{2,1,0:T(8,128)S(1)} all-gather(f32[6,16,128]{2,1,0:T(8,128)S(1)} %get-tuple-element.39), channel_id=1, replica_groups={{0,4},{8,12},{16,20},{24,28},{1,5},{9,13},{17,21},{25,29},{2,6},{10,14}..., dimensions={0}, use_global_device_ids=true | all-gather | bytes 147456 | tf_op jit(solution)/shard_map/all_gather | solution.py:395
  17.9 6.0 %collective-permute-start.2 = (f32[5,16,128]{2,1,0:T(8,128)S(1)}, f32[5,16,128]{2,1,0:T(8,128)S(1)}, u32[]{:S(2)}, u32[]{:S(2)}) collective-permute-start(f32[5,16,128]{2,1,0:T(8,128)S(1)} %get-tuple-element.42), channel_id=1, source_target_pairs={{4,8},{12,16},{20,24},{8,4},{16,12},{24,20},{5,9},{13,17},{21,25},... | collective-permute-start | bytes 122888 | tf_op jit(solution)/shard_map/ppermute | solution.py:405
  23.9 2.1 %all_gather.38.spread = f32[24,16,128]{2,1,0:T(8,128)S(1)} all-gather(f32[12,16,128]{2,1,0:T(8,128)S(1)} %shard_map.125), channel_id=1, replica_groups={{0,4},{8,12},{16,20},{24,28},{1,5},{9,13},{17,21},{25,29},{2,6},{10,14}..., dimensions={0}, use_global_device_ids=true | all-gather | bytes 294912 | tf_op jit(solution)/shard_map/all_gather | solution.py:407
  26.4 1.9 %all_gather.39.pair = f32[10,16,128]{2,1,0:T(8,128)S(1)} all-gather(f32[5,16,128]{2,1,0:T(8,128)S(1)} %get-tuple-element.45), channel_id=1, replica_groups={{0,4},{8,12},{16,20},{24,28},{1,5},{9,13},{17,21},{25,29},{2,6},{10,14}..., dimensions={0}, use_global_device_ids=true | all-gather | bytes 122880 | tf_op jit(solution)/shard_map/all_gather | solution.py:383
  28.3 1.3 %collective-permute-start.3 = (f32[10,16,128]{2,1,0:T(8,128)S(1)}, f32[10,16,128]{2,1,0:T(8,128)S(1)}, u32[]{:S(2)}, u32[]{:S(2)}) collective-permute-start(f32[10,16,128]{2,1,0:T(8,128)S(1)} %shard_map.127.refs_1_), channel_id=1, source_target_pairs={{0,32},{32,64},{64,96},{96,128},{128,160},{160,192},{192,224},{224... | collective-permute-start | bytes 245768 | tf_op jit(solution)/shard_map/ppermute | solution.py:389
  29.7 1.5 %shard_map.128 = (f32[3,16,16,128]{3,2,1,0:T(8,128)S(1)}, f32[6,16,128]{2,1,0:T(8,128)S(1)}, f32[6,16,128]{2,1,0:T(8,128)S(1)}) custom-call(s32[1]{0:T(128)} %bitcast.core, f32[6,16,16,128]{3,2,1,0:T(8,128)S(1)} %copy-done.1, f32[3,16,16,128]{3,2,1,0:T(8,128)S(1)} %copy-done.4, f32[16,16,128]{2,1,0:T(8,128)S(1)} %copy-done.3, ...), custom_call_target="tpu_custom_call" | custom-call | flops 4194304 | bytes 4194304 | tf_op jit(solution)/shard_map/pallas_call | solution.py:362
  31.2 8.7 %all_gather.40.pair.refs_5_ = f32[12,16,128]{2,1,0:T(8,128)S(1)} all-gather(f32[6,16,128]{2,1,0:T(8,128)S(1)} %get-tuple-element.47), channel_id=1, replica_groups={{0,4},{8,12},{16,20},{24,28},{1,5},{9,13},{17,21},{25,29},{2,6},{10,14}..., dimensions={0}, use_global_device_ids=true | all-gather | bytes 147456 | tf_op jit(solution)/shard_map/all_gather | solution.py:395
  41.2 5.1 %collective-permute-start.5 = (f32[5,16,128]{2,1,0:T(8,128)S(1)}, f32[5,16,128]{2,1,0:T(8,128)S(1)}, u32[]{:S(2)}, u32[]{:S(2)}) collective-permute-start(f32[5,16,128]{2,1,0:T(8,128)S(1)} %get-tuple-element.50), channel_id=1, source_target_pairs={{4,8},{12,16},{20,24},{8,4},{16,12},{24,20},{5,9},{13,17},{21,25},... | collective-permute-start | bytes 122888 | tf_op jit(solution)/shard_map/ppermute | solution.py:405
  46.3 1.9 %all_gather.41.refs_6_ = f32[24,16,128]{2,1,0:T(8,128)S(1)} all-gather(f32[12,16,128]{2,1,0:T(8,128)S(1)} %shard_map.130), channel_id=1, replica_groups={{0,4},{8,12},{16,20},{24,28},{1,5},{9,13},{17,21},{25,29},{2,6},{10,14}..., dimensions={0}, use_global_device_ids=true | all-gather | bytes 294912 | tf_op jit(solution)/shard_map/all_gather | solution.py:407
  49.9 1.9 %all_gather.42.pair = f32[10,16,128]{2,1,0:T(8,128)S(1)} all-gather(f32[5,16,128]{2,1,0:T(8,128)S(1)} %get-tuple-element.54), channel_id=1, replica_groups={{0,4},{8,12},{16,20},{24,28},{1,5},{9,13},{17,21},{25,29},{2,6},{10,14}..., dimensions={0}, use_global_device_ids=true | all-gather | bytes 122880 | tf_op jit(solution)/shard_map/all_gather | solution.py:383
  51.8 1.3 %collective-permute-start.6 = (f32[10,16,128]{2,1,0:T(8,128)S(1)}, f32[10,16,128]{2,1,0:T(8,128)S(1)}, u32[]{:S(2)}, u32[]{:S(2)}) collective-permute-start(f32[10,16,128]{2,1,0:T(8,128)S(1)} %shard_map.132.refs_10_), channel_id=1, source_target_pairs={{0,32},{32,64},{64,96},{96,128},{128,160},{160,192},{192,224},{224... | collective-permute-start | bytes 245768 | tf_op jit(solution)/shard_map/ppermute | solution.py:389
  53.1 2.3 %shard_map.133 = (f32[6,16,16,128]{3,2,1,0:T(8,128)S(1)}, f32[6,16,16,128]{3,2,1,0:T(8,128)S(1)}, f32[6,16,128]{2,1,0:T(8,128)S(1)}, f32[6,16,128]{2,1,0:T(8,128)S(1)}) custom-call(s32[1]{0:T(128)} %bitcast.core, s32[1]{0:T(128)} %bitcast.1.first, f32[8]{0:T(128)S(1)} %copy-done.11, f32[3,16,16,128]{3,2,1,0:T(8,128)S(1)} %get-tuple-element.46.velocity, ...), custom_call_target="tpu_custom_call" | custom-call | flops 4194304 | bytes 4194304 | tf_op jit(solution)/shard_map/pallas_call | solution.py:362
  55.4 4.7 %all_gather.43.pair = f32[12,16,128]{2,1,0:T(8,128)S(1)} all-gather(f32[6,16,128]{2,1,0:T(8,128)S(1)} %get-tuple-element.56), channel_id=1, replica_groups={{0,4},{8,12},{16,20},{24,28},{1,5},{9,13},{17,21},{25,29},{2,6},{10,14}..., dimensions={0}, use_global_device_ids=true | all-gather | bytes 147456 | tf_op jit(solution)/shard_map/all_gather | solution.py:395
  61.4 5.1 %collective-permute-start.8 = (f32[5,16,128]{2,1,0:T(8,128)S(1)}, f32[5,16,128]{2,1,0:T(8,128)S(1)}, u32[]{:S(2)}, u32[]{:S(2)}) collective-permute-start(f32[5,16,128]{2,1,0:T(8,128)S(1)} %get-tuple-element.59), channel_id=1, source_target_pairs={{4,8},{12,16},{20,24},{8,4},{16,12},{24,20},{5,9},{13,17},{21,25},... | collective-permute-start | bytes 122888 | tf_op jit(solution)/shard_map/ppermute | solution.py:405
  66.5 1.9 %all_gather.44.spread = f32[24,16,128]{2,1,0:T(8,128)S(1)} all-gather(f32[12,16,128]{2,1,0:T(8,128)S(1)} %shard_map.135), channel_id=1, replica_groups={{0,4},{8,12},{16,20},{24,28},{1,5},{9,13},{17,21},{25,29},{2,6},{10,14}..., dimensions={0}, use_global_device_ids=true | all-gather | bytes 294912 | tf_op jit(solution)/shard_map/all_gather | solution.py:407
  69.0 1.9 %all_gather.45.pair = f32[10,16,128]{2,1,0:T(8,128)S(1)} all-gather(f32[5,16,128]{2,1,0:T(8,128)S(1)} %get-tuple-element.62), channel_id=1, replica_groups={{0,4},{8,12},{16,20},{24,28},{1,5},{9,13},{17,21},{25,29},{2,6},{10,14}..., dimensions={0}, use_global_device_ids=true | all-gather | bytes 122880 | tf_op jit(solution)/shard_map/all_gather | solution.py:383
  70.8 1.3 %collective-permute-start.9 = (f32[10,16,128]{2,1,0:T(8,128)S(1)}, f32[10,16,128]{2,1,0:T(8,128)S(1)}, u32[]{:S(2)}, u32[]{:S(2)}) collective-permute-start(f32[10,16,128]{2,1,0:T(8,128)S(1)} %shard_map.137.refs_1_), channel_id=1, source_target_pairs={{0,32},{32,64},{64,96},{96,128},{128,160},{160,192},{192,224},{224... | collective-permute-start | bytes 245768 | tf_op jit(solution)/shard_map/ppermute | solution.py:389
  72.1 2.3 %shard_map.138 = (f32[3,16,16,128]{3,2,1,0:T(8,128)}, f32[6,16,128]{2,1,0:T(8,128)S(1)}, f32[6,16,128]{2,1,0:T(8,128)S(1)}) custom-call(s32[1]{0:T(128)} %bitcast.core, f32[6,16,16,128]{3,2,1,0:T(8,128)S(1)} %get-tuple-element.55.stress, f32[3,16,16,128]{3,2,1,0:T(8,128)S(1)} %get-tuple-element.46.velocity, f32[16,16,128]{2,1,0:T(8,128)S(1)} %copy-done.3, ...), custom_call_target="tpu_custom_call" | custom-call | flops 4194304 | bytes 4194304 | tf_op jit(solution)/shard_map/pallas_call | solution.py:362
  74.4 5.7 %all_gather.46.pair.refs_5_ = f32[12,16,128]{2,1,0:T(8,128)S(1)} all-gather(f32[6,16,128]{2,1,0:T(8,128)S(1)} %get-tuple-element.65), channel_id=1, replica_groups={{0,4},{8,12},{16,20},{24,28},{1,5},{9,13},{17,21},{25,29},{2,6},{10,14}..., dimensions={0}, use_global_device_ids=true | all-gather | bytes 147456 | tf_op jit(solution)/shard_map/all_gather | solution.py:395
  81.4 4.8 %collective-permute-start.11 = (f32[5,16,128]{2,1,0:T(8,128)S(1)}, f32[5,16,128]{2,1,0:T(8,128)S(1)}, u32[]{:S(2)}, u32[]{:S(2)}) collective-permute-start(f32[5,16,128]{2,1,0:T(8,128)S(1)} %get-tuple-element.68), channel_id=1, source_target_pairs={{4,8},{12,16},{20,24},{8,4},{16,12},{24,20},{5,9},{13,17},{21,25},... | collective-permute-start | bytes 122888 | tf_op jit(solution)/shard_map/ppermute | solution.py:405
  86.3 1.9 %all_gather.47.refs_6_ = f32[24,16,128]{2,1,0:T(8,128)S(1)} all-gather(f32[12,16,128]{2,1,0:T(8,128)S(1)} %shard_map.140), channel_id=1, replica_groups={{0,4},{8,12},{16,20},{24,28},{1,5},{9,13},{17,21},{25,29},{2,6},{10,14}..., dimensions={0}, use_global_device_ids=true | all-gather | bytes 294912 | tf_op jit(solution)/shard_map/all_gather | solution.py:407
  88.2 2.7 %shard_map.141 = (f32[6,16,16,128]{3,2,1,0:T(8,128)}, f32[6,16,16,128]{3,2,1,0:T(8,128)}) custom-call(s32[1]{0:T(128)} %bitcast.core, s32[1]{0:T(128)} %bitcast.1.first, f32[8]{0:T(128)S(1)} %copy-done.11, f32[3,16,16,128]{3,2,1,0:T(8,128)S(1)} %copy-done.9, f32[6,16,16,128]{3,2,1,0:T(8,128)S(1)} %get-tuple-element.55.stress, ...), custom_call_target="tpu_custom_call" | custom-call | tf_op jit(solution)/shard_map/pallas_call | solution.py:362
  (57 shorter events, 9.4 us)
Async XLA Ops:
  0.6 1.1 %copy-start = (f32[6,16,16,128]{3,2,1,0:T(8,128)S(1)}, f32[6,16,16,128]{3,2,1,0:T(8,128)}, u32[]{:S(2)}) copy-start(f32[6,16,16,128]{3,2,1,0:T(8,128)} %stress.11) | copy-start | bytes 2359300
  1.8 9.8 %copy-start.1 = (f32[6,16,16,128]{3,2,1,0:T(8,128)S(1)}, f32[6,16,16,128]{3,2,1,0:T(8,128)}, u32[]{:S(2)}) copy-start(f32[6,16,16,128]{3,2,1,0:T(8,128)} %stress.11) | copy-start | bytes 2359300
  10.3 13.5 %collective-permute-start = (f32[10,16,128]{2,1,0:T(8,128)S(1)}, f32[10,16,128]{2,1,0:T(8,128)S(1)}, u32[]{:S(2)}, u32[]{:S(2)}) collective-permute-start(f32[10,16,128]{2,1,0:T(8,128)S(1)} %shard_map.122.behind), channel_id=1, source_target_pairs={{0,32},{32,64},{64,96},{96,128},{128,160},{160,192},{192,224},{224... | collective-permute-start | bytes 245768 | tf_op jit(solution)/shard_map/ppermute | solution.py:389
  12.1 13.9 %copy-start.4 = (f32[3,16,16,128]{3,2,1,0:T(8,128)S(1)}, f32[3,16,16,128]{3,2,1,0:T(8,128)}, u32[]{:S(2)}) copy-start(f32[3,16,16,128]{3,2,1,0:T(8,128)} %velocity.3) | copy-start | bytes 1179652
  16.6 7.3 %collective-permute-start.1 = (f32[2,16,128]{2,1,0:T(8,128)S(1)}, f32[2,16,128]{2,1,0:T(8,128)S(1)}, u32[]{:S(2)}, u32[]{:S(2)}) collective-permute-start(f32[2,16,128]{2,1,0:T(8,128)S(1)} %get-tuple-element.41), channel_id=1, source_target_pairs={{0,1},{1,2},{2,3},{5,4},{6,5},{7,6},{8,9},{9,10},{10,11},{13,12},{... | collective-permute-start | bytes 49160 | tf_op jit(solution)/shard_map/ppermute | solution.py:403
  17.9 8.1 %collective-permute-start.2 = (f32[5,16,128]{2,1,0:T(8,128)S(1)}, f32[5,16,128]{2,1,0:T(8,128)S(1)}, u32[]{:S(2)}, u32[]{:S(2)}) collective-permute-start(f32[5,16,128]{2,1,0:T(8,128)S(1)} %get-tuple-element.42), channel_id=1, source_target_pairs={{4,8},{12,16},{20,24},{8,4},{16,12},{24,20},{5,9},{13,17},{21,25},... | collective-permute-start | bytes 122888 | tf_op jit(solution)/shard_map/ppermute | solution.py:405
  23.9 2.1 %copy-start.3 = (f32[16,16,128]{2,1,0:T(8,128)S(1)}, f32[16,16,128]{2,1,0:T(8,128)}, u32[]{:S(2)}) copy-start(f32[16,16,128]{2,1,0:T(8,128)} %buoyancy.7) | copy-start | bytes 393220
  28.3 18.0 %collective-permute-start.3 = (f32[10,16,128]{2,1,0:T(8,128)S(1)}, f32[10,16,128]{2,1,0:T(8,128)S(1)}, u32[]{:S(2)}, u32[]{:S(2)}) collective-permute-start(f32[10,16,128]{2,1,0:T(8,128)S(1)} %shard_map.127.refs_1_), channel_id=1, source_target_pairs={{0,32},{32,64},{64,96},{96,128},{128,160},{160,192},{192,224},{224... | collective-permute-start | bytes 245768 | tf_op jit(solution)/shard_map/ppermute | solution.py:389
  29.6 18.7 %copy-start.5 = (f32[16,16,128]{2,1,0:T(8,128)S(1)}, f32[16,16,128]{2,1,0:T(8,128)}, u32[]{:S(2)}) copy-start(f32[16,16,128]{2,1,0:T(8,128)} %refs_0_.5) | copy-start | bytes 393220
  29.6 18.6 %copy-start.6 = (f32[16,16,128]{2,1,0:T(8,128)S(1)}, f32[16,16,128]{2,1,0:T(8,128)}, u32[]{:S(2)}) copy-start(f32[16,16,128]{2,1,0:T(8,128)} %refs_1_.5) | copy-start | bytes 393220
  29.6 18.6 %copy-start.7 = (f32[16,16,128]{2,1,0:T(8,128)S(1)}, f32[16,16,128]{2,1,0:T(8,128)}, u32[]{:S(2)}) copy-start(f32[16,16,128]{2,1,0:T(8,128)} %refs_2_.5) | copy-start | bytes 393220
  29.6 18.6 %copy-start.8 = (s32[16,16,128]{2,1,0:T(8,128)S(1)}, s32[16,16,128]{2,1,0:T(8,128)}, u32[]{:S(2)}) copy-start(s32[16,16,128]{2,1,0:T(8,128)} %refs_3_.5) | copy-start | bytes 393220
  31.2 17.1 %copy-start.2 = (f32[6,16,16,128]{3,2,1,0:T(8,128)S(1)}, f32[6,16,16,128]{3,2,1,0:T(8,128)}, u32[]{:S(2)}) copy-start(f32[6,16,16,128]{3,2,1,0:T(8,128)} %memory.3) | copy-start | bytes 2359300
  39.9 6.4 %collective-permute-start.4 = (f32[2,16,128]{2,1,0:T(8,128)S(1)}, f32[2,16,128]{2,1,0:T(8,128)S(1)}, u32[]{:S(2)}, u32[]{:S(2)}) collective-permute-start(f32[2,16,128]{2,1,0:T(8,128)S(1)} %get-tuple-element.49), channel_id=1, source_target_pairs={{0,1},{1,2},{2,3},{5,4},{6,5},{7,6},{8,9},{9,10},{10,11},{13,12},{... | collective-permute-start | bytes 49160 | tf_op jit(solution)/shard_map/ppermute | solution.py:403
  41.2 7.1 %collective-permute-start.5 = (f32[5,16,128]{2,1,0:T(8,128)S(1)}, f32[5,16,128]{2,1,0:T(8,128)S(1)}, u32[]{:S(2)}, u32[]{:S(2)}) collective-permute-start(f32[5,16,128]{2,1,0:T(8,128)S(1)} %get-tuple-element.50), channel_id=1, source_target_pairs={{4,8},{12,16},{20,24},{8,4},{16,12},{24,20},{5,9},{13,17},{21,25},... | collective-permute-start | bytes 122888 | tf_op jit(solution)/shard_map/ppermute | solution.py:405
  46.3 2.0 %copy-start.10 = (s32[16,16]{1,0:T(8,128)S(1)}, s32[16,16]{1,0:T(8,128)}, u32[]{:S(2)}) copy-start(s32[16,16]{1,0:T(8,128)} %refs_4_.5) | copy-start | bytes 3076
  48.3 0.7 copy-start.11
  51.8 14.7 %collective-permute-start.6 = (f32[10,16,128]{2,1,0:T(8,128)S(1)}, f32[10,16,128]{2,1,0:T(8,128)S(1)}, u32[]{:S(2)}, u32[]{:S(2)}) collective-permute-start(f32[10,16,128]{2,1,0:T(8,128)S(1)} %shard_map.132.refs_10_), channel_id=1, source_target_pairs={{0,32},{32,64},{64,96},{96,128},{128,160},{160,192},{192,224},{224... | collective-permute-start | bytes 245768 | tf_op jit(solution)/shard_map/ppermute | solution.py:389
  60.1 6.4 %collective-permute-start.7 = (f32[2,16,128]{2,1,0:T(8,128)S(1)}, f32[2,16,128]{2,1,0:T(8,128)S(1)}, u32[]{:S(2)}, u32[]{:S(2)}) collective-permute-start(f32[2,16,128]{2,1,0:T(8,128)S(1)} %get-tuple-element.58), channel_id=1, source_target_pairs={{0,1},{1,2},{2,3},{5,4},{6,5},{7,6},{8,9},{9,10},{10,11},{13,12},{... | collective-permute-start | bytes 49160 | tf_op jit(solution)/shard_map/ppermute | solution.py:403
  61.4 7.1 %collective-permute-start.8 = (f32[5,16,128]{2,1,0:T(8,128)S(1)}, f32[5,16,128]{2,1,0:T(8,128)S(1)}, u32[]{:S(2)}, u32[]{:S(2)}) collective-permute-start(f32[5,16,128]{2,1,0:T(8,128)S(1)} %get-tuple-element.59), channel_id=1, source_target_pairs={{4,8},{12,16},{20,24},{8,4},{16,12},{24,20},{5,9},{13,17},{21,25},... | collective-permute-start | bytes 122888 | tf_op jit(solution)/shard_map/ppermute | solution.py:405
  70.8 15.4 %collective-permute-start.9 = (f32[10,16,128]{2,1,0:T(8,128)S(1)}, f32[10,16,128]{2,1,0:T(8,128)S(1)}, u32[]{:S(2)}, u32[]{:S(2)}) collective-permute-start(f32[10,16,128]{2,1,0:T(8,128)S(1)} %shard_map.137.refs_1_), channel_id=1, source_target_pairs={{0,32},{32,64},{64,96},{96,128},{128,160},{160,192},{192,224},{224... | collective-permute-start | bytes 245768 | tf_op jit(solution)/shard_map/ppermute | solution.py:389
  74.4 13.8 %copy-start.9 = (f32[3,16,16,128]{3,2,1,0:T(8,128)S(1)}, f32[3,16,16,128]{3,2,1,0:T(8,128)}, u32[]{:S(2)}) copy-start(f32[3,16,16,128]{3,2,1,0:T(8,128)} %get-tuple-element.34.velocity) | copy-start | bytes 1179652
  80.1 6.1 %collective-permute-start.10 = (f32[2,16,128]{2,1,0:T(8,128)S(1)}, f32[2,16,128]{2,1,0:T(8,128)S(1)}, u32[]{:S(2)}, u32[]{:S(2)}) collective-permute-start(f32[2,16,128]{2,1,0:T(8,128)S(1)} %get-tuple-element.67), channel_id=1, source_target_pairs={{0,1},{1,2},{2,3},{5,4},{6,5},{7,6},{8,9},{9,10},{10,11},{13,12},{... | collective-permute-start | bytes 49160 | tf_op jit(solution)/shard_map/ppermute | solution.py:403
  81.4 6.8 %collective-permute-start.11 = (f32[5,16,128]{2,1,0:T(8,128)S(1)}, f32[5,16,128]{2,1,0:T(8,128)S(1)}, u32[]{:S(2)}, u32[]{:S(2)}) collective-permute-start(f32[5,16,128]{2,1,0:T(8,128)S(1)} %get-tuple-element.68), channel_id=1, source_target_pairs={{4,8},{12,16},{20,24},{8,4},{16,12},{24,20},{5,9},{13,17},{21,25},... | collective-permute-start | bytes 122888 | tf_op jit(solution)/shard_map/ppermute | solution.py:405

commit v4 on v3

v4 whole, which is shorter than its diff:
```python
import jax
import jax.numpy as jnp
from jax import lax
from jax.experimental import pallas as pl
from jax.experimental.pallas import tpu as pltpu
from jax.sharding import PartitionSpec as P

STEPS = 2
COEF_NEAR = 9.0 / 8.0
COEF_FAR = -1.0 / 24.0
TIME_STEP = 0.2
AXES = ("gx", "gy", "gz")

STRESS = (
    ((0, "f"), (3, "b"), (4, "b")),
    ((3, "b"), (1, "f"), (5, "b")),
    ((4, "b"), (5, "b"), (2, "f")),
)
VELOCITY = (
    ((0, "b"), (1, "f"), (2, "f")),
    ((1, "b"), (0, "f"), (2, "f")),
    ((2, "b"), (0, "f"), (1, "f")),
)
BEFORE = {"f": (-1,), "b": (-2, -1)}
AFTER = {"f": (0, 1), "b": (0,)}
TAPS = {
    "f": ((1, COEF_NEAR), (0, -COEF_NEAR), (2, COEF_FAR), (-1, -COEF_FAR)),
    "b": ((0, COEF_NEAR), (-1, -COEF_NEAR), (1, COEF_FAR), (-2, -COEF_FAR)),
}

FACE = 5
TAKEN = 3 * FACE
LANES = 8


def edge_planes(nx):
    return {0: 0, 1: 1, nx - 2: 2, nx - 1: 3}


def layers(spec, sides):
    return [(comp, off) for comp, kind in spec for off in sides[kind]]


def weighted(taps):
    a, b, c, d = taps
    return COEF_NEAR * (a - b) + COEF_FAR * (c - d)


class Faces:
    def __init__(self, spec, fields, planes, core, halos, rows):
        self.spec, self.fields, self.planes, self.core, self.rows = spec, fields, planes, core, rows
        self.spread, self.outer, low, high = halos
        self.nx, self.ny, self.nz = fields.shape[1:]
        self.before = [{k: i for i, k in enumerate(layers(s, BEFORE))} for s in spec]
        self.after = [{k: i for i, k in enumerate(layers(s, AFTER))} for s in spec]
        self.low, self.high = low[...], high[...]
        self.lane = lax.broadcasted_iota(jnp.int32, (1, self.nz), 1)
        self.prepare()

    def prepare(self):
        ny = self.ny
        for slot, (comp, kind) in enumerate(self.spec[1]):
            for x in self.planes:
                self.rows[slot, x, 8 : 8 + ny, :] = self.fields[comp, x]

        def beside(before, after):
            for slot, (comp, kind) in enumerate(self.spec[1]):
                for x in self.planes:
                    for off in BEFORE[kind]:
                        i = self.before[1][comp, off]
                        self.rows[slot, x, 8 + off : 9 + off, :] = before(i, x)
                    for off in AFTER[kind]:
                        i = self.after[1][comp, off]
                        self.rows[slot, x, 8 + ny + off : 9 + ny + off, :] = after(i, x)

        outer = lambda i, x: self.outer[i, x : x + 1, :]

        @pl.when(self.core == 0)
        def _():
            beside(outer, lambda i, x: self.spread[TAKEN + 2 * FACE + i, x : x + 1, :])

        @pl.when(self.core == 1)
        def _():
            beside(lambda i, x: self.spread[2 * FACE + i, x : x + 1, :], outer)

    def dx(self, comp, x):
        kind = dict(self.spec[0])[comp]

        def plane(at):
            if at < 0:
                return self.spread[self.core * FACE + self.before[0][comp, at]]
            if at >= self.nx:
                return self.spread[TAKEN + self.core * FACE + self.after[0][comp, at - self.nx]]
            return self.fields[comp, at]

        return weighted([plane(x + off) for off, _ in TAPS[kind]])

    def dy(self, comp, x):
        slot = [c for c, _ in self.spec[1]].index(comp)
        kind = self.spec[1][slot][1]
        return weighted(
            [self.rows[slot, x, 8 + off : 8 + off + self.ny, :] for off, _ in TAPS[kind]]
        )

    def dz(self, comp, x):
        slot = [c for c, _ in self.spec[2]].index(comp)
        kind = self.spec[2][slot][1]
        nz, here = self.nz, self.fields[comp, x]
        first, count = self.before[2][comp, BEFORE[kind][0]], len(BEFORE[kind])
        low = pltpu.roll(self.low, (nz - count - LANES * x - first) % nz, 1)
        shift = (-LANES * x - self.after[2][comp, 0]) % nz
        high = pltpu.roll(self.high, shift, 1) if shift else self.high
        taps = {0: here}
        for off, _ in TAPS[kind]:
            if off < 0:
                taps[off] = pltpu.roll(jnp.where(self.lane >= nz + off, low, here), -off, 1)
            elif off > 0:
                taps[off] = pltpu.roll(jnp.where(self.lane < off, high, here), nz - off, 1)
        return weighted([taps[off] for off, _ in TAPS[kind]])


def pack_x(spec, fields, place, nx, core, own, given):
    def write(up, down):
        for i, (comp, off) in enumerate(layers(spec[0], BEFORE)):
            up[i] = fields[comp, place[nx + off]]
        for i, (comp, off) in enumerate(layers(spec[0], AFTER)):
            down[i] = fields[comp, place[off]]

    @pl.when(core == 0)
    def _():
        write(own, given)

    @pl.when(core == 1)
    def _():
        write(given, own)


def pack_yz(spec, fields, core, up, down, inner, outer):
    nx, ny, nz = fields.shape[1:]
    lane = lax.broadcasted_iota(jnp.int32, (1, nz), 1)
    for ref, sides in ((up, BEFORE), (down, AFTER)):
        total = jnp.zeros((ny, nz), jnp.float32)
        place = {k: i for i, k in enumerate(layers(spec[2], sides))}
        for comp, kind in spec[2]:
            offs = sides[kind]
            for x in range(nx):
                start = LANES * x + place[comp, offs[0]]
                shift = (start - offs[0]) % nz
                here = fields[comp, x]
                moved = pltpu.roll(here, shift, 1) if shift else here
                total = jnp.where((lane >= start) & (lane < start + len(offs)), moved, total)
        ref[...] = total

    def write(inner_sides, outer_sides):
        for ref, sides in ((inner, inner_sides), (outer, outer_sides)):
            for i, (comp, off) in enumerate(layers(spec[1], sides)):
                ref[i] = fields[comp, :, ny + off if sides is BEFORE else off, :]

    @pl.when(core == 0)
    def _():
        write(BEFORE, AFTER)

    @pl.when(core == 1)
    def _():
        write(AFTER, BEFORE)


def first_x_kernel(core, stress, own, given):
    nx = stress.shape[1]
    pack_x(STRESS, stress, {x: x for x in range(nx)}, nx, core[0], own, given)


def first_yz_kernel(core, stress, behind, *faces):
    pack_yz(STRESS, stress, core[0], *faces)


def gather_x_kernel(core, own, pair, along_x):
    here = core[0]
    there = 1 - here
    along_x[pl.ds(here * FACE, FACE)] = own[...]
    along_x[pl.ds(there * FACE, FACE)] = pair[pl.ds(there * FACE, FACE)]


def join_kernel(got_x, inner, taken):
    taken[: 2 * FACE] = got_x[...]
    taken[2 * FACE :] = inner[...]


def velocity_planes(faces, velocity, buoyancy, write):
    for x in faces.planes:
        scale = TIME_STEP * buoyancy[x]
        write(0, x, velocity[0, x] + scale * (faces.dx(0, x) + faces.dy(3, x) + faces.dz(4, x)))
        write(1, x, velocity[1, x] + scale * (faces.dx(3, x) + faces.dy(1, x) + faces.dz(5, x)))
        write(2, x, velocity[2, x] + scale * (faces.dx(4, x) + faces.dy(5, x) + faces.dz(2, x)))


def velocity_edge_kernel(core, stress, velocity, buoyancy, *refs):
    halos, (out, own, given, rows) = refs[:4], refs[4:]
    nx = stress.shape[1]
    place = edge_planes(nx)
    faces = Faces(STRESS, stress, list(place), core[0], halos, rows)

    def write(comp, x, value):
        out[comp, place[x]] = value

    velocity_planes(faces, velocity, buoyancy, write)
    pack_x(VELOCITY, out, place, nx, core[0], own, given)


def velocity_rest_kernel(core, stress, velocity, buoyancy, *refs):
    halos, (edge, behind, out, *packed, rows) = refs[:4], refs[4:]
    nx = stress.shape[1]
    place = edge_planes(nx)
    for x, at in place.items():
        for comp in range(3):
            out[comp, x] = edge[comp, at]
    inner = [x for x in range(nx) if x not in place]
    faces = Faces(STRESS, stress, inner, core[0], halos, rows)

    def write(comp, x, value):
        out[comp, x] = value

    velocity_planes(faces, velocity, buoyancy, write)
    pack_yz(VELOCITY, out, core[0], *packed)


def stress_planes(faces, first, table, stress, memory, cells, write):
    lam, shear, weight, mech, top_ref = cells
    nx, ny, nz = lam.shape
    tops = top_ref[...].astype(jnp.float32).T
    depth = (first[0] + lax.broadcasted_iota(jnp.int32, (1, nz), 1)).astype(jnp.float32)
    for x in faces.planes:
        decay = jnp.zeros((ny, nz), jnp.float32)
        for level in range(table.shape[0]):
            decay = jnp.where(mech[x] == level, table[level], decay)
        gain = (1.0 - decay) * weight[x]
        top = tops[:, x : x + 1]
        solid = depth >= top
        below = depth > top
        xx, yy, zz = faces.dx(0, x), faces.dy(1, x), faces.dz(2, x)
        volume = lam[x] * (xx + yy + zz)
        double = 2.0 * shear[x]
        rates = (
            volume + double * xx,
            volume + double * yy,
            volume + double * zz,
            shear[x] * (faces.dy(0, x) + faces.dx(1, x)),
            shear[x] * (faces.dz(0, x) + faces.dx(2, x)),
            shear[x] * (faces.dz(1, x) + faces.dy(2, x)),
        )
        for comp, rate in enumerate(rates):
            new = decay * memory[comp, x] + gain * rate
            keep = below if comp in (2, 4, 5) else solid
            moved = jnp.where(keep, stress[comp, x] + TIME_STEP * (rate - new), 0.0)
            write(comp, x, moved, new)


def stress_edge_kernel(core, first, table, velocity, stress, memory, *refs):
    cells, halos, (out, kept, own, given, rows) = refs[:5], refs[5:9], refs[9:]
    nx = stress.shape[1]
    place = edge_planes(nx)
    faces = Faces(VELOCITY, velocity, list(place), core[0], halos, rows)

    def write(comp, x, moved, new):
        out[comp, place[x]] = moved
        kept[comp, place[x]] = new

    stress_planes(faces, first, table, stress, memory, cells, write)
    pack_x(STRESS, out, place, nx, core[0], own, given)


def stress_rest_kernel(core, first, table, velocity, stress, memory, *refs):
    cells, halos = refs[:5], refs[5:9]
    edge, edge_kept, behind, out, kept, *packed, rows = refs[9:]
    nx = stress.shape[1]
    place = edge_planes(nx)
    for x, at in place.items():
        for comp in range(6):
            out[comp, x] = edge[comp, at]
            kept[comp, x] = edge_kept[comp, at]
    inner = [x for x in range(nx) if x not in place]
    faces = Faces(VELOCITY, velocity, inner, core[0], halos, rows)

    def write(comp, x, moved, new):
        out[comp, x] = moved
        kept[comp, x] = new

    stress_planes(faces, first, table, stress, memory, cells, write)
    pack_yz(STRESS, out, core[0], *packed)


def last_kernel(core, first, table, velocity, stress, memory, *refs):
    cells, halos, (out, kept, rows) = refs[:5], refs[5:9], refs[9:]
    planes = list(range(stress.shape[1]))
    faces = Faces(VELOCITY, velocity, planes, core[0], halos, rows)

    def write(comp, x, moved, new):
        out[comp, x] = moved
        kept[comp, x] = new

    stress_planes(faces, first, table, stress, memory, cells, write)


def call(body, outs, operands, scalars=1, scratch=(), hold=False, cost=None):
    vmem = pl.BlockSpec(memory_space=pltpu.VMEM)
    specs = [pl.BlockSpec(memory_space=pltpu.SMEM)] * scalars
    specs += [vmem] * (len(operands) - scalars)
    if hold:
        specs[-1] = pl.BlockSpec(memory_space=pl.ANY)
    return pl.pallas_call(
        body,
        out_shape=outs,
        in_specs=specs,
        out_specs=[vmem] * len(outs),
        scratch_shapes=list(scratch),
        cost_estimate=cost,
        compiler_params=pltpu.CompilerParams(vmem_limit_bytes=24 * 1024 * 1024),
    )(*operands)


def float32(*shape):
    return jax.ShapeDtypeStruct(shape, jnp.float32)


def core_pairs(gy):
    return [[j, j + 1] for j in range(0, gy, 2)]


def send_x(core, own, given):
    gx, gy = lax.axis_size("gx"), lax.axis_size("gy")
    pair = lax.all_gather(given, "gy", axis=0, tiled=True, axis_index_groups=core_pairs(gy))
    (along,) = call(gather_x_kernel, [float32(2 * FACE, *own.shape[1:])], [core, own, pair])
    pairs = []
    for j in range(gy):
        step = 1 - 2 * (j % 2)
        pairs += [(i * gy + j, (i + step) * gy + j) for i in range(gx) if 0 <= i + step < gx]
    return along, lax.ppermute(along, ("gx", "gy"), pairs)


def send_yz(up, down, inner, outer, got_x):
    gy, gz = lax.axis_size("gy"), lax.axis_size("gz")
    plane = up.shape
    pairs = [(k, k + 1) for k in range(gz - 1)]
    low = lax.ppermute(up, "gz", pairs)
    high = lax.ppermute(down, "gz", [(k, j) for j, k in pairs])
    chips = [(j, j + 1) for j in range(1, gy - 1, 2)]
    outer = lax.ppermute(outer, "gy", chips + [(k, j) for j, k in chips])
    (taken,) = call(join_kernel, [float32(TAKEN, *plane)], [got_x, inner], scalars=0)
    spread = lax.all_gather(taken, "gy", axis=0, tiled=True, axis_index_groups=core_pairs(gy))
    return spread, outer, low, high


def shards(
    velocity,
    stress,
    memory,
    lame_lambda,
    shear_modulus,
    buoyancy,
    anelastic_weight,
    decay_table,
    mech_index,
    surface_depth,
):
    nx, ny, nz = lame_lambda.shape
    core = (lax.axis_index("gy") % 2).astype(jnp.int32).reshape(1)
    first = (lax.axis_index("gz") * nz).astype(jnp.int32).reshape(1)
    like = lambda a: float32(*a.shape)
    scratch = [pltpu.VMEM((3, nx, ny + 16, nz), jnp.float32)]
    cost = pl.CostEstimate(flops=2**22, bytes_accessed=2**22, transcendentals=0)
    face_x = [float32(FACE, ny, nz)] * 2
    face_yz = [float32(ny, nz)] * 2 + [float32(FACE, ny, nz)] * 2
    cells = [lame_lambda, shear_modulus, anelastic_weight, mech_index, surface_depth]
    along, got_x = send_x(core, *call(first_x_kernel, face_x, [core, stress]))
    packed = call(first_yz_kernel, face_yz, [core, stress, along], hold=True, cost=cost)
    for step in range(STEPS):
        halos = send_yz(*packed, got_x)
        operands = [core, stress, velocity, buoyancy, *halos]
        edge, own, given = call(
            velocity_edge_kernel, [float32(3, 4, ny, nz)] + face_x, operands, scratch=scratch
        )
        along, got_x = send_x(core, own, given)
        velocity, *packed = call(
            velocity_rest_kernel,
            [like(velocity)] + face_yz,
            operands + [edge, along],
            scratch=scratch,
            hold=True,
            cost=cost,
        )
        halos = send_yz(*packed, got_x)
        operands = [core, first, decay_table, velocity, stress, memory, *cells, *halos]
        if step == STEPS - 1:
            stress, memory = call(
                last_kernel, [like(stress), like(memory)], operands, scalars=3, scratch=scratch
            )
            break
        edge, edge_kept, own, given = call(
            stress_edge_kernel,
            [float32(6, 4, ny, nz)] * 2 + face_x,
            operands,
            scalars=3,
            scratch=scratch,
        )
        along, got_x = send_x(core, own, given)
        stress, memory, *packed = call(
            stress_rest_kernel,
            [like(stress), like(memory)] + face_yz,
            operands + [edge, edge_kept, along],
            scalars=3,
            scratch=scratch,
            hold=True,
            cost=cost,
        )
    return (velocity, stress, memory)


def solution(mesh):
    fields = P(None, *AXES)
    cells = P(*AXES)
    return jax.shard_map(
        shards,
        mesh=mesh,
        in_specs=(fields,) * 3 + (cells,) * 4 + (P(), cells, P("gx", "gy")),
        out_specs=(fields,) * 3,
        check_vma=False,
    )
```

time: 91.6 us -> 100 us (1.092)
  starting transfers between devices: 31.3 us -> 56.8 us
  blocking collectives: 45.6 us -> 22.3 us
  Pallas kernels: 11.2 us -> 16.5 us
    ppermute x8 -> x12, starting transfers between devices: 26.2 us -> 51.6 us  [the longest x4 32.1 us: send_yz(): outer = lax.ppermute(outer, 'gy', chips + [(k, j) for j, k in chips])]
    all_gather x4 -> x0, blocking collectives: 23.5 us -> none  [send_yz(): lax.all_gather(given, 'gy', axis=0, tiled=True, axis_index_groups=core_pa...]
    pallas_call x21 -> x17, Pallas kernels: 11.2 us -> 16.5 us  [call(): pl.pallas_call(body, out_shape=outs, in_specs=specs, out_specs=[vmem] * l...]
  transfers between devices with their start and end apart: 12 -> 16, of which waited for: 0 -> 0; matrix products, arithmetic and copies ran while one was open for 0% -> 0% of each run, Pallas kernels for 7% -> 10%
where the time goes in v4:
time: 100 us; the launch traced here: 98.5 us
  starting transfers between devices  56.8 us (57%)
  blocking collectives  22.3 us (22%)
  Pallas kernels  16.5 us (16%)
  local copies, waits for them, and re-layouts  1.77 us (2%)
  between operations  1.07 us (1%)
    ppermute x4, starting transfers between devices, send_yz(): outer = lax.ppermute(outer, 'gy', chips + [(k, j) for j, k in chips])  32.1 us
    pallas_call x17, Pallas kernels, call(): pl.pallas_call(body, out_shape=outs, in_specs=specs, out_specs=[vmem] * l...  16.5 us
    ppermute x4, starting transfers between devices, send_yz(): low = lax.ppermute(up, 'gz', pairs)  14.3 us
    all_gather x4, blocking collectives, send_x(): lax.all_gather(given, 'gy', axis=0, tiled=True, axis_index_groups=core_pa...  14.1 us
    all_gather x4, blocking collectives, send_yz(): lax.all_gather(taken, 'gy', axis=0, tiled=True, axis_index_groups=core_pa...  8.19 us
    ppermute x4, starting transfers between devices, send_yz(): high = lax.ppermute(down, 'gz', [(k, j) for j, k in pairs])  5.17 us
    ppermute x4, starting transfers between devices, send_x(): return (along, lax.ppermute(along, ('gx', 'gy'), pairs))  5.16 us
  transfers between devices with their start and end apart: 16, of which 0 were waited for; matrix products, arithmetic and copies ran while one was open for 0% of the time, Pallas kernels for 10%

profile of v4, /device:TPU:1, one launch (start us, length us, event | category | flops | bytes accessed | tf_op | source)
XLA Modules:
  0.0 98.5 jit_solution(16301474190073303811)
XLA Ops:
  1.8 8.5 %all_gather.24.pair = f32[10,16,128]{2,1,0:T(8,128)S(1)} all-gather(f32[5,16,128]{2,1,0:T(8,128)S(1)} %get-tuple-element.38), channel_id=1, replica_groups={{0,4},{8,12},{16,20},{24,28},{1,5},{9,13},{17,21},{25,29},{2,6},{10,14}..., dimensions={0}, use_global_device_ids=true | all-gather | bytes 122880 | tf_op jit(solution)/shard_map/all_gather | solution.py:331
  12.0 1.4 %collective-permute-start.2 = (f32[16,128]{1,0:T(8,128)S(1)}, f32[16,128]{1,0:T(8,128)S(1)}, u32[]{:S(2)}, u32[]{:S(2)}) collective-permute-start(f32[16,128]{1,0:T(8,128)S(1)} %get-tuple-element.41), channel_id=1, source_target_pairs={{0,1},{1,2},{2,3},{4,5},{5,6},{6,7},{8,9},{9,10},{10,11},{12,13},{... | collective-permute-start | bytes 24584 | tf_op jit(solution)/shard_map/ppermute | solution.py:344
  13.4 1.3 %collective-permute-start.3 = (f32[16,128]{1,0:T(8,128)S(1)}, f32[16,128]{1,0:T(8,128)S(1)}, u32[]{:S(2)}, u32[]{:S(2)}) collective-permute-start(f32[16,128]{1,0:T(8,128)S(1)} %get-tuple-element.42), channel_id=1, source_target_pairs={{1,0},{2,1},{3,2},{5,4},{6,5},{7,6},{9,8},{10,9},{11,10},{13,12},{... | collective-permute-start | bytes 24584 | tf_op jit(solution)/shard_map/ppermute | solution.py:345
  14.7 8.4 %collective-permute-start.1 = (f32[5,16,128]{2,1,0:T(8,128)S(1)}, f32[5,16,128]{2,1,0:T(8,128)S(1)}, u32[]{:S(2)}, u32[]{:S(2)}) collective-permute-start(f32[5,16,128]{2,1,0:T(8,128)S(1)} %get-tuple-element.40), channel_id=1, source_target_pairs={{4,8},{12,16},{20,24},{8,4},{16,12},{24,20},{5,9},{13,17},{21,25},... | collective-permute-start | bytes 122888 | tf_op jit(solution)/shard_map/ppermute | solution.py:347
  23.1 2.1 %all_gather.25.refs_0_ = f32[30,16,128]{2,1,0:T(8,128)S(1)} all-gather(f32[15,16,128]{2,1,0:T(8,128)S(1)} %shard_map.124), channel_id=1, replica_groups={{0,4},{8,12},{16,20},{24,28},{1,5},{9,13},{17,21},{25,29},{2,6},{10,14}..., dimensions={0}, use_global_device_ids=true | all-gather | bytes 368640 | tf_op jit(solution)/shard_map/all_gather | solution.py:349
  25.6 1.9 %all_gather.26.pair = f32[10,16,128]{2,1,0:T(8,128)S(1)} all-gather(f32[5,16,128]{2,1,0:T(8,128)S(1)} %get-tuple-element.45), channel_id=1, replica_groups={{0,4},{8,12},{16,20},{24,28},{1,5},{9,13},{17,21},{25,29},{2,6},{10,14}..., dimensions={0}, use_global_device_ids=true | all-gather | bytes 122880 | tf_op jit(solution)/shard_map/all_gather | solution.py:331
  27.5 1.3 %collective-permute-start.4 = (f32[10,16,128]{2,1,0:T(8,128)S(1)}, f32[10,16,128]{2,1,0:T(8,128)S(1)}, u32[]{:S(2)}, u32[]{:S(2)}) collective-permute-start(f32[10,16,128]{2,1,0:T(8,128)S(1)} %shard_map.126.refs_5_), channel_id=1, source_target_pairs={{0,32},{32,64},{64,96},{96,128},{128,160},{160,192},{192,224},{224... | collective-permute-start | bytes 245768 | tf_op jit(solution)/shard_map/ppermute | solution.py:337
  28.8 2.7 %shard_map.127 = (f32[3,16,16,128]{3,2,1,0:T(8,128)S(1)}, f32[16,128]{1,0:T(8,128)S(1)}, f32[16,128]{1,0:T(8,128)S(1)}, f32[5,16,128]{2,1,0:T(8,128)S(1)}, f32[5,16,128]{2,1,0:T(8,128)S(1)}) custom-call(s32[1]{0:T(128)} %bitcast.core, f32[6,16,16,128]{3,2,1,0:T(8,128)S(1)} %copy-done.1, f32[3,16,16,128]{3,2,1,0:T(8,128)S(1)} %copy-done.4, ...), custom_call_target="tpu_custom_call" | custom-call | flops 4194304 | bytes 4194304 | tf_op jit(solution)/shard_map/pallas_call | solution.py:310
  31.5 4.3 %collective-permute-start.6 = (f32[16,128]{1,0:T(8,128)S(1)}, f32[16,128]{1,0:T(8,128)S(1)}, u32[]{:S(2)}, u32[]{:S(2)}) collective-permute-start(f32[16,128]{1,0:T(8,128)S(1)} %get-tuple-element.49), channel_id=1, source_target_pairs={{0,1},{1,2},{2,3},{4,5},{5,6},{6,7},{8,9},{9,10},{10,11},{12,13},{... | collective-permute-start | bytes 24584 | tf_op jit(solution)/shard_map/ppermute | solution.py:344
  37.1 10.4 %collective-permute-start.5 = (f32[5,16,128]{2,1,0:T(8,128)S(1)}, f32[5,16,128]{2,1,0:T(8,128)S(1)}, u32[]{:S(2)}, u32[]{:S(2)}) collective-permute-start(f32[5,16,128]{2,1,0:T(8,128)S(1)} %get-tuple-element.48), channel_id=1, source_target_pairs={{4,8},{12,16},{20,24},{8,4},{16,12},{24,20},{5,9},{13,17},{21,25},... | collective-permute-start | bytes 122888 | tf_op jit(solution)/shard_map/ppermute | solution.py:347
  47.6 2.1 %all_gather.27.refs_5_ = f32[30,16,128]{2,1,0:T(8,128)S(1)} all-gather(f32[15,16,128]{2,1,0:T(8,128)S(1)} %shard_map.128), channel_id=1, replica_groups={{0,4},{8,12},{16,20},{24,28},{1,5},{9,13},{17,21},{25,29},{2,6},{10,14}..., dimensions={0}, use_global_device_ids=true | all-gather | bytes 368640 | tf_op jit(solution)/shard_map/all_gather | solution.py:349
  51.3 1.9 %all_gather.28.pair = f32[10,16,128]{2,1,0:T(8,128)S(1)} all-gather(f32[5,16,128]{2,1,0:T(8,128)S(1)} %get-tuple-element.54), channel_id=1, replica_groups={{0,4},{8,12},{16,20},{24,28},{1,5},{9,13},{17,21},{25,29},{2,6},{10,14}..., dimensions={0}, use_global_device_ids=true | all-gather | bytes 122880 | tf_op jit(solution)/shard_map/all_gather | solution.py:331
  53.2 1.3 %collective-permute-start.8 = (f32[10,16,128]{2,1,0:T(8,128)S(1)}, f32[10,16,128]{2,1,0:T(8,128)S(1)}, u32[]{:S(2)}, u32[]{:S(2)}) collective-permute-start(f32[10,16,128]{2,1,0:T(8,128)S(1)} %shard_map.130.refs_11_), channel_id=1, source_target_pairs={{0,32},{32,64},{64,96},{96,128},{128,160},{160,192},{192,224},{224... | collective-permute-start | bytes 245768 | tf_op jit(solution)/shard_map/ppermute | solution.py:337
  54.5 3.5 %shard_map.131 = (f32[6,16,16,128]{3,2,1,0:T(8,128)S(1)}, f32[6,16,16,128]{3,2,1,0:T(8,128)S(1)}, f32[16,128]{1,0:T(8,128)S(1)}, f32[16,128]{1,0:T(8,128)S(1)}, ...) custom-call(s32[1]{0:T(128)} %bitcast.core, s32[1]{0:T(128)} %bitcast.1.first, f32[8]{0:T(128)S(1)} %copy-done.11, ...), custom_call_target="tpu_custom_call" | custom-call | flops 4194304 | bytes 4194304 | tf_op jit(solution)/shard_map/pallas_call | solution.py:310
  58.0 4.3 %collective-permute-start.10 = (f32[16,128]{1,0:T(8,128)S(1)}, f32[16,128]{1,0:T(8,128)S(1)}, u32[]{:S(2)}, u32[]{:S(2)}) collective-permute-start(f32[16,128]{1,0:T(8,128)S(1)} %get-tuple-element.58), channel_id=1, source_target_pairs={{0,1},{1,2},{2,3},{4,5},{5,6},{6,7},{8,9},{9,10},{10,11},{12,13},{... | collective-permute-start | bytes 24584 | tf_op jit(solution)/shard_map/ppermute | solution.py:344
  63.6 6.4 %collective-permute-start.9 = (f32[5,16,128]{2,1,0:T(8,128)S(1)}, f32[5,16,128]{2,1,0:T(8,128)S(1)}, u32[]{:S(2)}, u32[]{:S(2)}) collective-permute-start(f32[5,16,128]{2,1,0:T(8,128)S(1)} %get-tuple-element.57), channel_id=1, source_target_pairs={{4,8},{12,16},{20,24},{8,4},{16,12},{24,20},{5,9},{13,17},{21,25},... | collective-permute-start | bytes 122888 | tf_op jit(solution)/shard_map/ppermute | solution.py:347
  70.0 2.0 %all_gather.29.refs_0_ = f32[30,16,128]{2,1,0:T(8,128)S(1)} all-gather(f32[15,16,128]{2,1,0:T(8,128)S(1)} %shard_map.132), channel_id=1, replica_groups={{0,4},{8,12},{16,20},{24,28},{1,5},{9,13},{17,21},{25,29},{2,6},{10,14}..., dimensions={0}, use_global_device_ids=true | all-gather | bytes 368640 | tf_op jit(solution)/shard_map/all_gather | solution.py:349
  72.3 1.9 %all_gather.30.pair = f32[10,16,128]{2,1,0:T(8,128)S(1)} all-gather(f32[5,16,128]{2,1,0:T(8,128)S(1)} %get-tuple-element.62), channel_id=1, replica_groups={{0,4},{8,12},{16,20},{24,28},{1,5},{9,13},{17,21},{25,29},{2,6},{10,14}..., dimensions={0}, use_global_device_ids=true | all-gather | bytes 122880 | tf_op jit(solution)/shard_map/all_gather | solution.py:331
  75.5 3.5 %shard_map.135 = (f32[3,16,16,128]{3,2,1,0:T(8,128)}, f32[16,128]{1,0:T(8,128)S(1)}, f32[16,128]{1,0:T(8,128)S(1)}, f32[5,16,128]{2,1,0:T(8,128)S(1)}, f32[5,16,128]{2,1,0:T(8,128)S(1)}) custom-call(s32[1]{0:T(128)} %bitcast.core, f32[6,16,16,128]{3,2,1,0:T(8,128)S(1)} %get-tuple-element.55.stress, f32[3,16,16,128]{3,2,1,0:T(8,128)S(1)} %get-tuple-element.46.velocity, ...), custom_call_target="tpu_custom_call" | custom-call | flops 4194304 | bytes 4194304 | tf_op jit(solution)/shard_map/pallas_call | solution.py:310
  79.0 4.4 %collective-permute-start.14 = (f32[16,128]{1,0:T(8,128)S(1)}, f32[16,128]{1,0:T(8,128)S(1)}, u32[]{:S(2)}, u32[]{:S(2)}) collective-permute-start(f32[16,128]{1,0:T(8,128)S(1)} %get-tuple-element.67), channel_id=1, source_target_pairs={{0,1},{1,2},{2,3},{4,5},{5,6},{6,7},{8,9},{9,10},{10,11},{12,13},{... | collective-permute-start | bytes 24584 | tf_op jit(solution)/shard_map/ppermute | solution.py:344
  83.4 1.3 %collective-permute-start.15 = (f32[16,128]{1,0:T(8,128)S(1)}, f32[16,128]{1,0:T(8,128)S(1)}, u32[]{:S(2)}, u32[]{:S(2)}) collective-permute-start(f32[16,128]{1,0:T(8,128)S(1)} %get-tuple-element.68), channel_id=1, source_target_pairs={{1,0},{2,1},{3,2},{5,4},{6,5},{7,6},{9,8},{10,9},{11,10},{13,12},{... | collective-permute-start | bytes 24584 | tf_op jit(solution)/shard_map/ppermute | solution.py:345
  84.7 6.9 %collective-permute-start.13 = (f32[5,16,128]{2,1,0:T(8,128)S(1)}, f32[5,16,128]{2,1,0:T(8,128)S(1)}, u32[]{:S(2)}, u32[]{:S(2)}) collective-permute-start(f32[5,16,128]{2,1,0:T(8,128)S(1)} %get-tuple-element.66), channel_id=1, source_target_pairs={{4,8},{12,16},{20,24},{8,4},{16,12},{24,20},{5,9},{13,17},{21,25},... | collective-permute-start | bytes 122888 | tf_op jit(solution)/shard_map/ppermute | solution.py:347
  91.6 2.0 %all_gather.31.refs_5_ = f32[30,16,128]{2,1,0:T(8,128)S(1)} all-gather(f32[15,16,128]{2,1,0:T(8,128)S(1)} %shard_map.136), channel_id=1, replica_groups={{0,4},{8,12},{16,20},{24,28},{1,5},{9,13},{17,21},{25,29},{2,6},{10,14}..., dimensions={0}, use_global_device_ids=true | all-gather | bytes 368640 | tf_op jit(solution)/shard_map/all_gather | solution.py:349
  93.6 4.9 %shard_map.137 = (f32[6,16,16,128]{3,2,1,0:T(8,128)}, f32[6,16,16,128]{3,2,1,0:T(8,128)}) custom-call(s32[1]{0:T(128)} %bitcast.core, s32[1]{0:T(128)} %bitcast.1.first, f32[8]{0:T(128)S(1)} %copy-done.11, f32[3,16,16,128]{3,2,1,0:T(8,128)S(1)} %copy-done.9, f32[6,16,16,128]{3,2,1,0:T(8,128)S(1)} %get-tuple-element.55.stress, ...), custom_call_target="tpu_custom_call" | custom-call | tf_op jit(solution)/shard_map/pallas_call | solution.py:310
  (57 shorter events, 8.9 us)
Async XLA Ops:
  1.8 9.8 %copy-start.1 = (f32[6,16,16,128]{3,2,1,0:T(8,128)S(1)}, f32[6,16,16,128]{3,2,1,0:T(8,128)}, u32[]{:S(2)}) copy-start(f32[6,16,16,128]{3,2,1,0:T(8,128)} %stress.11) | copy-start | bytes 2359300
  10.3 12.8 %collective-permute-start = (f32[10,16,128]{2,1,0:T(8,128)S(1)}, f32[10,16,128]{2,1,0:T(8,128)S(1)}, u32[]{:S(2)}, u32[]{:S(2)}) collective-permute-start(f32[10,16,128]{2,1,0:T(8,128)S(1)} %shard_map.122.behind), channel_id=1, source_target_pairs={{0,32},{32,64},{64,96},{96,128},{128,160},{160,192},{192,224},{224... | collective-permute-start | bytes 245768 | tf_op jit(solution)/shard_map/ppermute | solution.py:337
  11.9 13.3 %copy-start.4 = (f32[3,16,16,128]{3,2,1,0:T(8,128)S(1)}, f32[3,16,16,128]{3,2,1,0:T(8,128)}, u32[]{:S(2)}) copy-start(f32[3,16,16,128]{3,2,1,0:T(8,128)} %velocity.3) | copy-start | bytes 1179652
  12.0 13.3 %collective-permute-start.2 = (f32[16,128]{1,0:T(8,128)S(1)}, f32[16,128]{1,0:T(8,128)S(1)}, u32[]{:S(2)}, u32[]{:S(2)}) collective-permute-start(f32[16,128]{1,0:T(8,128)S(1)} %get-tuple-element.41), channel_id=1, source_target_pairs={{0,1},{1,2},{2,3},{4,5},{5,6},{6,7},{8,9},{9,10},{10,11},{12,13},{... | collective-permute-start | bytes 24584 | tf_op jit(solution)/shard_map/ppermute | solution.py:344
  13.4 11.9 %collective-permute-start.3 = (f32[16,128]{1,0:T(8,128)S(1)}, f32[16,128]{1,0:T(8,128)S(1)}, u32[]{:S(2)}, u32[]{:S(2)}) collective-permute-start(f32[16,128]{1,0:T(8,128)S(1)} %get-tuple-element.42), channel_id=1, source_target_pairs={{1,0},{2,1},{3,2},{5,4},{6,5},{7,6},{9,8},{10,9},{11,10},{13,12},{... | collective-permute-start | bytes 24584 | tf_op jit(solution)/shard_map/ppermute | solution.py:345
  14.7 10.6 %collective-permute-start.1 = (f32[5,16,128]{2,1,0:T(8,128)S(1)}, f32[5,16,128]{2,1,0:T(8,128)S(1)}, u32[]{:S(2)}, u32[]{:S(2)}) collective-permute-start(f32[5,16,128]{2,1,0:T(8,128)S(1)} %get-tuple-element.40), channel_id=1, source_target_pairs={{4,8},{12,16},{20,24},{8,4},{16,12},{24,20},{5,9},{13,17},{21,25},... | collective-permute-start | bytes 122888 | tf_op jit(solution)/shard_map/ppermute | solution.py:347
  27.5 20.0 %collective-permute-start.4 = (f32[10,16,128]{2,1,0:T(8,128)S(1)}, f32[10,16,128]{2,1,0:T(8,128)S(1)}, u32[]{:S(2)}, u32[]{:S(2)}) collective-permute-start(f32[10,16,128]{2,1,0:T(8,128)S(1)} %shard_map.126.refs_5_), channel_id=1, source_target_pairs={{0,32},{32,64},{64,96},{96,128},{128,160},{160,192},{192,224},{224... | collective-permute-start | bytes 245768 | tf_op jit(solution)/shard_map/ppermute | solution.py:337
  28.8 21.0 %copy-start.2 = (f32[6,16,16,128]{3,2,1,0:T(8,128)S(1)}, f32[6,16,16,128]{3,2,1,0:T(8,128)}, u32[]{:S(2)}) copy-start(f32[6,16,16,128]{3,2,1,0:T(8,128)} %memory.3) | copy-start | bytes 2359300
  31.5 18.2 %collective-permute-start.6 = (f32[16,128]{1,0:T(8,128)S(1)}, f32[16,128]{1,0:T(8,128)S(1)}, u32[]{:S(2)}, u32[]{:S(2)}) collective-permute-start(f32[16,128]{1,0:T(8,128)S(1)} %get-tuple-element.49), channel_id=1, source_target_pairs={{0,1},{1,2},{2,3},{4,5},{5,6},{6,7},{8,9},{9,10},{10,11},{12,13},{... | collective-permute-start | bytes 24584 | tf_op jit(solution)/shard_map/ppermute | solution.py:344
  35.8 13.9 %collective-permute-start.7 = (f32[16,128]{1,0:T(8,128)S(1)}, f32[16,128]{1,0:T(8,128)S(1)}, u32[]{:S(2)}, u32[]{:S(2)}) collective-permute-start(f32[16,128]{1,0:T(8,128)S(1)} %get-tuple-element.50), channel_id=1, source_target_pairs={{1,0},{2,1},{3,2},{5,4},{6,5},{7,6},{9,8},{10,9},{11,10},{13,12},{... | collective-permute-start | bytes 24584 | tf_op jit(solution)/shard_map/ppermute | solution.py:345
  37.1 12.6 %collective-permute-start.5 = (f32[5,16,128]{2,1,0:T(8,128)S(1)}, f32[5,16,128]{2,1,0:T(8,128)S(1)}, u32[]{:S(2)}, u32[]{:S(2)}) collective-permute-start(f32[5,16,128]{2,1,0:T(8,128)S(1)} %get-tuple-element.48), channel_id=1, source_target_pairs={{4,8},{12,16},{20,24},{8,4},{16,12},{24,20},{5,9},{13,17},{21,25},... | collective-permute-start | bytes 122888 | tf_op jit(solution)/shard_map/ppermute | solution.py:347
  47.5 2.2 %copy-start.7 = (f32[16,16,128]{2,1,0:T(8,128)S(1)}, f32[16,16,128]{2,1,0:T(8,128)}, u32[]{:S(2)}) copy-start(f32[16,16,128]{2,1,0:T(8,128)} %refs_2_.5) | copy-start | bytes 393220
  47.5 2.2 %copy-start.8 = (s32[16,16,128]{2,1,0:T(8,128)S(1)}, s32[16,16,128]{2,1,0:T(8,128)}, u32[]{:S(2)}) copy-start(s32[16,16,128]{2,1,0:T(8,128)} %refs_3_.5) | copy-start | bytes 393220
  47.6 2.2 %copy-start.5 = (f32[16,16,128]{2,1,0:T(8,128)S(1)}, f32[16,16,128]{2,1,0:T(8,128)}, u32[]{:S(2)}) copy-start(f32[16,16,128]{2,1,0:T(8,128)} %refs_0_.5) | copy-start | bytes 393220
  47.6 2.2 %copy-start.6 = (f32[16,16,128]{2,1,0:T(8,128)S(1)}, f32[16,16,128]{2,1,0:T(8,128)}, u32[]{:S(2)}) copy-start(f32[16,16,128]{2,1,0:T(8,128)} %refs_1_.5) | copy-start | bytes 393220
  53.2 16.8 %collective-permute-start.8 = (f32[10,16,128]{2,1,0:T(8,128)S(1)}, f32[10,16,128]{2,1,0:T(8,128)S(1)}, u32[]{:S(2)}, u32[]{:S(2)}) collective-permute-start(f32[10,16,128]{2,1,0:T(8,128)S(1)} %shard_map.130.refs_11_), channel_id=1, source_target_pairs={{0,32},{32,64},{64,96},{96,128},{128,160},{160,192},{192,224},{224... | collective-permute-start | bytes 245768 | tf_op jit(solution)/shard_map/ppermute | solution.py:337
  58.0 14.0 %collective-permute-start.10 = (f32[16,128]{1,0:T(8,128)S(1)}, f32[16,128]{1,0:T(8,128)S(1)}, u32[]{:S(2)}, u32[]{:S(2)}) collective-permute-start(f32[16,128]{1,0:T(8,128)S(1)} %get-tuple-element.58), channel_id=1, source_target_pairs={{0,1},{1,2},{2,3},{4,5},{5,6},{6,7},{8,9},{9,10},{10,11},{12,13},{... | collective-permute-start | bytes 24584 | tf_op jit(solution)/shard_map/ppermute | solution.py:344
  62.3 9.7 %collective-permute-start.11 = (f32[16,128]{1,0:T(8,128)S(1)}, f32[16,128]{1,0:T(8,128)S(1)}, u32[]{:S(2)}, u32[]{:S(2)}) collective-permute-start(f32[16,128]{1,0:T(8,128)S(1)} %get-tuple-element.59), channel_id=1, source_target_pairs={{1,0},{2,1},{3,2},{5,4},{6,5},{7,6},{9,8},{10,9},{11,10},{13,12},{... | collective-permute-start | bytes 24584 | tf_op jit(solution)/shard_map/ppermute | solution.py:345
  63.6 8.4 %collective-permute-start.9 = (f32[5,16,128]{2,1,0:T(8,128)S(1)}, f32[5,16,128]{2,1,0:T(8,128)S(1)}, u32[]{:S(2)}, u32[]{:S(2)}) collective-permute-start(f32[5,16,128]{2,1,0:T(8,128)S(1)} %get-tuple-element.57), channel_id=1, source_target_pairs={{4,8},{12,16},{20,24},{8,4},{16,12},{24,20},{5,9},{13,17},{21,25},... | collective-permute-start | bytes 122888 | tf_op jit(solution)/shard_map/ppermute | solution.py:347
  74.2 17.4 %collective-permute-start.12 = (f32[10,16,128]{2,1,0:T(8,128)S(1)}, f32[10,16,128]{2,1,0:T(8,128)S(1)}, u32[]{:S(2)}, u32[]{:S(2)}) collective-permute-start(f32[10,16,128]{2,1,0:T(8,128)S(1)} %shard_map.134.refs_5_), channel_id=1, source_target_pairs={{0,32},{32,64},{64,96},{96,128},{128,160},{160,192},{192,224},{224... | collective-permute-start | bytes 245768 | tf_op jit(solution)/shard_map/ppermute | solution.py:337
  79.0 14.6 %copy-start.9 = (f32[3,16,16,128]{3,2,1,0:T(8,128)S(1)}, f32[3,16,16,128]{3,2,1,0:T(8,128)}, u32[]{:S(2)}) copy-start(f32[3,16,16,128]{3,2,1,0:T(8,128)} %get-tuple-element.34.velocity) | copy-start | bytes 1179652
  79.0 14.6 %collective-permute-start.14 = (f32[16,128]{1,0:T(8,128)S(1)}, f32[16,128]{1,0:T(8,128)S(1)}, u32[]{:S(2)}, u32[]{:S(2)}) collective-permute-start(f32[16,128]{1,0:T(8,128)S(1)} %get-tuple-element.67), channel_id=1, source_target_pairs={{0,1},{1,2},{2,3},{4,5},{5,6},{6,7},{8,9},{9,10},{10,11},{12,13},{... | collective-permute-start | bytes 24584 | tf_op jit(solution)/shard_map/ppermute | solution.py:344
  83.4 10.2 %collective-permute-start.15 = (f32[16,128]{1,0:T(8,128)S(1)}, f32[16,128]{1,0:T(8,128)S(1)}, u32[]{:S(2)}, u32[]{:S(2)}) collective-permute-start(f32[16,128]{1,0:T(8,128)S(1)} %get-tuple-element.68), channel_id=1, source_target_pairs={{1,0},{2,1},{3,2},{5,4},{6,5},{7,6},{9,8},{10,9},{11,10},{13,12},{... | collective-permute-start | bytes 24584 | tf_op jit(solution)/shard_map/ppermute | solution.py:345
  84.7 8.9 %collective-permute-start.13 = (f32[5,16,128]{2,1,0:T(8,128)S(1)}, f32[5,16,128]{2,1,0:T(8,128)S(1)}, u32[]{:S(2)}, u32[]{:S(2)}) collective-permute-start(f32[5,16,128]{2,1,0:T(8,128)S(1)} %get-tuple-element.66), channel_id=1, source_target_pairs={{4,8},{12,16},{20,24},{8,4},{16,12},{24,20},{5,9},{13,17},{21,25},... | collective-permute-start | bytes 122888 | tf_op jit(solution)/shard_map/ppermute | solution.py:347
  (4 other events, 6.1 us)

commit v5 on v2

--- a/solution.py
+++ b/solution.py
@@ -45,6 +45,13 @@
     return COEF_NEAR * (a - b) + COEF_FAR * (c - d)
 
 
+def thirds(value):
+    high = value.astype(jnp.bfloat16)
+    rest = value - high.astype(jnp.float32)
+    middle = rest.astype(jnp.bfloat16)
+    return high, middle, (rest - middle.astype(jnp.float32)).astype(jnp.bfloat16)
+
+
 class Faces:
     def __init__(self, spec, fields, core, pair, spread, outer, rows, edges):
         self.spec, self.fields, self.rows, self.edges = spec, fields, rows, edges
@@ -83,26 +90,28 @@
         got = jnp.concatenate([jnp.concatenate([e[:8], e[8:]], axis=1) for e in ends], axis=0)
         row = lax.broadcasted_iota(jnp.int32, (16, nz), 0)
         lane = lax.broadcasted_iota(jnp.int32, (16, nz), 1)
-        for slot, (comp, kind) in enumerate(self.spec[2]):
-            weights = jnp.zeros((16, nz), jnp.float32)
+        weights = []
+        for comp, kind in self.spec[2]:
+            here = jnp.zeros((16, nz), jnp.float32)
             for shift, weight in TAPS[kind]:
+                scaled = float(round(24 * weight))
                 for off in BEFORE[kind]:
                     at = off - shift
                     if 0 <= at < nz:
                         hit = (row == self.before[2][comp, off]) & (lane == at)
-                        weights = weights + jnp.where(hit, weight, 0.0)
+                        here = jnp.where(hit, scaled, here)
                 for off in AFTER[kind]:
                     at = nz + off - shift
                     if 0 <= at < nz:
                         hit = (row == 8 + self.after[2][comp, off]) & (lane == at)
-                        weights = weights + jnp.where(hit, weight, 0.0)
-            self.edges[slot] = lax.dot_general(
-                got,
-                weights,
-                (((0,), (0,)), ((), ())),
-                precision=lax.Precision.HIGHEST,
-                preferred_element_type=jnp.float32,
-            )
+                        here = jnp.where(hit, scaled, here)
+            weights.append(here)
+        weights = jnp.concatenate(weights, axis=1).astype(jnp.bfloat16)
+        weights = jnp.concatenate([weights] * 3, axis=0)
+        stacked = jnp.concatenate([p.astype(jnp.float32) for p in thirds(got)], axis=0).T
+        total = jnp.dot(stacked.astype(jnp.bfloat16), weights, preferred_element_type=jnp.float32)
+        for slot in range(3):
+            self.edges[slot] = total[:, slot * nz : (slot + 1) * nz] * (1.0 / 24.0)
 
     def dx(self, comp, x):
         kind = dict(self.spec[0])[comp]
@@ -153,14 +162,12 @@
         for i, (c, off) in enumerate(after):
             if c == comp:
                 pick = jnp.where((row == 8 + i) & (lane == off), 1.0, pick)
-        part = lax.dot_general(
-            pick,
-            fields[comp].reshape(nx * ny, nz),
-            (((1,), (1,)), ((), ())),
-            precision=lax.Precision.HIGHEST,
-            preferred_element_type=jnp.float32,
-        )
-        total = part if total is None else total + part
+        pick = pick.astype(jnp.bfloat16)
+        for third in thirds(fields[comp].reshape(nx * ny, nz)):
+            part = lax.dot_general(
+                pick, third, (((1,), (1,)), ((), ())), preferred_element_type=jnp.float32
+            )
+            total = part if total is None else total + part
     half = nx * ny // 2
     ends = [jnp.concatenate([t[:, :half], t[:, half:]], axis=0) for t in (total[:8], total[8:])]
 
@@ -216,14 +223,21 @@
     pack(VELOCITY, out, core[0], *refs[8:10])
 
 
+GROUPS = 4
+
+
 def stress_kernel(send, *refs):
     core, first, table, velocity, stress, memory, lam, shear, weight, mech, top_ref = refs[:11]
     pair, spread, outer, out, kept = refs[11:16]
+    if not send:
+        finals = out, kept
+        out, kept, sems = refs[16:19]
     faces = Faces(VELOCITY, velocity, core[0], pair, spread, outer, refs[-2], refs[-1])
     faces.prepare()
     nx, ny, nz = lam.shape
     tops = top_ref[...].astype(jnp.float32).T
     depth = (first[0] + lax.broadcasted_iota(jnp.int32, (1, nz), 1)).astype(jnp.float32)
+    copies = []
     for x in range(nx):
         decay = jnp.zeros((ny, nz), jnp.float32)
         for level in range(table.shape[0]):
@@ -248,18 +262,29 @@
             kept[comp, x] = new
             keep = below if comp in (2, 4, 5) else solid
             out[comp, x] = jnp.where(keep, stress[comp, x] + TIME_STEP * (rate - new), 0.0)
+        size = nx // GROUPS
+        if not send and (x + 1) % size == 0:
+            part = pl.ds(x + 1 - size, size)
+            for i, (held, final) in enumerate(zip((out, kept), finals)):
+                copy = pltpu.make_async_copy(
+                    held.at[:, part], final.at[:, part], sems.at[i, x // size]
+                )
+                copy.start()
+                copies.append(copy)
+    for copy in copies:
+        copy.wait()
     if send:
         pack(STRESS, out, core[0], *refs[16:18])
 
 
-def call(body, outs, operands, scalars=1, scratch=()):
+def call(body, outs, operands, scalars=1, scratch=(), out_space=pltpu.VMEM):
     vmem = pl.BlockSpec(memory_space=pltpu.VMEM)
     smem = pl.BlockSpec(memory_space=pltpu.SMEM)
     return pl.pallas_call(
         body,
         out_shape=outs,
         in_specs=[smem if i < scalars else vmem for i in range(len(operands))],
-        out_specs=[vmem] * len(outs),
+        out_specs=[pl.BlockSpec(memory_space=out_space)] * len(outs),
         scratch_shapes=list(scratch),
         compiler_params=pltpu.CompilerParams(vmem_limit_bytes=24 * 1024 * 1024),
     )(*operands)
@@ -308,6 +333,11 @@
     scratch = (
         pltpu.VMEM((3, nx, ny + 16, nz), jnp.float32),
         pltpu.VMEM((3, nx * ny, nz), jnp.float32),
+    )
+    held = (
+        pltpu.VMEM(stress.shape, jnp.float32),
+        pltpu.VMEM(memory.shape, jnp.float32),
+        pltpu.SemaphoreType.DMA((2, GROUPS)),
     )
     own, given = call(first_kernel, packed, [core, stress])
     for step in range(STEPS):
@@ -336,7 +366,8 @@
                 *exchange(core, own, given),
             ],
             scalars=3,
-            scratch=scratch,
+            scratch=scratch if send else held + scratch,
+            out_space=pltpu.VMEM if send else pl.ANY,
         )
         if send:
             own, given = rest

time: 85.8 us -> 83.3 us (0.971)
  Pallas kernels: 9.48 us -> 6.96 us
    pallas_call x13, Pallas kernels: 9.48 us -> 6.96 us  [call(): pl.pallas_call(body, out_shape=outs, in_specs=[smem if i < scalars else v...]
where the time goes in v5:
time: 83.3 us; the launch traced here: 82 us
  starting transfers between devices  49.4 us (59%)
  blocking collectives  22.4 us (27%)
  Pallas kernels  6.96 us (8%)
  local copies, waits for them, and re-layouts  1.78 us (2%)
  between operations  0.99 us (1%)
    ppermute x4, starting transfers between devices, exchange(): outer = lax.ppermute(along_y, 'gy', to_y)  38.8 us
    all_gather x4, blocking collectives, exchange(): lax.all_gather(given, 'gy', axis=0, tiled=True, axis_index_groups=cores)  14.4 us
    all_gather x4, blocking collectives, exchange(): lax.all_gather(taken, 'gy', axis=0, tiled=True, axis_index_groups=cores)  8.05 us
    pallas_call x13, Pallas kernels, call(): pl.pallas_call(body, out_shape=outs, in_specs=[smem if i < scalars else v...  6.96 us
    ppermute x4, starting transfers between devices, exchange(): got_x = lax.ppermute(along_x, ('gx', 'gy'), to_x)  5.43 us
    ppermute x4, starting transfers between devices, exchange(): got_z = lax.ppermute(along_z, ('gy', 'gz'), to_z)  5.17 us
    unnamed x24, local copies, waits for them, and re-layouts  1.78 us
  transfers between devices with their start and end apart: 12, of which 1 were waited for; matrix products, arithmetic and copies ran while one was open for 0% of the time, Pallas kernels for 0%

profile of v5, /device:TPU:1, one launch (start us, length us, event | category | flops | bytes accessed | tf_op | source)
XLA Modules:
  0.0 82.0 jit_solution(2043762386185660763)
XLA Ops:
  0.7 1.1 %copy-done = f32[6,16,16,128]{3,2,1,0:T(8,128)S(1)} copy-done((f32[6,16,16,128]{3,2,1,0:T(8,128)S(1)}, f32[6,16,16,128]{3,2,1,0:T(8,128)}, u32[]{:S(2)}) %copy-start) | copy-done | bytes 786456
  2.1 8.4 %all_gather.24.pair.refs_4_ = f32[22,16,128]{2,1,0:T(8,128)S(1)} all-gather(f32[11,16,128]{2,1,0:T(8,128)S(1)} %get-tuple-element.29), channel_id=1, replica_groups={{0,4},{8,12},{16,20},{24,28},{1,5},{9,13},{17,21},{25,29},{2,6},{10,14}..., dimensions={0}, use_global_device_ids=true | all-gather | bytes 270336 | tf_op jit(solution)/shard_map/all_gather | solution.py:298
  10.6 1.4 %collective-permute-start = (f32[10,16,128]{2,1,0:T(8,128)S(1)}, f32[10,16,128]{2,1,0:T(8,128)S(1)}, u32[]{:S(2)}, u32[]{:S(2)}) collective-permute-start(f32[10,16,128]{2,1,0:T(8,128)S(1)} %get-tuple-element.31), channel_id=1, source_target_pairs={{0,32},{32,64},{64,96},{96,128},{128,160},{160,192},{192,224},{224... | collective-permute-start | bytes 245768 | tf_op jit(solution)/shard_map/ppermute | solution.py:308
  12.0 1.3 %collective-permute-start.1 = (f32[2,16,128]{2,1,0:T(8,128)S(1)}, f32[2,16,128]{2,1,0:T(8,128)S(1)}, u32[]{:S(2)}, u32[]{:S(2)}) collective-permute-start(f32[2,16,128]{2,1,0:T(8,128)S(1)} %get-tuple-element.32), channel_id=1, source_target_pairs={{0,1},{1,2},{2,3},{5,4},{6,5},{7,6},{8,9},{9,10},{10,11},{13,12},{... | collective-permute-start | bytes 49160 | tf_op jit(solution)/shard_map/ppermute | solution.py:309
  13.3 8.4 %collective-permute-start.2 = (f32[5,16,128]{2,1,0:T(8,128)S(1)}, f32[5,16,128]{2,1,0:T(8,128)S(1)}, u32[]{:S(2)}, u32[]{:S(2)}) collective-permute-start(f32[5,16,128]{2,1,0:T(8,128)S(1)} %get-tuple-element.33), channel_id=1, source_target_pairs={{4,8},{12,16},{20,24},{8,4},{16,12},{24,20},{5,9},{13,17},{21,25},... | collective-permute-start | bytes 122888 | tf_op jit(solution)/shard_map/ppermute | solution.py:310
  21.8 2.1 %all_gather.25.refs_5_ = f32[24,16,128]{2,1,0:T(8,128)S(1)} all-gather(f32[12,16,128]{2,1,0:T(8,128)S(1)} %shard_map.123), channel_id=1, replica_groups={{0,4},{8,12},{16,20},{24,28},{1,5},{9,13},{17,21},{25,29},{2,6},{10,14}..., dimensions={0}, use_global_device_ids=true | all-gather | bytes 294912 | tf_op jit(solution)/shard_map/all_gather | solution.py:312
  24.8 2.1 %all_gather.26.pair.refs_11_ = f32[22,16,128]{2,1,0:T(8,128)S(1)} all-gather(f32[11,16,128]{2,1,0:T(8,128)S(1)} %get-tuple-element.35), channel_id=1, replica_groups={{0,4},{8,12},{16,20},{24,28},{1,5},{9,13},{17,21},{25,29},{2,6},{10,14}..., dimensions={0}, use_global_device_ids=true | all-gather | bytes 270336 | tf_op jit(solution)/shard_map/all_gather | solution.py:298
  26.9 1.3 %collective-permute-start.3 = (f32[10,16,128]{2,1,0:T(8,128)S(1)}, f32[10,16,128]{2,1,0:T(8,128)S(1)}, u32[]{:S(2)}, u32[]{:S(2)}) collective-permute-start(f32[10,16,128]{2,1,0:T(8,128)S(1)} %get-tuple-element.37), channel_id=1, source_target_pairs={{0,32},{32,64},{64,96},{96,128},{128,160},{160,192},{192,224},{224... | collective-permute-start | bytes 245768 | tf_op jit(solution)/shard_map/ppermute | solution.py:308
  28.2 1.3 %collective-permute-start.4 = (f32[2,16,128]{2,1,0:T(8,128)S(1)}, f32[2,16,128]{2,1,0:T(8,128)S(1)}, u32[]{:S(2)}, u32[]{:S(2)}) collective-permute-start(f32[2,16,128]{2,1,0:T(8,128)S(1)} %get-tuple-element.38), channel_id=1, source_target_pairs={{0,1},{1,2},{2,3},{5,4},{6,5},{7,6},{8,9},{9,10},{10,11},{13,12},{... | collective-permute-start | bytes 49160 | tf_op jit(solution)/shard_map/ppermute | solution.py:309
  29.5 11.8 %collective-permute-start.5 = (f32[5,16,128]{2,1,0:T(8,128)S(1)}, f32[5,16,128]{2,1,0:T(8,128)S(1)}, u32[]{:S(2)}, u32[]{:S(2)}) collective-permute-start(f32[5,16,128]{2,1,0:T(8,128)S(1)} %get-tuple-element.39), channel_id=1, source_target_pairs={{4,8},{12,16},{20,24},{8,4},{16,12},{24,20},{5,9},{13,17},{21,25},... | collective-permute-start | bytes 122888 | tf_op jit(solution)/shard_map/ppermute | solution.py:310
  41.4 2.1 %all_gather.27.refs_12_ = f32[24,16,128]{2,1,0:T(8,128)S(1)} all-gather(f32[12,16,128]{2,1,0:T(8,128)S(1)} %shard_map.126), channel_id=1, replica_groups={{0,4},{8,12},{16,20},{24,28},{1,5},{9,13},{17,21},{25,29},{2,6},{10,14}..., dimensions={0}, use_global_device_ids=true | all-gather | bytes 294912 | tf_op jit(solution)/shard_map/all_gather | solution.py:312
  44.1 1.7 %shard_map.127 = (f32[6,16,16,128]{3,2,1,0:T(8,128)S(1)}, f32[6,16,16,128]{3,2,1,0:T(8,128)S(1)}, f32[11,16,128]{2,1,0:T(8,128)S(1)}, f32[11,16,128]{2,1,0:T(8,128)S(1)}) custom-call(s32[1]{0:T(128)} %bitcast.core.refs_0_, s32[1]{0:T(128)} %bitcast.1.refs_1_, f32[8]{0:T(128)S(1)} %copy-done.11, f32[3,16,16,128]{3,2,1,0:T(8,128)S(1)} %get-tuple-element.34.refs_3_.refs_2_, ...), custom_call_target="tpu_custom_call" | custom-call | tf_op jit(solution)/shard_map/pallas_call | solution.py:283
  45.8 1.9 %all_gather.28.pair.refs_4_ = f32[22,16,128]{2,1,0:T(8,128)S(1)} all-gather(f32[11,16,128]{2,1,0:T(8,128)S(1)} %get-tuple-element.41), channel_id=1, replica_groups={{0,4},{8,12},{16,20},{24,28},{1,5},{9,13},{17,21},{25,29},{2,6},{10,14}..., dimensions={0}, use_global_device_ids=true | all-gather | bytes 270336 | tf_op jit(solution)/shard_map/all_gather | solution.py:298
  47.8 1.3 %collective-permute-start.6 = (f32[10,16,128]{2,1,0:T(8,128)S(1)}, f32[10,16,128]{2,1,0:T(8,128)S(1)}, u32[]{:S(2)}, u32[]{:S(2)}) collective-permute-start(f32[10,16,128]{2,1,0:T(8,128)S(1)} %get-tuple-element.43), channel_id=1, source_target_pairs={{0,32},{32,64},{64,96},{96,128},{128,160},{160,192},{192,224},{224... | collective-permute-start | bytes 245768 | tf_op jit(solution)/shard_map/ppermute | solution.py:308
  49.1 1.3 %collective-permute-start.7 = (f32[2,16,128]{2,1,0:T(8,128)S(1)}, f32[2,16,128]{2,1,0:T(8,128)S(1)}, u32[]{:S(2)}, u32[]{:S(2)}) collective-permute-start(f32[2,16,128]{2,1,0:T(8,128)S(1)} %get-tuple-element.44), channel_id=1, source_target_pairs={{0,1},{1,2},{2,3},{5,4},{6,5},{7,6},{8,9},{9,10},{10,11},{13,12},{... | collective-permute-start | bytes 49160 | tf_op jit(solution)/shard_map/ppermute | solution.py:309
  50.4 9.9 %collective-permute-start.8 = (f32[5,16,128]{2,1,0:T(8,128)S(1)}, f32[5,16,128]{2,1,0:T(8,128)S(1)}, u32[]{:S(2)}, u32[]{:S(2)}) collective-permute-start(f32[5,16,128]{2,1,0:T(8,128)S(1)} %get-tuple-element.45), channel_id=1, source_target_pairs={{4,8},{12,16},{20,24},{8,4},{16,12},{24,20},{5,9},{13,17},{21,25},... | collective-permute-start | bytes 122888 | tf_op jit(solution)/shard_map/ppermute | solution.py:310
  60.3 1.9 %all_gather.29.refs_5_ = f32[24,16,128]{2,1,0:T(8,128)S(1)} all-gather(f32[12,16,128]{2,1,0:T(8,128)S(1)} %shard_map.129), channel_id=1, replica_groups={{0,4},{8,12},{16,20},{24,28},{1,5},{9,13},{17,21},{25,29},{2,6},{10,14}..., dimensions={0}, use_global_device_ids=true | all-gather | bytes 294912 | tf_op jit(solution)/shard_map/all_gather | solution.py:312
  62.3 1.7 %shard_map.130 = (f32[3,16,16,128]{3,2,1,0:T(8,128)}, f32[11,16,128]{2,1,0:T(8,128)S(1)}, f32[11,16,128]{2,1,0:T(8,128)S(1)}) custom-call(s32[1]{0:T(128)} %bitcast.core.refs_0_, f32[6,16,16,128]{3,2,1,0:T(8,128)S(1)} %get-tuple-element.40.refs_1_.refs_4_, f32[3,16,16,128]{3,2,1,0:T(8,128)S(1)} %get-tuple-element.34.refs_3_.refs_2_, ...), custom_call_target="tpu_custom_call" | custom-call | tf_op jit(solution)/shard_map/pallas_call | solution.py:283
  63.9 1.9 %all_gather.30.pair.refs_11_ = f32[22,16,128]{2,1,0:T(8,128)S(1)} all-gather(f32[11,16,128]{2,1,0:T(8,128)S(1)} %get-tuple-element.48), channel_id=1, replica_groups={{0,4},{8,12},{16,20},{24,28},{1,5},{9,13},{17,21},{25,29},{2,6},{10,14}..., dimensions={0}, use_global_device_ids=true | all-gather | bytes 270336 | tf_op jit(solution)/shard_map/all_gather | solution.py:298
  65.9 1.4 %collective-permute-start.9 = (f32[10,16,128]{2,1,0:T(8,128)S(1)}, f32[10,16,128]{2,1,0:T(8,128)S(1)}, u32[]{:S(2)}, u32[]{:S(2)}) collective-permute-start(f32[10,16,128]{2,1,0:T(8,128)S(1)} %get-tuple-element.50), channel_id=1, source_target_pairs={{0,32},{32,64},{64,96},{96,128},{128,160},{160,192},{192,224},{224... | collective-permute-start | bytes 245768 | tf_op jit(solution)/shard_map/ppermute | solution.py:308
  67.3 1.3 %collective-permute-start.10 = (f32[2,16,128]{2,1,0:T(8,128)S(1)}, f32[2,16,128]{2,1,0:T(8,128)S(1)}, u32[]{:S(2)}, u32[]{:S(2)}) collective-permute-start(f32[2,16,128]{2,1,0:T(8,128)S(1)} %get-tuple-element.51), channel_id=1, source_target_pairs={{0,1},{1,2},{2,3},{5,4},{6,5},{7,6},{8,9},{9,10},{10,11},{13,12},{... | collective-permute-start | bytes 49160 | tf_op jit(solution)/shard_map/ppermute | solution.py:309
  68.6 8.7 %collective-permute-start.11 = (f32[5,16,128]{2,1,0:T(8,128)S(1)}, f32[5,16,128]{2,1,0:T(8,128)S(1)}, u32[]{:S(2)}, u32[]{:S(2)}) collective-permute-start(f32[5,16,128]{2,1,0:T(8,128)S(1)} %get-tuple-element.52), channel_id=1, source_target_pairs={{4,8},{12,16},{20,24},{8,4},{16,12},{24,20},{5,9},{13,17},{21,25},... | collective-permute-start | bytes 122888 | tf_op jit(solution)/shard_map/ppermute | solution.py:310
  77.7 1.9 %all_gather.31.refs_12_ = f32[24,16,128]{2,1,0:T(8,128)S(1)} all-gather(f32[12,16,128]{2,1,0:T(8,128)S(1)} %shard_map.132), channel_id=1, replica_groups={{0,4},{8,12},{16,20},{24,28},{1,5},{9,13},{17,21},{25,29},{2,6},{10,14}..., dimensions={0}, use_global_device_ids=true | all-gather | bytes 294912 | tf_op jit(solution)/shard_map/all_gather | solution.py:312
  79.7 2.3 %shard_map.133 = (f32[6,16,16,128]{3,2,1,0:T(8,128)}, f32[6,16,16,128]{3,2,1,0:T(8,128)}) custom-call(s32[1]{0:T(128)} %bitcast.core.refs_0_, s32[1]{0:T(128)} %bitcast.1.refs_1_, f32[8]{0:T(128)S(1)} %copy-done.11, f32[3,16,16,128]{3,2,1,0:T(8,128)S(1)} %copy-done.9, f32[6,16,16,128]{3,2,1,0:T(8,128)S(1)} %get-tuple-element.40.refs_1_.refs_4_, ...), custom_call_target="tpu_custom_call" | custom-call | tf_op jit(solution)/shard_map/pallas_call | solution.py:283
  (45 shorter events, 2.4 us)
Async XLA Ops:
  0.6 1.1 %copy-start = (f32[6,16,16,128]{3,2,1,0:T(8,128)S(1)}, f32[6,16,16,128]{3,2,1,0:T(8,128)}, u32[]{:S(2)}) copy-start(f32[6,16,16,128]{3,2,1,0:T(8,128)} %refs_4_.1) | copy-start | bytes 2359300
  1.8 22.1 %copy-start.1 = (f32[6,16,16,128]{3,2,1,0:T(8,128)S(1)}, f32[6,16,16,128]{3,2,1,0:T(8,128)}, u32[]{:S(2)}) copy-start(f32[6,16,16,128]{3,2,1,0:T(8,128)} %refs_4_.1) | copy-start | bytes 2359300
  10.6 13.3 %copy-start.8 = (f32[3,16,16,128]{3,2,1,0:T(8,128)S(1)}, f32[3,16,16,128]{3,2,1,0:T(8,128)}, u32[]{:S(2)}) copy-start(f32[3,16,16,128]{3,2,1,0:T(8,128)} %refs_2_.3) | copy-start | bytes 1179652
  10.6 11.2 %collective-permute-start = (f32[10,16,128]{2,1,0:T(8,128)S(1)}, f32[10,16,128]{2,1,0:T(8,128)S(1)}, u32[]{:S(2)}, u32[]{:S(2)}) collective-permute-start(f32[10,16,128]{2,1,0:T(8,128)S(1)} %get-tuple-element.31), channel_id=1, source_target_pairs={{0,32},{32,64},{64,96},{96,128},{128,160},{160,192},{192,224},{224... | collective-permute-start | bytes 245768 | tf_op jit(solution)/shard_map/ppermute | solution.py:308
  12.0 9.7 %collective-permute-start.1 = (f32[2,16,128]{2,1,0:T(8,128)S(1)}, f32[2,16,128]{2,1,0:T(8,128)S(1)}, u32[]{:S(2)}, u32[]{:S(2)}) collective-permute-start(f32[2,16,128]{2,1,0:T(8,128)S(1)} %get-tuple-element.32), channel_id=1, source_target_pairs={{0,1},{1,2},{2,3},{5,4},{6,5},{7,6},{8,9},{9,10},{10,11},{13,12},{... | collective-permute-start | bytes 49160 | tf_op jit(solution)/shard_map/ppermute | solution.py:309
  13.3 10.5 %collective-permute-start.2 = (f32[5,16,128]{2,1,0:T(8,128)S(1)}, f32[5,16,128]{2,1,0:T(8,128)S(1)}, u32[]{:S(2)}, u32[]{:S(2)}) collective-permute-start(f32[5,16,128]{2,1,0:T(8,128)S(1)} %get-tuple-element.33), channel_id=1, source_target_pairs={{4,8},{12,16},{20,24},{8,4},{16,12},{24,20},{5,9},{13,17},{21,25},... | collective-permute-start | bytes 122888 | tf_op jit(solution)/shard_map/ppermute | solution.py:310
  21.8 2.1 %copy-start.3 = (f32[16,16,128]{2,1,0:T(8,128)S(1)}, f32[16,16,128]{2,1,0:T(8,128)}, u32[]{:S(2)}) copy-start(f32[16,16,128]{2,1,0:T(8,128)} %refs_3_.3) | copy-start | bytes 393220
  23.9 19.6 %copy-start.6 = (f32[16,16,128]{2,1,0:T(8,128)S(1)}, f32[16,16,128]{2,1,0:T(8,128)}, u32[]{:S(2)}) copy-start(f32[16,16,128]{2,1,0:T(8,128)} %refs_8_.3) | copy-start | bytes 393220
  23.9 19.5 %copy-start.7 = (s32[16,16,128]{2,1,0:T(8,128)S(1)}, s32[16,16,128]{2,1,0:T(8,128)}, u32[]{:S(2)}) copy-start(s32[16,16,128]{2,1,0:T(8,128)} %refs_9_.3) | copy-start | bytes 393220
  23.9 19.5 %copy-start.10 = (s32[16,16]{1,0:T(8,128)S(1)}, s32[16,16]{1,0:T(8,128)}, u32[]{:S(2)}) copy-start(s32[16,16]{1,0:T(8,128)} %refs_10_.3) | copy-start | bytes 3076
  24.8 18.7 %copy-start.2 = (f32[6,16,16,128]{3,2,1,0:T(8,128)S(1)}, f32[6,16,16,128]{3,2,1,0:T(8,128)}, u32[]{:S(2)}) copy-start(f32[6,16,16,128]{3,2,1,0:T(8,128)} %refs_5_.1) | copy-start | bytes 2359300
  26.9 14.4 %collective-permute-start.3 = (f32[10,16,128]{2,1,0:T(8,128)S(1)}, f32[10,16,128]{2,1,0:T(8,128)S(1)}, u32[]{:S(2)}, u32[]{:S(2)}) collective-permute-start(f32[10,16,128]{2,1,0:T(8,128)S(1)} %get-tuple-element.37), channel_id=1, source_target_pairs={{0,32},{32,64},{64,96},{96,128},{128,160},{160,192},{192,224},{224... | collective-permute-start | bytes 245768 | tf_op jit(solution)/shard_map/ppermute | solution.py:308
  28.2 13.1 %collective-permute-start.4 = (f32[2,16,128]{2,1,0:T(8,128)S(1)}, f32[2,16,128]{2,1,0:T(8,128)S(1)}, u32[]{:S(2)}, u32[]{:S(2)}) collective-permute-start(f32[2,16,128]{2,1,0:T(8,128)S(1)} %get-tuple-element.38), channel_id=1, source_target_pairs={{0,1},{1,2},{2,3},{5,4},{6,5},{7,6},{8,9},{9,10},{10,11},{13,12},{... | collective-permute-start | bytes 49160 | tf_op jit(solution)/shard_map/ppermute | solution.py:309
  29.5 13.9 %collective-permute-start.5 = (f32[5,16,128]{2,1,0:T(8,128)S(1)}, f32[5,16,128]{2,1,0:T(8,128)S(1)}, u32[]{:S(2)}, u32[]{:S(2)}) collective-permute-start(f32[5,16,128]{2,1,0:T(8,128)S(1)} %get-tuple-element.39), channel_id=1, source_target_pairs={{4,8},{12,16},{20,24},{8,4},{16,12},{24,20},{5,9},{13,17},{21,25},... | collective-permute-start | bytes 122888 | tf_op jit(solution)/shard_map/ppermute | solution.py:310
  41.3 2.1 %copy-start.4 = (f32[16,16,128]{2,1,0:T(8,128)S(1)}, f32[16,16,128]{2,1,0:T(8,128)}, u32[]{:S(2)}) copy-start(f32[16,16,128]{2,1,0:T(8,128)} %refs_6_.3) | copy-start | bytes 393220
  41.3 2.1 %copy-start.5 = (f32[16,16,128]{2,1,0:T(8,128)S(1)}, f32[16,16,128]{2,1,0:T(8,128)}, u32[]{:S(2)}) copy-start(f32[16,16,128]{2,1,0:T(8,128)} %refs_7_.3) | copy-start | bytes 393220
  43.4 0.7 copy-start.11
  47.8 12.5 %collective-permute-start.6 = (f32[10,16,128]{2,1,0:T(8,128)S(1)}, f32[10,16,128]{2,1,0:T(8,128)S(1)}, u32[]{:S(2)}, u32[]{:S(2)}) collective-permute-start(f32[10,16,128]{2,1,0:T(8,128)S(1)} %get-tuple-element.43), channel_id=1, source_target_pairs={{0,32},{32,64},{64,96},{96,128},{128,160},{160,192},{192,224},{224... | collective-permute-start | bytes 245768 | tf_op jit(solution)/shard_map/ppermute | solution.py:308
  49.1 11.2 %collective-permute-start.7 = (f32[2,16,128]{2,1,0:T(8,128)S(1)}, f32[2,16,128]{2,1,0:T(8,128)S(1)}, u32[]{:S(2)}, u32[]{:S(2)}) collective-permute-start(f32[2,16,128]{2,1,0:T(8,128)S(1)} %get-tuple-element.44), channel_id=1, source_target_pairs={{0,1},{1,2},{2,3},{5,4},{6,5},{7,6},{8,9},{9,10},{10,11},{13,12},{... | collective-permute-start | bytes 49160 | tf_op jit(solution)/shard_map/ppermute | solution.py:309
  50.4 11.9 %collective-permute-start.8 = (f32[5,16,128]{2,1,0:T(8,128)S(1)}, f32[5,16,128]{2,1,0:T(8,128)S(1)}, u32[]{:S(2)}, u32[]{:S(2)}) collective-permute-start(f32[5,16,128]{2,1,0:T(8,128)S(1)} %get-tuple-element.45), channel_id=1, source_target_pairs={{4,8},{12,16},{20,24},{8,4},{16,12},{24,20},{5,9},{13,17},{21,25},... | collective-permute-start | bytes 122888 | tf_op jit(solution)/shard_map/ppermute | solution.py:310
  65.8 13.8 %copy-start.9 = (f32[3,16,16,128]{3,2,1,0:T(8,128)S(1)}, f32[3,16,16,128]{3,2,1,0:T(8,128)}, u32[]{:S(2)}) copy-start(f32[3,16,16,128]{3,2,1,0:T(8,128)} %get-tuple-element.26.refs_3_) | copy-start | bytes 1179652
  65.9 11.9 %collective-permute-start.9 = (f32[10,16,128]{2,1,0:T(8,128)S(1)}, f32[10,16,128]{2,1,0:T(8,128)S(1)}, u32[]{:S(2)}, u32[]{:S(2)}) collective-permute-start(f32[10,16,128]{2,1,0:T(8,128)S(1)} %get-tuple-element.50), channel_id=1, source_target_pairs={{0,32},{32,64},{64,96},{96,128},{128,160},{160,192},{192,224},{224... | collective-permute-start | bytes 245768 | tf_op jit(solution)/shard_map/ppermute | solution.py:308
  67.3 10.0 %collective-permute-start.10 = (f32[2,16,128]{2,1,0:T(8,128)S(1)}, f32[2,16,128]{2,1,0:T(8,128)S(1)}, u32[]{:S(2)}, u32[]{:S(2)}) collective-permute-start(f32[2,16,128]{2,1,0:T(8,128)S(1)} %get-tuple-element.51), channel_id=1, source_target_pairs={{0,1},{1,2},{2,3},{5,4},{6,5},{7,6},{8,9},{9,10},{10,11},{13,12},{... | collective-permute-start | bytes 49160 | tf_op jit(solution)/shard_map/ppermute | solution.py:309
  68.6 11.1 %collective-permute-start.11 = (f32[5,16,128]{2,1,0:T(8,128)S(1)}, f32[5,16,128]{2,1,0:T(8,128)S(1)}, u32[]{:S(2)}, u32[]{:S(2)}) collective-permute-start(f32[5,16,128]{2,1,0:T(8,128)S(1)} %get-tuple-element.52), channel_id=1, source_target_pairs={{4,8},{12,16},{20,24},{8,4},{16,12},{24,20},{5,9},{13,17},{21,25},... | collective-permute-start | bytes 122888 | tf_op jit(solution)/shard_map/ppermute | solution.py:310

commit v6 on v5

v6 whole, which is shorter than its diff:
```python
import functools

import jax
import jax.numpy as jnp
from jax import lax
from jax.experimental import pallas as pl
from jax.experimental.pallas import tpu as pltpu
from jax.sharding import PartitionSpec as P

STEPS = 2
COEF_NEAR = 9.0 / 8.0
COEF_FAR = -1.0 / 24.0
TIME_STEP = 0.2
AXES = ("gx", "gy", "gz")

STRESS = (
    ((0, "f"), (3, "b"), (4, "b")),
    ((3, "b"), (1, "f"), (5, "b")),
    ((4, "b"), (5, "b"), (2, "f")),
)
VELOCITY = (
    ((0, "b"), (1, "f"), (2, "f")),
    ((1, "b"), (0, "f"), (2, "f")),
    ((2, "b"), (0, "f"), (1, "f")),
)
BEFORE = {"f": (-1,), "b": (-2, -1)}
AFTER = {"f": (0, 1), "b": (0,)}
TAPS = {
    "f": ((1, COEF_NEAR), (0, -COEF_NEAR), (2, COEF_FAR), (-1, -COEF_FAR)),
    "b": ((0, COEF_NEAR), (-1, -COEF_NEAR), (1, COEF_FAR), (-2, -COEF_FAR)),
}

GROUPS = 4
FACE = 5
INNER = FACE + 1
GIVEN = INNER + FACE
TAKEN = 2 * FACE + 2


def layers(spec, sides):
    return [(comp, off) for comp, kind in spec for off in sides[kind]]


def weighted(taps):
    a, b, c, d = taps
    return COEF_NEAR * (a - b) + COEF_FAR * (c - d)


def thirds(value):
    high = value.astype(jnp.bfloat16)
    rest = value - high.astype(jnp.float32)
    middle = rest.astype(jnp.bfloat16)
    return high, middle, (rest - middle.astype(jnp.float32)).astype(jnp.bfloat16)


class Near:
    def __init__(self, spec, fields, core, pair, outer, rows):
        self.spec, self.fields, self.rows = spec, fields, rows
        self.nx, self.ny, self.nz = nx, ny, nz = fields.shape[1:]
        first = {k: i for i, k in enumerate(layers(spec[1], BEFORE))}
        last = {k: i for i, k in enumerate(layers(spec[1], AFTER))}
        for slot, (comp, kind) in enumerate(spec[1]):
            for x in range(nx):
                rows[slot, x, 8 : 8 + ny, :] = fields[comp, x]

        def beside(before, after):
            for slot, (comp, kind) in enumerate(spec[1]):
                for x in range(nx):
                    for off in BEFORE[kind]:
                        rows[slot, x, 8 + off : 9 + off, :] = before(first[comp, off], x)
                    for off in AFTER[kind]:
                        rows[slot, x, 8 + ny + off : 9 + ny + off, :] = after(last[comp, off], x)

        beyond = lambda i, x: outer[i, x : x + 1, :]

        @pl.when(core == 0)
        def _():
            beside(beyond, lambda i, x: pair[GIVEN + INNER + i, x : x + 1, :])

        @pl.when(core == 1)
        def _():
            beside(lambda i, x: pair[INNER + i, x : x + 1, :], beyond)

    def dx(self, comp, x):
        taps = TAPS[dict(self.spec[0])[comp]]
        if all(0 <= x + off < self.nx for off, _ in taps):
            return weighted([self.fields[comp, x + off] for off, _ in taps])
        return sum(w * self.fields[comp, x + off] for off, w in taps if 0 <= x + off < self.nx)

    def dy(self, comp, x):
        slot = [c for c, _ in self.spec[1]].index(comp)
        kind = self.spec[1][slot][1]
        return weighted(
            [self.rows[slot, x, 8 + off : 8 + off + self.ny, :] for off, _ in TAPS[kind]]
        )

    def dz(self, comp, x):
        here = self.fields[comp, x]
        lane = lax.broadcasted_iota(jnp.int32, (1, self.nz), 1)
        total = None
        for off, weight in TAPS[dict(self.spec[2])[comp]]:
            if off == 0:
                term = weight * here
            else:
                inside = (lane + off >= 0) & (lane + off < self.nz)
                term = jnp.where(inside, weight, 0.0) * pltpu.roll(here, (-off) % self.nz, 1)
            total = term if total is None else total + term
        return total


class Far:
    def __init__(self, spec, shape, core, spread, edges):
        self.spec, self.core, self.spread, self.edges = spec, core, spread, edges
        self.nx, self.ny, self.nz = nx, ny, nz = shape
        self.before = [{k: i for i, k in enumerate(layers(s, BEFORE))} for s in spec]
        self.after = [{k: i for i, k in enumerate(layers(s, AFTER))} for s in spec]
        ends = [spread[side * TAKEN + 2 * FACE + core] for side in (0, 1)]
        got = jnp.concatenate([jnp.concatenate([e[:8], e[8:]], axis=1) for e in ends], axis=0)
        row = lax.broadcasted_iota(jnp.int32, (16, nz), 0)
        lane = lax.broadcasted_iota(jnp.int32, (16, nz), 1)
        weights = []
        for comp, kind in spec[2]:
            here = jnp.zeros((16, nz), jnp.float32)
            for shift, weight in TAPS[kind]:
                scaled = float(round(24 * weight))
                places = [(self.before[2][comp, off], off - shift) for off in BEFORE[kind]]
                places += [(8 + self.after[2][comp, off], nz + off - shift) for off in AFTER[kind]]
                for i, at in places:
                    if 0 <= at < nz:
                        here = jnp.where((row == i) & (lane == at), scaled, here)
            weights.append(here)
        weights = jnp.concatenate(weights, axis=1).astype(jnp.bfloat16)
        weights = jnp.concatenate([weights] * 3, axis=0)
        stacked = jnp.concatenate([p.astype(jnp.float32) for p in thirds(got)], axis=0).T
        total = jnp.dot(stacked.astype(jnp.bfloat16), weights, preferred_element_type=jnp.float32)
        for slot in range(3):
            edges[slot] = total[:, slot * nz : (slot + 1) * nz] * (1.0 / 24.0)

    def dx(self, comp, x):
        total = 0.0
        for off, weight in TAPS[dict(self.spec[0])[comp]]:
            at = x + off
            if at < 0:
                here = self.spread[self.core * FACE + self.before[0][comp, at]]
                total = total + weight * here
            elif at >= self.nx:
                i = self.after[0][comp, at - self.nx]
                total = total + weight * self.spread[TAKEN + self.core * FACE + i]
        return total

    def dz(self, comp, x):
        slot = [c for c, _ in self.spec[2]].index(comp)
        return self.edges[slot, x * self.ny : (x + 1) * self.ny, :]


def pack(spec, fields, core, own, given):
    nx, ny, nz = fields.shape[1:]
    row = lax.broadcasted_iota(jnp.int32, (16, nz), 0)
    lane = lax.broadcasted_iota(jnp.int32, (16, nz), 1)
    before, after = layers(spec[2], BEFORE), layers(spec[2], AFTER)
    total = None
    for comp, _ in spec[2]:
        pick = jnp.zeros((16, nz), jnp.float32)
        for i, (c, off) in enumerate(before):
            if c == comp:
                pick = jnp.where((row == i) & (lane == nz + off), 1.0, pick)
        for i, (c, off) in enumerate(after):
            if c == comp:
                pick = jnp.where((row == 8 + i) & (lane == off), 1.0, pick)
        pick = pick.astype(jnp.bfloat16)
        for third in thirds(fields[comp].reshape(nx * ny, nz)):
            part = lax.dot_general(
                pick, third, (((1,), (1,)), ((), ())), preferred_element_type=jnp.float32
            )
            total = part if total is None else total + part
    half = nx * ny // 2
    ends = [jnp.concatenate([t[:, :half], t[:, half:]], axis=0) for t in (total[:8], total[8:])]

    def write(up, down, inner_up):
        for ref, sides in ((up, BEFORE), (down, AFTER)):
            for i, (comp, off) in enumerate(layers(spec[0], sides)):
                ref[i] = fields[comp, nx + off if sides is BEFORE else off]
        up[FACE] = ends[0]
        down[FACE] = ends[1]
        inner, outer = (BEFORE, AFTER) if inner_up else (AFTER, BEFORE)
        for ref, sides in ((given, inner), (own, outer)):
            for i, (comp, off) in enumerate(layers(spec[1], sides)):
                ref[INNER + i] = fields[comp, :, ny + off if sides is BEFORE else off, :]

    @pl.when(core == 0)
    def _():
        write(own, given, True)

    @pl.when(core == 1)
    def _():
        write(given, own, False)


def first_kernel(core, stress, own, given):
    pack(STRESS, stress, core[0], own, given)


def gather_kernel(core, own, pair, along_x, along_y, along_z):
    here = core[0]
    there = 1 - here
    other = there * GIVEN
    along_x[pl.ds(here * FACE, FACE)] = own[:FACE]
    along_x[pl.ds(there * FACE, FACE)] = pair[pl.ds(other, FACE)]
    along_z[here] = own[FACE]
    along_z[there] = pair[other + FACE]
    along_y[...] = own[INNER:]


def join_kernel(along_x, along_z, near, taken):
    taken[: 2 * FACE] = along_x[...]
    taken[2 * FACE :] = along_z[...]


def cells_kernel(first, table, mech, weight, top, behind, decay, gain, limits):
    limits[...] = (top[...] - first[0]).astype(jnp.float32).T
    for x in range(mech.shape[0]):
        here = jnp.zeros(mech.shape[1:], jnp.float32)
        for level in range(table.shape[0]):
            here = jnp.where(mech[x] == level, table[level], here)
        decay[x] = here
        gain[x] = (1.0 - here) * weight[x]


def near_velocity_kernel(core, stress, velocity, buoyancy, pair, outer, behind, out, rows):
    near = Near(STRESS, stress, core[0], pair, outer, rows)
    for x in range(velocity.shape[1]):
        scale = TIME_STEP * buoyancy[x]
        out[0, x] = velocity[0, x] + scale * (near.dx(0, x) + near.dy(3, x) + near.dz(4, x))
        out[1, x] = velocity[1, x] + scale * (near.dx(3, x) + near.dy(1, x) + near.dz(5, x))
        out[2, x] = velocity[2, x] + scale * (near.dx(4, x) + near.dy(5, x) + near.dz(2, x))


def velocity_kernel(core, near, buoyancy, spread, out, own, given, edges):
    far = Far(STRESS, near.shape[1:], core[0], spread, edges)
    for x in range(near.shape[1]):
        scale = TIME_STEP * buoyancy[x]
        out[0, x] = near[0, x] + scale * (far.dx(0, x) + far.dz(4, x))
        out[1, x] = near[1, x] + scale * (far.dx(3, x) + far.dz(5, x))
        out[2, x] = near[2, x] + scale * (far.dx(4, x) + far.dz(2, x))
    pack(VELOCITY, out, core[0], own, given)


def near_strain_kernel(core, velocity, pair, outer, behind, out, rows):
    near = Near(VELOCITY, velocity, core[0], pair, outer, rows)
    for x in range(velocity.shape[1]):
        out[0, x] = near.dx(0, x)
        out[1, x] = near.dy(1, x)
        out[2, x] = near.dz(2, x)
        out[3, x] = near.dy(0, x) + near.dx(1, x)
        out[4, x] = near.dz(0, x) + near.dx(2, x)
        out[5, x] = near.dz(1, x) + near.dy(2, x)


def stress_kernel(send, core, near, stress, memory, lam, shear, decay, gain, limits, *refs):
    if send:
        spread, out, kept, own, given, edges = refs
    else:
        spread, *finals, out, kept, sems, edges = refs
    nx, ny, nz = lam.shape
    far = Far(VELOCITY, lam.shape, core[0], spread, edges)
    depth = lax.broadcasted_iota(jnp.int32, (1, nz), 1).astype(jnp.float32)
    copies = []
    for x in range(nx):
        top = limits[:, x : x + 1]
        solid = depth >= top
        below = depth > top
        xx, yy, zz = near[0, x] + far.dx(0, x), near[1, x], near[2, x] + far.dz(2, x)
        volume = lam[x] * (xx + yy + zz)
        double = 2.0 * shear[x]
        rates = (
            volume + double * xx,
            volume + double * yy,
            volume + double * zz,
            shear[x] * (near[3, x] + far.dx(1, x)),
            shear[x] * (near[4, x] + far.dz(0, x) + far.dx(2, x)),
            shear[x] * (near[5, x] + far.dz(1, x)),
        )
        for comp, rate in enumerate(rates):
            new = decay[x] * memory[comp, x] + gain[x] * rate
            kept[comp, x] = new
            keep = below if comp in (2, 4, 5) else solid
            out[comp, x] = jnp.where(keep, stress[comp, x] + TIME_STEP * (rate - new), 0.0)
        size = nx // GROUPS
        if not send and (x + 1) % size == 0:
            part = pl.ds(x + 1 - size, size)
            for i, (held, final) in enumerate(zip((out, kept), finals)):
                copy = pltpu.make_async_copy(
                    held.at[:, part], final.at[:, part], sems.at[i, x // size]
                )
                copy.start()
                copies.append(copy)
    for copy in copies:
        copy.wait()
    if send:
        pack(STRESS, out, core[0], own, given)


def call(body, outs, operands, scalars=1, scratch=(), hold=False, out_space=pltpu.VMEM):
    vmem = pl.BlockSpec(memory_space=pltpu.VMEM)
    specs = [pl.BlockSpec(memory_space=pltpu.SMEM)] * scalars
    specs += [vmem] * (len(operands) - scalars)
    if hold:
        specs[-1] = pl.BlockSpec(memory_space=pl.ANY)
    return pl.pallas_call(
        body,
        out_shape=outs,
        in_specs=specs,
        out_specs=[pl.BlockSpec(memory_space=out_space)] * len(outs),
        scratch_shapes=list(scratch),
        cost_estimate=pl.CostEstimate(flops=2**22, bytes_accessed=2**22, transcendentals=0)
        if hold
        else None,
        compiler_params=pltpu.CompilerParams(vmem_limit_bytes=24 * 1024 * 1024),
    )(*operands)


def exchange(core, own, given, near_kernel):
    plane = own.shape[1:]
    planes = lambda n: jax.ShapeDtypeStruct((n,) + plane, own.dtype)
    gx, gy, gz = [lax.axis_size(axis) for axis in AXES]
    cores = [[j, j + 1] for j in range(0, gy, 2)]
    pair = lax.all_gather(given, "gy", axis=0, tiled=True, axis_index_groups=cores)
    along_x, along_y, along_z = call(
        gather_kernel, [planes(2 * FACE), planes(FACE), planes(2)], [core, own, pair]
    )
    to_x, to_z = [], []
    for j in range(gy):
        step = 1 - 2 * (j % 2)
        to_x += [(i * gy + j, (i + step) * gy + j) for i in range(gx) if 0 <= i + step < gx]
        to_z += [(j * gz + k, j * gz + k + step) for k in range(gz) if 0 <= k + step < gz]
    to_y = [(j, j + 1) for j in range(1, gy - 1, 2)] + [(j + 1, j) for j in range(1, gy - 1, 2)]
    got_x = lax.ppermute(along_x, ("gx", "gy"), to_x)
    got_z = lax.ppermute(along_z, ("gy", "gz"), to_z)
    outer = lax.ppermute(along_y, "gy", to_y)
    near = near_kernel(pair, outer, along_x)
    (taken,) = call(join_kernel, [planes(TAKEN)], [got_x, got_z, near], scalars=0, hold=True)
    spread = lax.all_gather(taken, "gy", axis=0, tiled=True, axis_index_groups=cores)
    return near, spread, along_x


def shards(
    velocity,
    stress,
    memory,
    lame_lambda,
    shear_modulus,
    buoyancy,
    anelastic_weight,
    decay_table,
    mech_index,
    surface_depth,
):
    nx, ny, nz = lame_lambda.shape
    core = (lax.axis_index("gy") % 2).astype(jnp.int32).reshape(1)
    first = (lax.axis_index("gz") * nz).astype(jnp.int32).reshape(1)
    like = lambda a: jax.ShapeDtypeStruct(a.shape, jnp.float32)
    packed = [jax.ShapeDtypeStruct((GIVEN, ny, nz), jnp.float32)] * 2
    rows = [pltpu.VMEM((3, nx, ny + 16, nz), jnp.float32)]
    edges = [pltpu.VMEM((3, nx * ny, nz), jnp.float32)]
    held = [
        pltpu.VMEM(stress.shape, jnp.float32),
        pltpu.VMEM(memory.shape, jnp.float32),
        pltpu.SemaphoreType.DMA((2, GROUPS)),
    ]
    own, given = call(first_kernel, packed, [core, stress])
    for step in range(STEPS):

        def near_velocity(*got):
            operands = [core, stress, velocity, buoyancy, *got]
            outs = [like(velocity)]
            return call(near_velocity_kernel, outs, operands, scratch=rows, hold=True)[0]

        def near_strain(*got):
            outs = [like(stress)]
            return call(near_strain_kernel, outs, [core, velocity, *got], scratch=rows, hold=True)[0]

        near, spread, along = exchange(core, own, given, near_velocity)
        if step == 0:
            cells = call(
                cells_kernel,
                [like(lame_lambda)] * 2 + [like(surface_depth)],
                [first, decay_table, mech_index, anelastic_weight, surface_depth, along],
                scalars=2,
                hold=True,
            )
        velocity, own, given = call(
            velocity_kernel,
            [like(velocity)] + packed,
            [core, near, buoyancy, spread],
            scratch=edges,
        )
        near, spread, _ = exchange(core, own, given, near_strain)
        send = step < STEPS - 1
        stress, memory, *rest = call(
            functools.partial(stress_kernel, send),
            [like(stress), like(memory)] + (packed if send else []),
            [core, near, stress, memory, lame_lambda, shear_modulus, *cells, spread],
            scratch=edges if send else held + edges,
            out_space=pltpu.VMEM if send else pl.ANY,
        )
        if send:
            own, given = rest
    return (velocity, stress, memory)


def solution(mesh):
    fields = P(None, *AXES)
    cells = P(*AXES)
    return jax.shard_map(
        shards,
        mesh=mesh,
        in_specs=(fields,) * 3 + (cells,) * 4 + (P(), cells, P("gx", "gy")),
        out_specs=(fields,) * 3,
        check_vma=False,
    )
```

time: 83.3 us -> 83 us (level)
  starting transfers between devices: 49.4 us -> 40.2 us
  waiting for transfers between devices: 0.43 us -> 9.57 us
    ppermute x4, starting transfers between devices: 38.8 us -> 29.6 us  [exchange(): outer = lax.ppermute(along_y, 'gy', to_y)]
    ppermute x4, waiting for transfers between devices: 0.01 us -> 8.45 us  [exchange(): got_z = lax.ppermute(along_z, ('gy', 'gz'), to_z)]
    ppermute x4, waiting for transfers between devices: 0.01 us -> 1.12 us  [exchange(): outer = lax.ppermute(along_y, 'gy', to_y)]
    pallas_call x13 -> x18, Pallas kernels: 6.96 us -> 7.45 us  [call(): pl.pallas_call(body, out_shape=outs, in_specs=specs, out_specs=[pl.BlockS...]
  transfers between devices with their start and end apart: 12 -> 12, of which waited for: 1 -> 7; matrix products, arithmetic and copies ran while one was open for 0% -> 0% of each run, Pallas kernels for 0% -> 3%
where the time goes in v6:
time: 83 us; the launch traced here: 82.4 us
  starting transfers between devices  40.2 us (48%)
  blocking collectives  22.4 us (27%)
  waiting for transfers between devices  9.57 us (12%)
  Pallas kernels  7.45 us (9%)
  local copies, waits for them, and re-layouts  1.8 us (2%)
  between operations  0.94 us (1%)
    ppermute x4, starting transfers between devices, exchange(): outer = lax.ppermute(along_y, 'gy', to_y)  29.6 us
    all_gather x4, blocking collectives, exchange(): lax.all_gather(given, 'gy', axis=0, tiled=True, axis_index_groups=cores)  14.5 us
    ppermute x4, waiting for transfers between devices, exchange(): got_z = lax.ppermute(along_z, ('gy', 'gz'), to_z)  8.45 us
    all_gather x4, blocking collectives, exchange(): lax.all_gather(taken, 'gy', axis=0, tiled=True, axis_index_groups=cores)  7.92 us
    pallas_call x18, Pallas kernels, call(): pl.pallas_call(body, out_shape=outs, in_specs=specs, out_specs=[pl.BlockS...  7.45 us
    ppermute x4, starting transfers between devices, exchange(): got_x = lax.ppermute(along_x, ('gx', 'gy'), to_x)  5.43 us
    ppermute x4, starting transfers between devices, exchange(): got_z = lax.ppermute(along_z, ('gy', 'gz'), to_z)  5.17 us
    unnamed x24, local copies, waits for them, and re-layouts  1.8 us
  transfers between devices with their start and end apart: 12, of which 7 were waited for; matrix products, arithmetic and copies ran while one was open for 0% of the time, Pallas kernels for 3%

profile of v6, /device:TPU:1, one launch (start us, length us, event | category | flops | bytes accessed | tf_op | source)
XLA Modules:
  0.0 82.4 jit_solution(16239319622888831474)
XLA Ops:
  2.1 8.6 %all_gather.24.pair = f32[22,16,128]{2,1,0:T(8,128)S(1)} all-gather(f32[11,16,128]{2,1,0:T(8,128)S(1)} %get-tuple-element.32), channel_id=1, replica_groups={{0,4},{8,12},{16,20},{24,28},{1,5},{9,13},{17,21},{25,29},{2,6},{10,14}..., dimensions={0}, use_global_device_ids=true | all-gather | bytes 270336 | tf_op jit(solution)/shard_map/all_gather | solution.py:327
  10.7 1.4 %collective-permute-start.1 = (f32[10,16,128]{2,1,0:T(8,128)S(1)}, f32[10,16,128]{2,1,0:T(8,128)S(1)}, u32[]{:S(2)}, u32[]{:S(2)}) collective-permute-start(f32[10,16,128]{2,1,0:T(8,128)S(1)} %get-tuple-element.35.behind), channel_id=1, source_target_pairs={{0,32},{32,64},{64,96},{96,128},{128,160},{160,192},{192,224},{224... | collective-permute-start | bytes 245768 | tf_op jit(solution)/shard_map/ppermute | solution.py:337
  12.2 5.9 %collective-permute-start = (f32[5,16,128]{2,1,0:T(8,128)S(1)}, f32[5,16,128]{2,1,0:T(8,128)S(1)}, u32[]{:S(2)}, u32[]{:S(2)}) collective-permute-start(f32[5,16,128]{2,1,0:T(8,128)S(1)} %get-tuple-element.34), channel_id=1, source_target_pairs={{4,8},{12,16},{20,24},{8,4},{16,12},{24,20},{5,9},{13,17},{21,25},... | collective-permute-start | bytes 122888 | tf_op jit(solution)/shard_map/ppermute | solution.py:339
  18.0 1.3 %collective-permute-start.2 = (f32[2,16,128]{2,1,0:T(8,128)S(1)}, f32[2,16,128]{2,1,0:T(8,128)S(1)}, u32[]{:S(2)}, u32[]{:S(2)}) collective-permute-start(f32[2,16,128]{2,1,0:T(8,128)S(1)} %get-tuple-element.36), channel_id=1, source_target_pairs={{0,1},{1,2},{2,3},{5,4},{6,5},{7,6},{8,9},{9,10},{10,11},{13,12},{... | collective-permute-start | bytes 49160 | tf_op jit(solution)/shard_map/ppermute | solution.py:338
  20.2 2.5 %collective-permute-done.2.along_z = f32[2,16,128]{2,1,0:T(8,128)S(1)} collective-permute-done((f32[2,16,128]{2,1,0:T(8,128)S(1)}, f32[2,16,128]{2,1,0:T(8,128)S(1)}, u32[]{:S(2)}, u32[]{:S(2)}) %collective-permute-start.2) | collective-permute-done | bytes 16416 | tf_op jit(solution)/shard_map/ppermute | solution.py:338
  22.7 1.9 %all_gather.25.spread = f32[24,16,128]{2,1,0:T(8,128)S(1)} all-gather(f32[12,16,128]{2,1,0:T(8,128)S(1)} %shard_map.124), channel_id=1, replica_groups={{0,4},{8,12},{16,20},{24,28},{1,5},{9,13},{17,21},{25,29},{2,6},{10,14}..., dimensions={0}, use_global_device_ids=true | all-gather | bytes 294912 | tf_op jit(solution)/shard_map/all_gather | solution.py:342
  25.3 1.9 %all_gather.26.pair = f32[22,16,128]{2,1,0:T(8,128)S(1)} all-gather(f32[11,16,128]{2,1,0:T(8,128)S(1)} %get-tuple-element.38), channel_id=1, replica_groups={{0,4},{8,12},{16,20},{24,28},{1,5},{9,13},{17,21},{25,29},{2,6},{10,14}..., dimensions={0}, use_global_device_ids=true | all-gather | bytes 270336 | tf_op jit(solution)/shard_map/all_gather | solution.py:327
  27.2 1.4 %collective-permute-start.4 = (f32[10,16,128]{2,1,0:T(8,128)S(1)}, f32[10,16,128]{2,1,0:T(8,128)S(1)}, u32[]{:S(2)}, u32[]{:S(2)}) collective-permute-start(f32[10,16,128]{2,1,0:T(8,128)S(1)} %get-tuple-element.41.behind), channel_id=1, source_target_pairs={{0,32},{32,64},{64,96},{96,128},{128,160},{160,192},{192,224},{224... | collective-permute-start | bytes 245768 | tf_op jit(solution)/shard_map/ppermute | solution.py:337
  28.7 10.9 %collective-permute-start.3 = (f32[5,16,128]{2,1,0:T(8,128)S(1)}, f32[5,16,128]{2,1,0:T(8,128)S(1)}, u32[]{:S(2)}, u32[]{:S(2)}) collective-permute-start(f32[5,16,128]{2,1,0:T(8,128)S(1)} %get-tuple-element.40), channel_id=1, source_target_pairs={{4,8},{12,16},{20,24},{8,4},{16,12},{24,20},{5,9},{13,17},{21,25},... | collective-permute-start | bytes 122888 | tf_op jit(solution)/shard_map/ppermute | solution.py:339
  39.6 1.3 %collective-permute-start.5 = (f32[2,16,128]{2,1,0:T(8,128)S(1)}, f32[2,16,128]{2,1,0:T(8,128)S(1)}, u32[]{:S(2)}, u32[]{:S(2)}) collective-permute-start(f32[2,16,128]{2,1,0:T(8,128)S(1)} %get-tuple-element.45), channel_id=1, source_target_pairs={{0,1},{1,2},{2,3},{5,4},{6,5},{7,6},{8,9},{9,10},{10,11},{13,12},{... | collective-permute-start | bytes 49160 | tf_op jit(solution)/shard_map/ppermute | solution.py:338
  42.7 1.4 %collective-permute-done.5.along_z = f32[2,16,128]{2,1,0:T(8,128)S(1)} collective-permute-done((f32[2,16,128]{2,1,0:T(8,128)S(1)}, f32[2,16,128]{2,1,0:T(8,128)S(1)}, u32[]{:S(2)}, u32[]{:S(2)}) %collective-permute-start.5) | collective-permute-done | bytes 16416 | tf_op jit(solution)/shard_map/ppermute | solution.py:338
  44.1 2.1 %all_gather.27.refs_0_ = f32[24,16,128]{2,1,0:T(8,128)S(1)} all-gather(f32[12,16,128]{2,1,0:T(8,128)S(1)} %shard_map.129), channel_id=1, replica_groups={{0,4},{8,12},{16,20},{24,28},{1,5},{9,13},{17,21},{25,29},{2,6},{10,14}..., dimensions={0}, use_global_device_ids=true | all-gather | bytes 294912 | tf_op jit(solution)/shard_map/all_gather | solution.py:342
  47.0 1.9 %all_gather.28.pair = f32[22,16,128]{2,1,0:T(8,128)S(1)} all-gather(f32[11,16,128]{2,1,0:T(8,128)S(1)} %get-tuple-element.47), channel_id=1, replica_groups={{0,4},{8,12},{16,20},{24,28},{1,5},{9,13},{17,21},{25,29},{2,6},{10,14}..., dimensions={0}, use_global_device_ids=true | all-gather | bytes 270336 | tf_op jit(solution)/shard_map/all_gather | solution.py:327
  49.0 1.3 %collective-permute-start.7 = (f32[10,16,128]{2,1,0:T(8,128)S(1)}, f32[10,16,128]{2,1,0:T(8,128)S(1)}, u32[]{:S(2)}, u32[]{:S(2)}) collective-permute-start(f32[10,16,128]{2,1,0:T(8,128)S(1)} %get-tuple-element.50.behind), channel_id=1, source_target_pairs={{0,32},{32,64},{64,96},{96,128},{128,160},{160,192},{192,224},{224... | collective-permute-start | bytes 245768 | tf_op jit(solution)/shard_map/ppermute | solution.py:337
  50.3 6.3 %collective-permute-start.6 = (f32[5,16,128]{2,1,0:T(8,128)S(1)}, f32[5,16,128]{2,1,0:T(8,128)S(1)}, u32[]{:S(2)}, u32[]{:S(2)}) collective-permute-start(f32[5,16,128]{2,1,0:T(8,128)S(1)} %get-tuple-element.49), channel_id=1, source_target_pairs={{4,8},{12,16},{20,24},{8,4},{16,12},{24,20},{5,9},{13,17},{21,25},... | collective-permute-start | bytes 122888 | tf_op jit(solution)/shard_map/ppermute | solution.py:339
  56.6 1.3 %collective-permute-start.8 = (f32[2,16,128]{2,1,0:T(8,128)S(1)}, f32[2,16,128]{2,1,0:T(8,128)S(1)}, u32[]{:S(2)}, u32[]{:S(2)}) collective-permute-start(f32[2,16,128]{2,1,0:T(8,128)S(1)} %get-tuple-element.51), channel_id=1, source_target_pairs={{0,1},{1,2},{2,3},{5,4},{6,5},{7,6},{8,9},{9,10},{10,11},{13,12},{... | collective-permute-start | bytes 49160 | tf_op jit(solution)/shard_map/ppermute | solution.py:338
  58.8 2.3 %collective-permute-done.8.along_z = f32[2,16,128]{2,1,0:T(8,128)S(1)} collective-permute-done((f32[2,16,128]{2,1,0:T(8,128)S(1)}, f32[2,16,128]{2,1,0:T(8,128)S(1)}, u32[]{:S(2)}, u32[]{:S(2)}) %collective-permute-start.8) | collective-permute-done | bytes 16416 | tf_op jit(solution)/shard_map/ppermute | solution.py:338
  61.1 1.9 %all_gather.29.spread = f32[24,16,128]{2,1,0:T(8,128)S(1)} all-gather(f32[12,16,128]{2,1,0:T(8,128)S(1)} %shard_map.133), channel_id=1, replica_groups={{0,4},{8,12},{16,20},{24,28},{1,5},{9,13},{17,21},{25,29},{2,6},{10,14}..., dimensions={0}, use_global_device_ids=true | all-gather | bytes 294912 | tf_op jit(solution)/shard_map/all_gather | solution.py:342
  63.0 1.3 %shard_map.134 = (f32[3,16,16,128]{3,2,1,0:T(8,128)}, f32[11,16,128]{2,1,0:T(8,128)S(1)}, f32[11,16,128]{2,1,0:T(8,128)S(1)}) custom-call(s32[1]{0:T(128)} %bitcast.core, f32[3,16,16,128]{3,2,1,0:T(8,128)S(1)} %shard_map.132.near, f32[16,16,128]{2,1,0:T(8,128)S(1)} %copy-done.2, f32[24,16,128]{2,1,0:T(8,128)S(1)} %all_gather.29.spread), custom_call_target="tpu_custom_call" | custom-call | tf_op jit(solution)/shard_map/pallas_call | solution.py:309
  64.4 2.1 %all_gather.30.pair = f32[22,16,128]{2,1,0:T(8,128)S(1)} all-gather(f32[11,16,128]{2,1,0:T(8,128)S(1)} %get-tuple-element.53), channel_id=1, replica_groups={{0,4},{8,12},{16,20},{24,28},{1,5},{9,13},{17,21},{25,29},{2,6},{10,14}..., dimensions={0}, use_global_device_ids=true | all-gather | bytes 270336 | tf_op jit(solution)/shard_map/all_gather | solution.py:327
  67.8 6.6 %collective-permute-start.9 = (f32[5,16,128]{2,1,0:T(8,128)S(1)}, f32[5,16,128]{2,1,0:T(8,128)S(1)}, u32[]{:S(2)}, u32[]{:S(2)}) collective-permute-start(f32[5,16,128]{2,1,0:T(8,128)S(1)} %get-tuple-element.55), channel_id=1, source_target_pairs={{4,8},{12,16},{20,24},{8,4},{16,12},{24,20},{5,9},{13,17},{21,25},... | collective-permute-start | bytes 122888 | tf_op jit(solution)/shard_map/ppermute | solution.py:339
  76.5 2.3 %collective-permute-done.11.along_z = f32[2,16,128]{2,1,0:T(8,128)S(1)} collective-permute-done((f32[2,16,128]{2,1,0:T(8,128)S(1)}, f32[2,16,128]{2,1,0:T(8,128)S(1)}, u32[]{:S(2)}, u32[]{:S(2)}) %collective-permute-start.11) | collective-permute-done | bytes 16416 | tf_op jit(solution)/shard_map/ppermute | solution.py:338
  78.8 1.9 %all_gather.31.refs_0_ = f32[24,16,128]{2,1,0:T(8,128)S(1)} all-gather(f32[12,16,128]{2,1,0:T(8,128)S(1)} %shard_map.137), channel_id=1, replica_groups={{0,4},{8,12},{16,20},{24,28},{1,5},{9,13},{17,21},{25,29},{2,6},{10,14}..., dimensions={0}, use_global_device_ids=true | all-gather | bytes 294912 | tf_op jit(solution)/shard_map/all_gather | solution.py:342
  80.8 1.6 %shard_map.138 = (f32[6,16,16,128]{3,2,1,0:T(8,128)}, f32[6,16,16,128]{3,2,1,0:T(8,128)}) custom-call(s32[1]{0:T(128)} %bitcast.core, f32[6,16,16,128]{3,2,1,0:T(8,128)S(1)} %shard_map.136.near, f32[6,16,16,128]{3,2,1,0:T(8,128)S(1)} %get-tuple-element.46.stress, f32[6,16,16,128]{3,2,1,0:T(8,128)S(1)} %get-tuple-element.57.memory, ...), custom_call_target="tpu_custom_call" | custom-call | tf_op jit(solution)/shard_map/pallas_call | solution.py:309
  (50 shorter events, 10.0 us)
Async XLA Ops:
  0.6 1.1 %copy-start = (f32[6,16,16,128]{3,2,1,0:T(8,128)S(1)}, f32[6,16,16,128]{3,2,1,0:T(8,128)}, u32[]{:S(2)}) copy-start(f32[6,16,16,128]{3,2,1,0:T(8,128)} %stress.5) | copy-start | bytes 2359300
  1.8 17.9 %copy-start.1 = (f32[6,16,16,128]{3,2,1,0:T(8,128)S(1)}, f32[6,16,16,128]{3,2,1,0:T(8,128)}, u32[]{:S(2)}) copy-start(f32[6,16,16,128]{3,2,1,0:T(8,128)} %stress.5) | copy-start | bytes 2359300
  2.1 17.6 %copy-start.6 = (f32[3,16,16,128]{3,2,1,0:T(8,128)S(1)}, f32[3,16,16,128]{3,2,1,0:T(8,128)}, u32[]{:S(2)}) copy-start(f32[3,16,16,128]{3,2,1,0:T(8,128)} %velocity.1) | copy-start | bytes 1179652
  10.7 9.0 %copy-start.2 = (f32[16,16,128]{2,1,0:T(8,128)S(1)}, f32[16,16,128]{2,1,0:T(8,128)}, u32[]{:S(2)}) copy-start(f32[16,16,128]{2,1,0:T(8,128)} %buoyancy.7) | copy-start | bytes 393220
  10.7 12.0 %collective-permute-start.1 = (f32[10,16,128]{2,1,0:T(8,128)S(1)}, f32[10,16,128]{2,1,0:T(8,128)S(1)}, u32[]{:S(2)}, u32[]{:S(2)}) collective-permute-start(f32[10,16,128]{2,1,0:T(8,128)S(1)} %get-tuple-element.35.behind), channel_id=1, source_target_pairs={{0,32},{32,64},{64,96},{96,128},{128,160},{160,192},{192,224},{224... | collective-permute-start | bytes 245768 | tf_op jit(solution)/shard_map/ppermute | solution.py:337
  12.2 7.6 %collective-permute-start = (f32[5,16,128]{2,1,0:T(8,128)S(1)}, f32[5,16,128]{2,1,0:T(8,128)S(1)}, u32[]{:S(2)}, u32[]{:S(2)}) collective-permute-start(f32[5,16,128]{2,1,0:T(8,128)S(1)} %get-tuple-element.34), channel_id=1, source_target_pairs={{4,8},{12,16},{20,24},{8,4},{16,12},{24,20},{5,9},{13,17},{21,25},... | collective-permute-start | bytes 122888 | tf_op jit(solution)/shard_map/ppermute | solution.py:339
  18.0 4.7 %collective-permute-start.2 = (f32[2,16,128]{2,1,0:T(8,128)S(1)}, f32[2,16,128]{2,1,0:T(8,128)S(1)}, u32[]{:S(2)}, u32[]{:S(2)}) collective-permute-start(f32[2,16,128]{2,1,0:T(8,128)S(1)} %get-tuple-element.36), channel_id=1, source_target_pairs={{0,1},{1,2},{2,3},{5,4},{6,5},{7,6},{8,9},{9,10},{10,11},{13,12},{... | collective-permute-start | bytes 49160 | tf_op jit(solution)/shard_map/ppermute | solution.py:338
  27.2 13.7 %copy-start.8 = (s32[16,16,128]{2,1,0:T(8,128)S(1)}, s32[16,16,128]{2,1,0:T(8,128)}, u32[]{:S(2)}) copy-start(s32[16,16,128]{2,1,0:T(8,128)} %mech.1) | copy-start | bytes 393220
  27.2 13.7 %copy-start.9 = (f32[16,16,128]{2,1,0:T(8,128)S(1)}, f32[16,16,128]{2,1,0:T(8,128)}, u32[]{:S(2)}) copy-start(f32[16,16,128]{2,1,0:T(8,128)} %weight.1) | copy-start | bytes 393220
  27.2 13.7 %copy-start.10 = (s32[16,16]{1,0:T(8,128)S(1)}, s32[16,16]{1,0:T(8,128)}, u32[]{:S(2)}) copy-start(s32[16,16]{1,0:T(8,128)} %top.1) | copy-start | bytes 3076
  27.2 16.8 %collective-permute-start.4 = (f32[10,16,128]{2,1,0:T(8,128)S(1)}, f32[10,16,128]{2,1,0:T(8,128)S(1)}, u32[]{:S(2)}, u32[]{:S(2)}) collective-permute-start(f32[10,16,128]{2,1,0:T(8,128)S(1)} %get-tuple-element.41.behind), channel_id=1, source_target_pairs={{0,32},{32,64},{64,96},{96,128},{128,160},{160,192},{192,224},{224... | collective-permute-start | bytes 245768 | tf_op jit(solution)/shard_map/ppermute | solution.py:337
  28.7 13.5 %collective-permute-start.3 = (f32[5,16,128]{2,1,0:T(8,128)S(1)}, f32[5,16,128]{2,1,0:T(8,128)S(1)}, u32[]{:S(2)}, u32[]{:S(2)}) collective-permute-start(f32[5,16,128]{2,1,0:T(8,128)S(1)} %get-tuple-element.40), channel_id=1, source_target_pairs={{4,8},{12,16},{20,24},{8,4},{16,12},{24,20},{5,9},{13,17},{21,25},... | collective-permute-start | bytes 122888 | tf_op jit(solution)/shard_map/ppermute | solution.py:339
  39.6 4.5 %collective-permute-start.5 = (f32[2,16,128]{2,1,0:T(8,128)S(1)}, f32[2,16,128]{2,1,0:T(8,128)S(1)}, u32[]{:S(2)}, u32[]{:S(2)}) collective-permute-start(f32[2,16,128]{2,1,0:T(8,128)S(1)} %get-tuple-element.45), channel_id=1, source_target_pairs={{0,1},{1,2},{2,3},{5,4},{6,5},{7,6},{8,9},{9,10},{10,11},{13,12},{... | collective-permute-start | bytes 49160 | tf_op jit(solution)/shard_map/ppermute | solution.py:338
  40.9 0.7 copy-start.11
  42.7 3.5 %copy-start.3 = (f32[6,16,16,128]{3,2,1,0:T(8,128)S(1)}, f32[6,16,16,128]{3,2,1,0:T(8,128)}, u32[]{:S(2)}) copy-start(f32[6,16,16,128]{3,2,1,0:T(8,128)} %memory.1) | copy-start | bytes 2359300
  44.1 2.1 %copy-start.4 = (f32[16,16,128]{2,1,0:T(8,128)S(1)}, f32[16,16,128]{2,1,0:T(8,128)}, u32[]{:S(2)}) copy-start(f32[16,16,128]{2,1,0:T(8,128)} %lam.3) | copy-start | bytes 393220
  44.1 2.1 %copy-start.5 = (f32[16,16,128]{2,1,0:T(8,128)S(1)}, f32[16,16,128]{2,1,0:T(8,128)}, u32[]{:S(2)}) copy-start(f32[16,16,128]{2,1,0:T(8,128)} %shear.3) | copy-start | bytes 393220
  49.0 12.1 %collective-permute-start.7 = (f32[10,16,128]{2,1,0:T(8,128)S(1)}, f32[10,16,128]{2,1,0:T(8,128)S(1)}, u32[]{:S(2)}, u32[]{:S(2)}) collective-permute-start(f32[10,16,128]{2,1,0:T(8,128)S(1)} %get-tuple-element.50.behind), channel_id=1, source_target_pairs={{0,32},{32,64},{64,96},{96,128},{128,160},{160,192},{192,224},{224... | collective-permute-start | bytes 245768 | tf_op jit(solution)/shard_map/ppermute | solution.py:337
  50.3 8.0 %collective-permute-start.6 = (f32[5,16,128]{2,1,0:T(8,128)S(1)}, f32[5,16,128]{2,1,0:T(8,128)S(1)}, u32[]{:S(2)}, u32[]{:S(2)}) collective-permute-start(f32[5,16,128]{2,1,0:T(8,128)S(1)} %get-tuple-element.49), channel_id=1, source_target_pairs={{4,8},{12,16},{20,24},{8,4},{16,12},{24,20},{5,9},{13,17},{21,25},... | collective-permute-start | bytes 122888 | tf_op jit(solution)/shard_map/ppermute | solution.py:339
  56.6 4.5 %collective-permute-start.8 = (f32[2,16,128]{2,1,0:T(8,128)S(1)}, f32[2,16,128]{2,1,0:T(8,128)S(1)}, u32[]{:S(2)}, u32[]{:S(2)}) collective-permute-start(f32[2,16,128]{2,1,0:T(8,128)S(1)} %get-tuple-element.51), channel_id=1, source_target_pairs={{0,1},{1,2},{2,3},{5,4},{6,5},{7,6},{8,9},{9,10},{10,11},{13,12},{... | collective-permute-start | bytes 49160 | tf_op jit(solution)/shard_map/ppermute | solution.py:338
  64.4 11.6 %copy-start.7 = (f32[3,16,16,128]{3,2,1,0:T(8,128)S(1)}, f32[3,16,16,128]{3,2,1,0:T(8,128)}, u32[]{:S(2)}) copy-start(f32[3,16,16,128]{3,2,1,0:T(8,128)} %get-tuple-element.29.velocity) | copy-start | bytes 1179652
  66.5 12.4 %collective-permute-start.10 = (f32[10,16,128]{2,1,0:T(8,128)S(1)}, f32[10,16,128]{2,1,0:T(8,128)S(1)}, u32[]{:S(2)}, u32[]{:S(2)}) collective-permute-start(f32[10,16,128]{2,1,0:T(8,128)S(1)} %get-tuple-element.56.behind), channel_id=1, source_target_pairs={{0,32},{32,64},{64,96},{96,128},{128,160},{160,192},{192,224},{224... | collective-permute-start | bytes 245768 | tf_op jit(solution)/shard_map/ppermute | solution.py:337
  67.8 8.2 %collective-permute-start.9 = (f32[5,16,128]{2,1,0:T(8,128)S(1)}, f32[5,16,128]{2,1,0:T(8,128)S(1)}, u32[]{:S(2)}, u32[]{:S(2)}) collective-permute-start(f32[5,16,128]{2,1,0:T(8,128)S(1)} %get-tuple-element.55), channel_id=1, source_target_pairs={{4,8},{12,16},{20,24},{8,4},{16,12},{24,20},{5,9},{13,17},{21,25},... | collective-permute-start | bytes 122888 | tf_op jit(solution)/shard_map/ppermute | solution.py:339
  74.3 4.5 %collective-permute-start.11 = (f32[2,16,128]{2,1,0:T(8,128)S(1)}, f32[2,16,128]{2,1,0:T(8,128)S(1)}, u32[]{:S(2)}, u32[]{:S(2)}) collective-permute-start(f32[2,16,128]{2,1,0:T(8,128)S(1)} %get-tuple-element.58), channel_id=1, source_target_pairs={{0,1},{1,2},{2,3},{5,4},{6,5},{7,6},{8,9},{9,10},{10,11},{13,12},{... | collective-permute-start | bytes 49160 | tf_op jit(solution)/shard_map/ppermute | solution.py:338

commit v7 on v6

--- a/solution.py
+++ b/solution.py
@@ -54,7 +54,7 @@
 
 
 class Near:
-    def __init__(self, spec, fields, core, pair, outer, rows):
+    def __init__(self, spec, fields, core, pair, rows):
         self.spec, self.fields, self.rows = spec, fields, rows
         self.nx, self.ny, self.nz = nx, ny, nz = fields.shape[1:]
         first = {k: i for i, k in enumerate(layers(spec[1], BEFORE))}
@@ -71,7 +71,7 @@
                     for off in AFTER[kind]:
                         rows[slot, x, 8 + ny + off : 9 + ny + off, :] = after(last[comp, off], x)
 
-        beyond = lambda i, x: outer[i, x : x + 1, :]
+        beyond = lambda i, x: jnp.zeros((1, nz), jnp.float32)
 
         @pl.when(core == 0)
         def _():
@@ -148,6 +148,29 @@
                 total = total + weight * self.spread[TAKEN + self.core * FACE + i]
         return total
 
+    def outer_rows(self, outer, add):
+        ny = self.ny
+
+        def rows(sides, place, base):
+            for slot, (comp, kind) in enumerate(self.spec[1]):
+                terms = {}
+                for off in sides[kind]:
+                    for shift, weight in TAPS[kind]:
+                        at = base + off - shift
+                        if 0 <= at < ny:
+                            term = weight * outer[place[comp, off]]
+                            terms[at] = terms[at] + term if at in terms else term
+                for at, term in terms.items():
+                    add(slot, at, term)
+
+        @pl.when(self.core == 0)
+        def _():
+            rows(BEFORE, self.before[1], 0)
+
+        @pl.when(self.core == 1)
+        def _():
+            rows(AFTER, self.after[1], ny)
+
     def dz(self, comp, x):
         slot = [c for c, _ in self.spec[2]].index(comp)
         return self.edges[slot, x * self.ny : (x + 1) * self.ny, :]
@@ -226,8 +249,8 @@
         gain[x] = (1.0 - here) * weight[x]
 
 
-def near_velocity_kernel(core, stress, velocity, buoyancy, pair, outer, behind, out, rows):
-    near = Near(STRESS, stress, core[0], pair, outer, rows)
+def near_velocity_kernel(core, stress, velocity, buoyancy, pair, behind, out, rows):
+    near = Near(STRESS, stress, core[0], pair, rows)
     for x in range(velocity.shape[1]):
         scale = TIME_STEP * buoyancy[x]
         out[0, x] = velocity[0, x] + scale * (near.dx(0, x) + near.dy(3, x) + near.dz(4, x))
@@ -235,18 +258,23 @@
         out[2, x] = velocity[2, x] + scale * (near.dx(4, x) + near.dy(5, x) + near.dz(2, x))
 
 
-def velocity_kernel(core, near, buoyancy, spread, out, own, given, edges):
+def velocity_kernel(core, near, buoyancy, spread, outer, out, own, given, edges):
     far = Far(STRESS, near.shape[1:], core[0], spread, edges)
     for x in range(near.shape[1]):
         scale = TIME_STEP * buoyancy[x]
         out[0, x] = near[0, x] + scale * (far.dx(0, x) + far.dz(4, x))
         out[1, x] = near[1, x] + scale * (far.dx(3, x) + far.dz(5, x))
         out[2, x] = near[2, x] + scale * (far.dx(4, x) + far.dz(2, x))
+
+    def add(slot, row, terms):
+        out[slot, :, row, :] = out[slot, :, row, :] + TIME_STEP * buoyancy[:, row, :] * terms
+
+    far.outer_rows(outer, add)
     pack(VELOCITY, out, core[0], own, given)
 
 
-def near_strain_kernel(core, velocity, pair, outer, behind, out, rows):
-    near = Near(VELOCITY, velocity, core[0], pair, outer, rows)
+def near_strain_kernel(core, velocity, pair, behind, out, rows):
+    near = Near(VELOCITY, velocity, core[0], pair, rows)
     for x in range(velocity.shape[1]):
         out[0, x] = near.dx(0, x)
         out[1, x] = near.dy(1, x)
@@ -258,27 +286,33 @@
 
 def stress_kernel(send, core, near, stress, memory, lam, shear, decay, gain, limits, *refs):
     if send:
-        spread, out, kept, own, given, edges = refs
+        spread, outer, out, kept, own, given, edges, rows = refs
     else:
-        spread, *finals, out, kept, sems, edges = refs
+        spread, outer, *finals, out, kept, sems, edges, rows = refs
     nx, ny, nz = lam.shape
     far = Far(VELOCITY, lam.shape, core[0], spread, edges)
     depth = lax.broadcasted_iota(jnp.int32, (1, nz), 1).astype(jnp.float32)
+    rows[...] = jnp.zeros(rows.shape, jnp.float32)
+
+    def add(slot, row, terms):
+        rows[slot, :, row, :] = terms
+
+    far.outer_rows(outer, add)
     copies = []
     for x in range(nx):
         top = limits[:, x : x + 1]
         solid = depth >= top
         below = depth > top
-        xx, yy, zz = near[0, x] + far.dx(0, x), near[1, x], near[2, x] + far.dz(2, x)
+        xx, yy, zz = near[0, x] + far.dx(0, x), near[1, x] + rows[0, x], near[2, x] + far.dz(2, x)
         volume = lam[x] * (xx + yy + zz)
         double = 2.0 * shear[x]
         rates = (
             volume + double * xx,
             volume + double * yy,
             volume + double * zz,
-            shear[x] * (near[3, x] + far.dx(1, x)),
+            shear[x] * (near[3, x] + rows[1, x] + far.dx(1, x)),
             shear[x] * (near[4, x] + far.dz(0, x) + far.dx(2, x)),
-            shear[x] * (near[5, x] + far.dz(1, x)),
+            shear[x] * (near[5, x] + rows[2, x] + far.dz(1, x)),
         )
         for comp, rate in enumerate(rates):
             new = decay[x] * memory[comp, x] + gain[x] * rate
@@ -337,10 +371,10 @@
     got_x = lax.ppermute(along_x, ("gx", "gy"), to_x)
     got_z = lax.ppermute(along_z, ("gy", "gz"), to_z)
     outer = lax.ppermute(along_y, "gy", to_y)
-    near = near_kernel(pair, outer, along_x)
+    near = near_kernel(pair, along_x)
     (taken,) = call(join_kernel, [planes(TAKEN)], [got_x, got_z, near], scalars=0, hold=True)
     spread = lax.all_gather(taken, "gy", axis=0, tiled=True, axis_index_groups=cores)
-    return near, spread, along_x
+    return near, spread, outer, along_x
 
 
 def shards(
@@ -362,6 +396,7 @@
     packed = [jax.ShapeDtypeStruct((GIVEN, ny, nz), jnp.float32)] * 2
     rows = [pltpu.VMEM((3, nx, ny + 16, nz), jnp.float32)]
     edges = [pltpu.VMEM((3, nx * ny, nz), jnp.float32)]
+    terms = [pltpu.VMEM((3, nx, ny, nz), jnp.float32)]
     held = [
         pltpu.VMEM(stress.shape, jnp.float32),
         pltpu.VMEM(memory.shape, jnp.float32),
@@ -379,7 +414,7 @@
             outs = [like(stress)]
             return call(near_strain_kernel, outs, [core, velocity, *got], scratch=rows, hold=True)[0]
 
-        near, spread, along = exchange(core, own, given, near_velocity)
+        near, spread, outer, along = exchange(core, own, given, near_velocity)
         if step == 0:
             cells = call(
                 cells_kernel,
@@ -391,16 +426,16 @@
         velocity, own, given = call(
             velocity_kernel,
             [like(velocity)] + packed,
-            [core, near, buoyancy, spread],
+            [core, near, buoyancy, spread, outer],
             scratch=edges,
         )
-        near, spread, _ = exchange(core, own, given, near_strain)
+        near, spread, outer, _ = exchange(core, own, given, near_strain)
         send = step < STEPS - 1
         stress, memory, *rest = call(
             functools.partial(stress_kernel, send),
             [like(stress), like(memory)] + (packed if send else []),
-            [core, near, stress, memory, lame_lambda, shear_modulus, *cells, spread],
-            scratch=edges if send else held + edges,
+            [core, near, stress, memory, lame_lambda, shear_modulus, *cells, spread, outer],
+            scratch=(edges if send else held + edges) + terms,
             out_space=pltpu.VMEM if send else pl.ANY,
         )
         if send:

time: 83 us -> 81.8 us (0.986)
  waiting for transfers between devices: 9.57 us -> 0.21 us
  starting transfers between devices: 40.2 us -> 48 us
    ppermute x4, waiting for transfers between devices: 8.45 us -> 0.01 us  [exchange(): got_z = lax.ppermute(along_z, ('gy', 'gz'), to_z)]
    ppermute x4, starting transfers between devices: 29.6 us -> 37.4 us  [exchange(): outer = lax.ppermute(along_y, 'gy', to_y)]
    ppermute x4, waiting for transfers between devices: 1.12 us -> 0.01 us  [exchange(): outer = lax.ppermute(along_y, 'gy', to_y)]
  transfers between devices with their start and end apart: 12 -> 12, of which waited for: 7 -> 1; matrix products, arithmetic and copies ran while one was open for 0% -> 0% of each run, Pallas kernels for 3% -> 3%
where the time goes in v7:
time: 81.8 us; the launch traced here: 81.2 us
  starting transfers between devices  48 us (59%)
  blocking collectives  22.4 us (27%)
  Pallas kernels  7.77 us (9%)
  local copies, waits for them, and re-layouts  1.8 us (2%)
  between operations  1.03 us (1%)
    ppermute x4, starting transfers between devices, exchange(): outer = lax.ppermute(along_y, 'gy', to_y)  37.4 us
    all_gather x4, blocking collectives, exchange(): lax.all_gather(given, 'gy', axis=0, tiled=True, axis_index_groups=cores)  14.5 us
    all_gather x4, blocking collectives, exchange(): lax.all_gather(taken, 'gy', axis=0, tiled=True, axis_index_groups=cores)  7.92 us
    pallas_call x18, Pallas kernels, call(): pl.pallas_call(body, out_shape=outs, in_specs=specs, out_specs=[pl.BlockS...  7.77 us
    ppermute x4, starting transfers between devices, exchange(): got_x = lax.ppermute(along_x, ('gx', 'gy'), to_x)  5.43 us
    ppermute x4, starting transfers between devices, exchange(): got_z = lax.ppermute(along_z, ('gy', 'gz'), to_z)  5.17 us
    unnamed x24, local copies, waits for them, and re-layouts  1.8 us
  transfers between devices with their start and end apart: 12, of which 1 were waited for; matrix products, arithmetic and copies ran while one was open for 0% of the time, Pallas kernels for 3%

profile of v7, /device:TPU:1, one launch (start us, length us, event | category | flops | bytes accessed | tf_op | source)
XLA Modules:
  0.0 81.2 jit_solution(465000947700812434)
XLA Ops:
  0.7 1.1 %copy-done = f32[6,16,16,128]{3,2,1,0:T(8,128)S(1)} copy-done((f32[6,16,16,128]{3,2,1,0:T(8,128)S(1)}, f32[6,16,16,128]{3,2,1,0:T(8,128)}, u32[]{:S(2)}) %copy-start) | copy-done | bytes 786456
  2.1 8.6 %all_gather.24.pair = f32[22,16,128]{2,1,0:T(8,128)S(1)} all-gather(f32[11,16,128]{2,1,0:T(8,128)S(1)} %get-tuple-element.32), channel_id=1, replica_groups={{0,4},{8,12},{16,20},{24,28},{1,5},{9,13},{17,21},{25,29},{2,6},{10,14}..., dimensions={0}, use_global_device_ids=true | all-gather | bytes 270336 | tf_op jit(solution)/shard_map/all_gather | solution.py:361
  10.7 1.4 %collective-permute-start = (f32[10,16,128]{2,1,0:T(8,128)S(1)}, f32[10,16,128]{2,1,0:T(8,128)S(1)}, u32[]{:S(2)}, u32[]{:S(2)}) collective-permute-start(f32[10,16,128]{2,1,0:T(8,128)S(1)} %get-tuple-element.34.behind), channel_id=1, source_target_pairs={{0,32},{32,64},{64,96},{96,128},{128,160},{160,192},{192,224},{224... | collective-permute-start | bytes 245768 | tf_op jit(solution)/shard_map/ppermute | solution.py:371
  12.2 1.3 %collective-permute-start.1 = (f32[2,16,128]{2,1,0:T(8,128)S(1)}, f32[2,16,128]{2,1,0:T(8,128)S(1)}, u32[]{:S(2)}, u32[]{:S(2)}) collective-permute-start(f32[2,16,128]{2,1,0:T(8,128)S(1)} %get-tuple-element.35), channel_id=1, source_target_pairs={{0,1},{1,2},{2,3},{5,4},{6,5},{7,6},{8,9},{9,10},{10,11},{13,12},{... | collective-permute-start | bytes 49160 | tf_op jit(solution)/shard_map/ppermute | solution.py:372
  13.5 8.4 %collective-permute-start.2 = (f32[5,16,128]{2,1,0:T(8,128)S(1)}, f32[5,16,128]{2,1,0:T(8,128)S(1)}, u32[]{:S(2)}, u32[]{:S(2)}) collective-permute-start(f32[5,16,128]{2,1,0:T(8,128)S(1)} %get-tuple-element.36), channel_id=1, source_target_pairs={{4,8},{12,16},{20,24},{8,4},{16,12},{24,20},{5,9},{13,17},{21,25},... | collective-permute-start | bytes 122888 | tf_op jit(solution)/shard_map/ppermute | solution.py:373
  22.4 1.9 %all_gather.25.spread = f32[24,16,128]{2,1,0:T(8,128)S(1)} all-gather(f32[12,16,128]{2,1,0:T(8,128)S(1)} %shard_map.124), channel_id=1, replica_groups={{0,4},{8,12},{16,20},{24,28},{1,5},{9,13},{17,21},{25,29},{2,6},{10,14}..., dimensions={0}, use_global_device_ids=true | all-gather | bytes 294912 | tf_op jit(solution)/shard_map/all_gather | solution.py:376
  25.1 1.9 %all_gather.26.pair = f32[22,16,128]{2,1,0:T(8,128)S(1)} all-gather(f32[11,16,128]{2,1,0:T(8,128)S(1)} %get-tuple-element.38), channel_id=1, replica_groups={{0,4},{8,12},{16,20},{24,28},{1,5},{9,13},{17,21},{25,29},{2,6},{10,14}..., dimensions={0}, use_global_device_ids=true | all-gather | bytes 270336 | tf_op jit(solution)/shard_map/all_gather | solution.py:361
  27.0 1.4 %collective-permute-start.3 = (f32[10,16,128]{2,1,0:T(8,128)S(1)}, f32[10,16,128]{2,1,0:T(8,128)S(1)}, u32[]{:S(2)}, u32[]{:S(2)}) collective-permute-start(f32[10,16,128]{2,1,0:T(8,128)S(1)} %get-tuple-element.40.behind), channel_id=1, source_target_pairs={{0,32},{32,64},{64,96},{96,128},{128,160},{160,192},{192,224},{224... | collective-permute-start | bytes 245768 | tf_op jit(solution)/shard_map/ppermute | solution.py:371
  28.5 1.3 %collective-permute-start.4 = (f32[2,16,128]{2,1,0:T(8,128)S(1)}, f32[2,16,128]{2,1,0:T(8,128)S(1)}, u32[]{:S(2)}, u32[]{:S(2)}) collective-permute-start(f32[2,16,128]{2,1,0:T(8,128)S(1)} %get-tuple-element.44), channel_id=1, source_target_pairs={{0,1},{1,2},{2,3},{5,4},{6,5},{7,6},{8,9},{9,10},{10,11},{13,12},{... | collective-permute-start | bytes 49160 | tf_op jit(solution)/shard_map/ppermute | solution.py:372
  31.0 11.8 %collective-permute-start.5 = (f32[5,16,128]{2,1,0:T(8,128)S(1)}, f32[5,16,128]{2,1,0:T(8,128)S(1)}, u32[]{:S(2)}, u32[]{:S(2)}) collective-permute-start(f32[5,16,128]{2,1,0:T(8,128)S(1)} %get-tuple-element.45), channel_id=1, source_target_pairs={{4,8},{12,16},{20,24},{8,4},{16,12},{24,20},{5,9},{13,17},{21,25},... | collective-permute-start | bytes 122888 | tf_op jit(solution)/shard_map/ppermute | solution.py:373
  43.4 2.1 %all_gather.27.refs_0_ = f32[24,16,128]{2,1,0:T(8,128)S(1)} all-gather(f32[12,16,128]{2,1,0:T(8,128)S(1)} %shard_map.129), channel_id=1, replica_groups={{0,4},{8,12},{16,20},{24,28},{1,5},{9,13},{17,21},{25,29},{2,6},{10,14}..., dimensions={0}, use_global_device_ids=true | all-gather | bytes 294912 | tf_op jit(solution)/shard_map/all_gather | solution.py:376
  45.5 1.1 %shard_map.130 = (f32[6,16,16,128]{3,2,1,0:T(8,128)S(1)}, f32[6,16,16,128]{3,2,1,0:T(8,128)S(1)}, f32[11,16,128]{2,1,0:T(8,128)S(1)}, f32[11,16,128]{2,1,0:T(8,128)S(1)}) custom-call(s32[1]{0:T(128)} %bitcast.core, f32[6,16,16,128]{3,2,1,0:T(8,128)S(1)} %shard_map.127.near, f32[6,16,16,128]{3,2,1,0:T(8,128)S(1)} %copy-done.1, ...), custom_call_target="tpu_custom_call" | custom-call | tf_op jit(solution)/shard_map/pallas_call | solution.py:343
  46.6 1.9 %all_gather.28.pair = f32[22,16,128]{2,1,0:T(8,128)S(1)} all-gather(f32[11,16,128]{2,1,0:T(8,128)S(1)} %get-tuple-element.47), channel_id=1, replica_groups={{0,4},{8,12},{16,20},{24,28},{1,5},{9,13},{17,21},{25,29},{2,6},{10,14}..., dimensions={0}, use_global_device_ids=true | all-gather | bytes 270336 | tf_op jit(solution)/shard_map/all_gather | solution.py:361
  48.5 1.3 %collective-permute-start.6 = (f32[10,16,128]{2,1,0:T(8,128)S(1)}, f32[10,16,128]{2,1,0:T(8,128)S(1)}, u32[]{:S(2)}, u32[]{:S(2)}) collective-permute-start(f32[10,16,128]{2,1,0:T(8,128)S(1)} %get-tuple-element.49.behind), channel_id=1, source_target_pairs={{0,32},{32,64},{64,96},{96,128},{128,160},{160,192},{192,224},{224... | collective-permute-start | bytes 245768 | tf_op jit(solution)/shard_map/ppermute | solution.py:371
  49.8 1.3 %collective-permute-start.7 = (f32[2,16,128]{2,1,0:T(8,128)S(1)}, f32[2,16,128]{2,1,0:T(8,128)S(1)}, u32[]{:S(2)}, u32[]{:S(2)}) collective-permute-start(f32[2,16,128]{2,1,0:T(8,128)S(1)} %get-tuple-element.50), channel_id=1, source_target_pairs={{0,1},{1,2},{2,3},{5,4},{6,5},{7,6},{8,9},{9,10},{10,11},{13,12},{... | collective-permute-start | bytes 49160 | tf_op jit(solution)/shard_map/ppermute | solution.py:372
  51.1 8.8 %collective-permute-start.8 = (f32[5,16,128]{2,1,0:T(8,128)S(1)}, f32[5,16,128]{2,1,0:T(8,128)S(1)}, u32[]{:S(2)}, u32[]{:S(2)}) collective-permute-start(f32[5,16,128]{2,1,0:T(8,128)S(1)} %get-tuple-element.51), channel_id=1, source_target_pairs={{4,8},{12,16},{20,24},{8,4},{16,12},{24,20},{5,9},{13,17},{21,25},... | collective-permute-start | bytes 122888 | tf_op jit(solution)/shard_map/ppermute | solution.py:373
  60.5 1.9 %all_gather.29.spread = f32[24,16,128]{2,1,0:T(8,128)S(1)} all-gather(f32[12,16,128]{2,1,0:T(8,128)S(1)} %shard_map.133), channel_id=1, replica_groups={{0,4},{8,12},{16,20},{24,28},{1,5},{9,13},{17,21},{25,29},{2,6},{10,14}..., dimensions={0}, use_global_device_ids=true | all-gather | bytes 294912 | tf_op jit(solution)/shard_map/all_gather | solution.py:376
  62.4 1.4 %shard_map.134 = (f32[3,16,16,128]{3,2,1,0:T(8,128)}, f32[11,16,128]{2,1,0:T(8,128)S(1)}, f32[11,16,128]{2,1,0:T(8,128)S(1)}) custom-call(s32[1]{0:T(128)} %bitcast.core, f32[3,16,16,128]{3,2,1,0:T(8,128)S(1)} %shard_map.132.near, f32[16,16,128]{2,1,0:T(8,128)S(1)} %copy-done.2, f32[24,16,128]{2,1,0:T(8,128)S(1)} %all_gather.29.spread, ...), custom_call_target="tpu_custom_call" | custom-call | tf_op jit(solution)/shard_map/pallas_call | solution.py:343
  63.8 2.1 %all_gather.30.pair = f32[22,16,128]{2,1,0:T(8,128)S(1)} all-gather(f32[11,16,128]{2,1,0:T(8,128)S(1)} %get-tuple-element.53), channel_id=1, replica_groups={{0,4},{8,12},{16,20},{24,28},{1,5},{9,13},{17,21},{25,29},{2,6},{10,14}..., dimensions={0}, use_global_device_ids=true | all-gather | bytes 270336 | tf_op jit(solution)/shard_map/all_gather | solution.py:361
  65.9 1.3 %collective-permute-start.9 = (f32[10,16,128]{2,1,0:T(8,128)S(1)}, f32[10,16,128]{2,1,0:T(8,128)S(1)}, u32[]{:S(2)}, u32[]{:S(2)}) collective-permute-start(f32[10,16,128]{2,1,0:T(8,128)S(1)} %get-tuple-element.55.behind), channel_id=1, source_target_pairs={{0,32},{32,64},{64,96},{96,128},{128,160},{160,192},{192,224},{224... | collective-permute-start | bytes 245768 | tf_op jit(solution)/shard_map/ppermute | solution.py:371
  67.2 1.3 %collective-permute-start.10 = (f32[2,16,128]{2,1,0:T(8,128)S(1)}, f32[2,16,128]{2,1,0:T(8,128)S(1)}, u32[]{:S(2)}, u32[]{:S(2)}) collective-permute-start(f32[2,16,128]{2,1,0:T(8,128)S(1)} %get-tuple-element.57), channel_id=1, source_target_pairs={{0,1},{1,2},{2,3},{5,4},{6,5},{7,6},{8,9},{9,10},{10,11},{13,12},{... | collective-permute-start | bytes 49160 | tf_op jit(solution)/shard_map/ppermute | solution.py:372
  68.5 8.4 %collective-permute-start.11 = (f32[5,16,128]{2,1,0:T(8,128)S(1)}, f32[5,16,128]{2,1,0:T(8,128)S(1)}, u32[]{:S(2)}, u32[]{:S(2)}) collective-permute-start(f32[5,16,128]{2,1,0:T(8,128)S(1)} %get-tuple-element.58), channel_id=1, source_target_pairs={{4,8},{12,16},{20,24},{8,4},{16,12},{24,20},{5,9},{13,17},{21,25},... | collective-permute-start | bytes 122888 | tf_op jit(solution)/shard_map/ppermute | solution.py:373
  77.6 1.9 %all_gather.31.refs_0_ = f32[24,16,128]{2,1,0:T(8,128)S(1)} all-gather(f32[12,16,128]{2,1,0:T(8,128)S(1)} %shard_map.137), channel_id=1, replica_groups={{0,4},{8,12},{16,20},{24,28},{1,5},{9,13},{17,21},{25,29},{2,6},{10,14}..., dimensions={0}, use_global_device_ids=true | all-gather | bytes 294912 | tf_op jit(solution)/shard_map/all_gather | solution.py:376
  79.6 1.6 %shard_map.138 = (f32[6,16,16,128]{3,2,1,0:T(8,128)}, f32[6,16,16,128]{3,2,1,0:T(8,128)}) custom-call(s32[1]{0:T(128)} %bitcast.core, f32[6,16,16,128]{3,2,1,0:T(8,128)S(1)} %shard_map.136.near, f32[6,16,16,128]{3,2,1,0:T(8,128)S(1)} %get-tuple-element.46.stress, f32[6,16,16,128]{3,2,1,0:T(8,128)S(1)} %get-tuple-element.56.memory, ...), custom_call_target="tpu_custom_call" | custom-call | tf_op jit(solution)/shard_map/pallas_call | solution.py:343
  (50 shorter events, 4.6 us)
Async XLA Ops:
  0.6 1.1 %copy-start = (f32[6,16,16,128]{3,2,1,0:T(8,128)S(1)}, f32[6,16,16,128]{3,2,1,0:T(8,128)}, u32[]{:S(2)}) copy-start(f32[6,16,16,128]{3,2,1,0:T(8,128)} %stress.5) | copy-start | bytes 2359300
  1.8 20.1 %copy-start.1 = (f32[6,16,16,128]{3,2,1,0:T(8,128)S(1)}, f32[6,16,16,128]{3,2,1,0:T(8,128)}, u32[]{:S(2)}) copy-start(f32[6,16,16,128]{3,2,1,0:T(8,128)} %stress.5) | copy-start | bytes 2359300
  2.1 19.8 %copy-start.6 = (f32[3,16,16,128]{3,2,1,0:T(8,128)S(1)}, f32[3,16,16,128]{3,2,1,0:T(8,128)}, u32[]{:S(2)}) copy-start(f32[3,16,16,128]{3,2,1,0:T(8,128)} %velocity.1) | copy-start | bytes 1179652
  10.7 11.2 %copy-start.2 = (f32[16,16,128]{2,1,0:T(8,128)S(1)}, f32[16,16,128]{2,1,0:T(8,128)}, u32[]{:S(2)}) copy-start(f32[16,16,128]{2,1,0:T(8,128)} %buoyancy.7) | copy-start | bytes 393220
  10.7 11.7 %collective-permute-start = (f32[10,16,128]{2,1,0:T(8,128)S(1)}, f32[10,16,128]{2,1,0:T(8,128)S(1)}, u32[]{:S(2)}, u32[]{:S(2)}) collective-permute-start(f32[10,16,128]{2,1,0:T(8,128)S(1)} %get-tuple-element.34.behind), channel_id=1, source_target_pairs={{0,32},{32,64},{64,96},{96,128},{128,160},{160,192},{192,224},{224... | collective-permute-start | bytes 245768 | tf_op jit(solution)/shard_map/ppermute | solution.py:371
  12.2 10.2 %collective-permute-start.1 = (f32[2,16,128]{2,1,0:T(8,128)S(1)}, f32[2,16,128]{2,1,0:T(8,128)S(1)}, u32[]{:S(2)}, u32[]{:S(2)}) collective-permute-start(f32[2,16,128]{2,1,0:T(8,128)S(1)} %get-tuple-element.35), channel_id=1, source_target_pairs={{0,1},{1,2},{2,3},{5,4},{6,5},{7,6},{8,9},{9,10},{10,11},{13,12},{... | collective-permute-start | bytes 49160 | tf_op jit(solution)/shard_map/ppermute | solution.py:372
  13.5 10.9 %collective-permute-start.2 = (f32[5,16,128]{2,1,0:T(8,128)S(1)}, f32[5,16,128]{2,1,0:T(8,128)S(1)}, u32[]{:S(2)}, u32[]{:S(2)}) collective-permute-start(f32[5,16,128]{2,1,0:T(8,128)S(1)} %get-tuple-element.36), channel_id=1, source_target_pairs={{4,8},{12,16},{20,24},{8,4},{16,12},{24,20},{5,9},{13,17},{21,25},... | collective-permute-start | bytes 122888 | tf_op jit(solution)/shard_map/ppermute | solution.py:373
  27.0 2.8 %copy-start.8 = (s32[16,16,128]{2,1,0:T(8,128)S(1)}, s32[16,16,128]{2,1,0:T(8,128)}, u32[]{:S(2)}) copy-start(s32[16,16,128]{2,1,0:T(8,128)} %mech.1) | copy-start | bytes 393220
  27.0 2.8 %copy-start.9 = (f32[16,16,128]{2,1,0:T(8,128)S(1)}, f32[16,16,128]{2,1,0:T(8,128)}, u32[]{:S(2)}) copy-start(f32[16,16,128]{2,1,0:T(8,128)} %weight.1) | copy-start | bytes 393220
  27.0 2.8 %copy-start.10 = (s32[16,16]{1,0:T(8,128)S(1)}, s32[16,16]{1,0:T(8,128)}, u32[]{:S(2)}) copy-start(s32[16,16]{1,0:T(8,128)} %top.1) | copy-start | bytes 3076
  27.0 16.3 %collective-permute-start.3 = (f32[10,16,128]{2,1,0:T(8,128)S(1)}, f32[10,16,128]{2,1,0:T(8,128)S(1)}, u32[]{:S(2)}, u32[]{:S(2)}) collective-permute-start(f32[10,16,128]{2,1,0:T(8,128)S(1)} %get-tuple-element.40.behind), channel_id=1, source_target_pairs={{0,32},{32,64},{64,96},{96,128},{128,160},{160,192},{192,224},{224... | collective-permute-start | bytes 245768 | tf_op jit(solution)/shard_map/ppermute | solution.py:371
  28.5 14.9 %collective-permute-start.4 = (f32[2,16,128]{2,1,0:T(8,128)S(1)}, f32[2,16,128]{2,1,0:T(8,128)S(1)}, u32[]{:S(2)}, u32[]{:S(2)}) collective-permute-start(f32[2,16,128]{2,1,0:T(8,128)S(1)} %get-tuple-element.44), channel_id=1, source_target_pairs={{0,1},{1,2},{2,3},{5,4},{6,5},{7,6},{8,9},{9,10},{10,11},{13,12},{... | collective-permute-start | bytes 49160 | tf_op jit(solution)/shard_map/ppermute | solution.py:372
  29.8 0.7 copy-start.11
  31.0 14.5 %collective-permute-start.5 = (f32[5,16,128]{2,1,0:T(8,128)S(1)}, f32[5,16,128]{2,1,0:T(8,128)S(1)}, u32[]{:S(2)}, u32[]{:S(2)}) collective-permute-start(f32[5,16,128]{2,1,0:T(8,128)S(1)} %get-tuple-element.45), channel_id=1, source_target_pairs={{4,8},{12,16},{20,24},{8,4},{16,12},{24,20},{5,9},{13,17},{21,25},... | collective-permute-start | bytes 122888 | tf_op jit(solution)/shard_map/ppermute | solution.py:373
  43.3 2.2 %copy-start.3 = (f32[6,16,16,128]{3,2,1,0:T(8,128)S(1)}, f32[6,16,16,128]{3,2,1,0:T(8,128)}, u32[]{:S(2)}) copy-start(f32[6,16,16,128]{3,2,1,0:T(8,128)} %memory.1) | copy-start | bytes 2359300
  43.4 2.1 %copy-start.4 = (f32[16,16,128]{2,1,0:T(8,128)S(1)}, f32[16,16,128]{2,1,0:T(8,128)}, u32[]{:S(2)}) copy-start(f32[16,16,128]{2,1,0:T(8,128)} %lam.3) | copy-start | bytes 393220
  43.4 2.1 %copy-start.5 = (f32[16,16,128]{2,1,0:T(8,128)S(1)}, f32[16,16,128]{2,1,0:T(8,128)}, u32[]{:S(2)}) copy-start(f32[16,16,128]{2,1,0:T(8,128)} %shear.3) | copy-start | bytes 393220
  48.5 11.9 %collective-permute-start.6 = (f32[10,16,128]{2,1,0:T(8,128)S(1)}, f32[10,16,128]{2,1,0:T(8,128)S(1)}, u32[]{:S(2)}, u32[]{:S(2)}) collective-permute-start(f32[10,16,128]{2,1,0:T(8,128)S(1)} %get-tuple-element.49.behind), channel_id=1, source_target_pairs={{0,32},{32,64},{64,96},{96,128},{128,160},{160,192},{192,224},{224... | collective-permute-start | bytes 245768 | tf_op jit(solution)/shard_map/ppermute | solution.py:371
  49.8 10.6 %collective-permute-start.7 = (f32[2,16,128]{2,1,0:T(8,128)S(1)}, f32[2,16,128]{2,1,0:T(8,128)S(1)}, u32[]{:S(2)}, u32[]{:S(2)}) collective-permute-start(f32[2,16,128]{2,1,0:T(8,128)S(1)} %get-tuple-element.50), channel_id=1, source_target_pairs={{0,1},{1,2},{2,3},{5,4},{6,5},{7,6},{8,9},{9,10},{10,11},{13,12},{... | collective-permute-start | bytes 49160 | tf_op jit(solution)/shard_map/ppermute | solution.py:372
  51.1 11.3 %collective-permute-start.8 = (f32[5,16,128]{2,1,0:T(8,128)S(1)}, f32[5,16,128]{2,1,0:T(8,128)S(1)}, u32[]{:S(2)}, u32[]{:S(2)}) collective-permute-start(f32[5,16,128]{2,1,0:T(8,128)S(1)} %get-tuple-element.51), channel_id=1, source_target_pairs={{4,8},{12,16},{20,24},{8,4},{16,12},{24,20},{5,9},{13,17},{21,25},... | collective-permute-start | bytes 122888 | tf_op jit(solution)/shard_map/ppermute | solution.py:373
  63.8 13.1 %copy-start.7 = (f32[3,16,16,128]{3,2,1,0:T(8,128)S(1)}, f32[3,16,16,128]{3,2,1,0:T(8,128)}, u32[]{:S(2)}) copy-start(f32[3,16,16,128]{3,2,1,0:T(8,128)} %get-tuple-element.29.velocity) | copy-start | bytes 1179652
  65.9 11.7 %collective-permute-start.9 = (f32[10,16,128]{2,1,0:T(8,128)S(1)}, f32[10,16,128]{2,1,0:T(8,128)S(1)}, u32[]{:S(2)}, u32[]{:S(2)}) collective-permute-start(f32[10,16,128]{2,1,0:T(8,128)S(1)} %get-tuple-element.55.behind), channel_id=1, source_target_pairs={{0,32},{32,64},{64,96},{96,128},{128,160},{160,192},{192,224},{224... | collective-permute-start | bytes 245768 | tf_op jit(solution)/shard_map/ppermute | solution.py:371
  67.2 10.2 %collective-permute-start.10 = (f32[2,16,128]{2,1,0:T(8,128)S(1)}, f32[2,16,128]{2,1,0:T(8,128)S(1)}, u32[]{:S(2)}, u32[]{:S(2)}) collective-permute-start(f32[2,16,128]{2,1,0:T(8,128)S(1)} %get-tuple-element.57), channel_id=1, source_target_pairs={{0,1},{1,2},{2,3},{5,4},{6,5},{7,6},{8,9},{9,10},{10,11},{13,12},{... | collective-permute-start | bytes 49160 | tf_op jit(solution)/shard_map/ppermute | solution.py:372
  68.5 11.1 %collective-permute-start.11 = (f32[5,16,128]{2,1,0:T(8,128)S(1)}, f32[5,16,128]{2,1,0:T(8,128)S(1)}, u32[]{:S(2)}, u32[]{:S(2)}) collective-permute-start(f32[5,16,128]{2,1,0:T(8,128)S(1)} %get-tuple-element.58), channel_id=1, source_target_pairs={{4,8},{12,16},{20,24},{8,4},{16,12},{24,20},{5,9},{13,17},{21,25},... | collective-permute-start | bytes 122888 | tf_op jit(solution)/shard_map/ppermute | solution.py:373

commit v8 on v7

--- a/solution.py
+++ b/solution.py
@@ -273,7 +273,11 @@
     pack(VELOCITY, out, core[0], own, given)
 
 
-def near_strain_kernel(core, velocity, pair, behind, out, rows):
+def near_strain_kernel(core, velocity, pair, behind, out, *refs):
+    *final, rows = refs
+    if final:
+        copy = pltpu.make_async_copy(velocity, final[0], final[1].at[0])
+        copy.start()
     near = Near(VELOCITY, velocity, core[0], pair, rows)
     for x in range(velocity.shape[1]):
         out[0, x] = near.dx(0, x)
@@ -282,6 +286,8 @@
         out[3, x] = near.dy(0, x) + near.dx(1, x)
         out[4, x] = near.dz(0, x) + near.dx(2, x)
         out[5, x] = near.dz(1, x) + near.dy(2, x)
+    if final:
+        copy.wait()
 
 
 def stress_kernel(send, core, near, stress, memory, lam, shear, decay, gain, limits, *refs):
@@ -334,7 +340,7 @@
         pack(STRESS, out, core[0], own, given)
 
 
-def call(body, outs, operands, scalars=1, scratch=(), hold=False, out_space=pltpu.VMEM):
+def call(body, outs, operands, scalars=1, scratch=(), hold=False, out_space=None):
     vmem = pl.BlockSpec(memory_space=pltpu.VMEM)
     specs = [pl.BlockSpec(memory_space=pltpu.SMEM)] * scalars
     specs += [vmem] * (len(operands) - scalars)
@@ -344,7 +350,7 @@
         body,
         out_shape=outs,
         in_specs=specs,
-        out_specs=[pl.BlockSpec(memory_space=out_space)] * len(outs),
+        out_specs=[pl.BlockSpec(memory_space=s) for s in out_space or [pltpu.VMEM] * len(outs)],
         scratch_shapes=list(scratch),
         cost_estimate=pl.CostEstimate(flops=2**22, bytes_accessed=2**22, transcendentals=0)
         if hold
@@ -371,10 +377,10 @@
     got_x = lax.ppermute(along_x, ("gx", "gy"), to_x)
     got_z = lax.ppermute(along_z, ("gy", "gz"), to_z)
     outer = lax.ppermute(along_y, "gy", to_y)
-    near = near_kernel(pair, along_x)
+    near, *rest = near_kernel(pair, along_x)
     (taken,) = call(join_kernel, [planes(TAKEN)], [got_x, got_z, near], scalars=0, hold=True)
     spread = lax.all_gather(taken, "gy", axis=0, tiled=True, axis_index_groups=cores)
-    return near, spread, outer, along_x
+    return near, spread, outer, along_x, rest
 
 
 def shards(
@@ -408,13 +414,20 @@
         def near_velocity(*got):
             operands = [core, stress, velocity, buoyancy, *got]
             outs = [like(velocity)]
-            return call(near_velocity_kernel, outs, operands, scratch=rows, hold=True)[0]
+            return call(near_velocity_kernel, outs, operands, scratch=rows, hold=True)
 
         def near_strain(*got):
-            outs = [like(stress)]
-            return call(near_strain_kernel, outs, [core, velocity, *got], scratch=rows, hold=True)[0]
-
-        near, spread, outer, along = exchange(core, own, given, near_velocity)
+            last = step == STEPS - 1
+            return call(
+                near_strain_kernel,
+                [like(stress), like(velocity)] if last else [like(stress)],
+                [core, velocity, *got],
+                scratch=[pltpu.SemaphoreType.DMA((1,))] + rows if last else rows,
+                hold=True,
+                out_space=[pltpu.VMEM, pl.ANY] if last else None,
+            )
+
+        near, spread, outer, along, _ = exchange(core, own, given, near_velocity)
         if step == 0:
             cells = call(
                 cells_kernel,
@@ -429,18 +442,18 @@
             [core, near, buoyancy, spread, outer],
             scratch=edges,
         )
-        near, spread, outer, _ = exchange(core, own, given, near_strain)
+        near, spread, outer, _, final = exchange(core, own, given, near_strain)
         send = step < STEPS - 1
         stress, memory, *rest = call(
             functools.partial(stress_kernel, send),
             [like(stress), like(memory)] + (packed if send else []),
             [core, near, stress, memory, lame_lambda, shear_modulus, *cells, spread, outer],
             scratch=(edges if send else held + edges) + terms,
-            out_space=pltpu.VMEM if send else pl.ANY,
+            out_space=None if send else [pl.ANY] * 2,
         )
         if send:
             own, given = rest
-    return (velocity, stress, memory)
+    return (final[0], stress, memory)
 
 
 def solution(mesh):

time: 81.8 us -> 81 us (level)
    unnamed x24 -> x22, local copies, waits for them, and re-layouts: 1.8 us -> 1.79 us
  transfers between devices with their start and end apart: 12 -> 12, of which waited for: 1 -> 0; matrix products, arithmetic and copies ran while one was open for 0% -> 0% of each run, Pallas kernels for 3% -> 4%
where the time goes in v8:
time: 81 us; the launch traced here: 80.4 us
  starting transfers between devices  48 us (59%)
  blocking collectives  22.3 us (28%)
  Pallas kernels  7.27 us (9%)
  local copies, waits for them, and re-layouts  1.79 us (2%)
  between operations  1.04 us (1%)
    ppermute x4, starting transfers between devices, exchange(): outer = lax.ppermute(along_y, 'gy', to_y)  37.4 us
    all_gather x4, blocking collectives, exchange(): lax.all_gather(given, 'gy', axis=0, tiled=True, axis_index_groups=cores)  14.4 us
    all_gather x4, blocking collectives, exchange(): lax.all_gather(taken, 'gy', axis=0, tiled=True, axis_index_groups=cores)  7.92 us
    pallas_call x18, Pallas kernels, call(): pl.pallas_call(body, out_shape=outs, in_specs=specs, out_specs=[pl.BlockS...  7.27 us
    ppermute x4, starting transfers between devices, exchange(): got_x = lax.ppermute(along_x, ('gx', 'gy'), to_x)  5.43 us
    ppermute x4, starting transfers between devices, exchange(): got_z = lax.ppermute(along_z, ('gy', 'gz'), to_z)  5.17 us
    unnamed x22, local copies, waits for them, and re-layouts  1.79 us
  transfers between devices with their start and end apart: 12, of which 0 were waited for; matrix products, arithmetic and copies ran while one was open for 0% of the time, Pallas kernels for 4%

profile of v8, /device:TPU:1, one launch (start us, length us, event | category | flops | bytes accessed | tf_op | source)
XLA Modules:
  0.0 80.4 jit_solution(14833199273287740590)
XLA Ops:
  0.7 1.1 %copy-done = f32[6,16,16,128]{3,2,1,0:T(8,128)S(1)} copy-done((f32[6,16,16,128]{3,2,1,0:T(8,128)S(1)}, f32[6,16,16,128]{3,2,1,0:T(8,128)}, u32[]{:S(2)}) %copy-start) | copy-done | bytes 786456
  2.1 8.6 %all_gather.24.pair = f32[22,16,128]{2,1,0:T(8,128)S(1)} all-gather(f32[11,16,128]{2,1,0:T(8,128)S(1)} %get-tuple-element.34), channel_id=1, replica_groups={{0,4},{8,12},{16,20},{24,28},{1,5},{9,13},{17,21},{25,29},{2,6},{10,14}..., dimensions={0}, use_global_device_ids=true | all-gather | bytes 270336 | tf_op jit(solution)/shard_map/all_gather | solution.py:367
  10.7 1.4 %collective-permute-start = (f32[10,16,128]{2,1,0:T(8,128)S(1)}, f32[10,16,128]{2,1,0:T(8,128)S(1)}, u32[]{:S(2)}, u32[]{:S(2)}) collective-permute-start(f32[10,16,128]{2,1,0:T(8,128)S(1)} %get-tuple-element.36.behind), channel_id=1, source_target_pairs={{0,32},{32,64},{64,96},{96,128},{128,160},{160,192},{192,224},{224... | collective-permute-start | bytes 245768 | tf_op jit(solution)/shard_map/ppermute | solution.py:377
  12.2 1.3 %collective-permute-start.1 = (f32[2,16,128]{2,1,0:T(8,128)S(1)}, f32[2,16,128]{2,1,0:T(8,128)S(1)}, u32[]{:S(2)}, u32[]{:S(2)}) collective-permute-start(f32[2,16,128]{2,1,0:T(8,128)S(1)} %get-tuple-element.37), channel_id=1, source_target_pairs={{0,1},{1,2},{2,3},{5,4},{6,5},{7,6},{8,9},{9,10},{10,11},{13,12},{... | collective-permute-start | bytes 49160 | tf_op jit(solution)/shard_map/ppermute | solution.py:378
  13.5 8.4 %collective-permute-start.2 = (f32[5,16,128]{2,1,0:T(8,128)S(1)}, f32[5,16,128]{2,1,0:T(8,128)S(1)}, u32[]{:S(2)}, u32[]{:S(2)}) collective-permute-start(f32[5,16,128]{2,1,0:T(8,128)S(1)} %get-tuple-element.38), channel_id=1, source_target_pairs={{4,8},{12,16},{20,24},{8,4},{16,12},{24,20},{5,9},{13,17},{21,25},... | collective-permute-start | bytes 122888 | tf_op jit(solution)/shard_map/ppermute | solution.py:379
  22.4 1.9 %all_gather.25.spread = f32[24,16,128]{2,1,0:T(8,128)S(1)} all-gather(f32[12,16,128]{2,1,0:T(8,128)S(1)} %shard_map.124), channel_id=1, replica_groups={{0,4},{8,12},{16,20},{24,28},{1,5},{9,13},{17,21},{25,29},{2,6},{10,14}..., dimensions={0}, use_global_device_ids=true | all-gather | bytes 294912 | tf_op jit(solution)/shard_map/all_gather | solution.py:382
  25.1 1.9 %all_gather.26.pair = f32[22,16,128]{2,1,0:T(8,128)S(1)} all-gather(f32[11,16,128]{2,1,0:T(8,128)S(1)} %get-tuple-element.40), channel_id=1, replica_groups={{0,4},{8,12},{16,20},{24,28},{1,5},{9,13},{17,21},{25,29},{2,6},{10,14}..., dimensions={0}, use_global_device_ids=true | all-gather | bytes 270336 | tf_op jit(solution)/shard_map/all_gather | solution.py:367
  27.0 1.4 %collective-permute-start.3 = (f32[10,16,128]{2,1,0:T(8,128)S(1)}, f32[10,16,128]{2,1,0:T(8,128)S(1)}, u32[]{:S(2)}, u32[]{:S(2)}) collective-permute-start(f32[10,16,128]{2,1,0:T(8,128)S(1)} %get-tuple-element.42.behind), channel_id=1, source_target_pairs={{0,32},{32,64},{64,96},{96,128},{128,160},{160,192},{192,224},{224... | collective-permute-start | bytes 245768 | tf_op jit(solution)/shard_map/ppermute | solution.py:377
  28.5 1.3 %collective-permute-start.4 = (f32[2,16,128]{2,1,0:T(8,128)S(1)}, f32[2,16,128]{2,1,0:T(8,128)S(1)}, u32[]{:S(2)}, u32[]{:S(2)}) collective-permute-start(f32[2,16,128]{2,1,0:T(8,128)S(1)} %get-tuple-element.46), channel_id=1, source_target_pairs={{0,1},{1,2},{2,3},{5,4},{6,5},{7,6},{8,9},{9,10},{10,11},{13,12},{... | collective-permute-start | bytes 49160 | tf_op jit(solution)/shard_map/ppermute | solution.py:378
  31.0 11.8 %collective-permute-start.5 = (f32[5,16,128]{2,1,0:T(8,128)S(1)}, f32[5,16,128]{2,1,0:T(8,128)S(1)}, u32[]{:S(2)}, u32[]{:S(2)}) collective-permute-start(f32[5,16,128]{2,1,0:T(8,128)S(1)} %get-tuple-element.47), channel_id=1, source_target_pairs={{4,8},{12,16},{20,24},{8,4},{16,12},{24,20},{5,9},{13,17},{21,25},... | collective-permute-start | bytes 122888 | tf_op jit(solution)/shard_map/ppermute | solution.py:379
  43.4 2.1 %all_gather.27.refs_0_ = f32[24,16,128]{2,1,0:T(8,128)S(1)} all-gather(f32[12,16,128]{2,1,0:T(8,128)S(1)} %shard_map.129), channel_id=1, replica_groups={{0,4},{8,12},{16,20},{24,28},{1,5},{9,13},{17,21},{25,29},{2,6},{10,14}..., dimensions={0}, use_global_device_ids=true | all-gather | bytes 294912 | tf_op jit(solution)/shard_map/all_gather | solution.py:382
  45.5 1.1 %shard_map.130 = (f32[6,16,16,128]{3,2,1,0:T(8,128)S(1)}, f32[6,16,16,128]{3,2,1,0:T(8,128)S(1)}, f32[11,16,128]{2,1,0:T(8,128)S(1)}, f32[11,16,128]{2,1,0:T(8,128)S(1)}) custom-call(s32[1]{0:T(128)} %bitcast.core, f32[6,16,16,128]{3,2,1,0:T(8,128)S(1)} %shard_map.127.near, f32[6,16,16,128]{3,2,1,0:T(8,128)S(1)} %copy-done.1, ...), custom_call_target="tpu_custom_call" | custom-call | tf_op jit(solution)/shard_map/pallas_call | solution.py:349
  46.6 1.9 %all_gather.28.pair = f32[22,16,128]{2,1,0:T(8,128)S(1)} all-gather(f32[11,16,128]{2,1,0:T(8,128)S(1)} %get-tuple-element.49), channel_id=1, replica_groups={{0,4},{8,12},{16,20},{24,28},{1,5},{9,13},{17,21},{25,29},{2,6},{10,14}..., dimensions={0}, use_global_device_ids=true | all-gather | bytes 270336 | tf_op jit(solution)/shard_map/all_gather | solution.py:367
  48.5 1.3 %collective-permute-start.6 = (f32[10,16,128]{2,1,0:T(8,128)S(1)}, f32[10,16,128]{2,1,0:T(8,128)S(1)}, u32[]{:S(2)}, u32[]{:S(2)}) collective-permute-start(f32[10,16,128]{2,1,0:T(8,128)S(1)} %get-tuple-element.51.behind), channel_id=1, source_target_pairs={{0,32},{32,64},{64,96},{96,128},{128,160},{160,192},{192,224},{224... | collective-permute-start | bytes 245768 | tf_op jit(solution)/shard_map/ppermute | solution.py:377
  49.8 1.3 %collective-permute-start.7 = (f32[2,16,128]{2,1,0:T(8,128)S(1)}, f32[2,16,128]{2,1,0:T(8,128)S(1)}, u32[]{:S(2)}, u32[]{:S(2)}) collective-permute-start(f32[2,16,128]{2,1,0:T(8,128)S(1)} %get-tuple-element.52), channel_id=1, source_target_pairs={{0,1},{1,2},{2,3},{5,4},{6,5},{7,6},{8,9},{9,10},{10,11},{13,12},{... | collective-permute-start | bytes 49160 | tf_op jit(solution)/shard_map/ppermute | solution.py:378
  51.1 8.8 %collective-permute-start.8 = (f32[5,16,128]{2,1,0:T(8,128)S(1)}, f32[5,16,128]{2,1,0:T(8,128)S(1)}, u32[]{:S(2)}, u32[]{:S(2)}) collective-permute-start(f32[5,16,128]{2,1,0:T(8,128)S(1)} %get-tuple-element.53), channel_id=1, source_target_pairs={{4,8},{12,16},{20,24},{8,4},{16,12},{24,20},{5,9},{13,17},{21,25},... | collective-permute-start | bytes 122888 | tf_op jit(solution)/shard_map/ppermute | solution.py:379
  60.5 1.9 %all_gather.29.spread = f32[24,16,128]{2,1,0:T(8,128)S(1)} all-gather(f32[12,16,128]{2,1,0:T(8,128)S(1)} %shard_map.133), channel_id=1, replica_groups={{0,4},{8,12},{16,20},{24,28},{1,5},{9,13},{17,21},{25,29},{2,6},{10,14}..., dimensions={0}, use_global_device_ids=true | all-gather | bytes 294912 | tf_op jit(solution)/shard_map/all_gather | solution.py:382
  63.1 1.9 %all_gather.30.pair = f32[22,16,128]{2,1,0:T(8,128)S(1)} all-gather(f32[11,16,128]{2,1,0:T(8,128)S(1)} %get-tuple-element.55), channel_id=1, replica_groups={{0,4},{8,12},{16,20},{24,28},{1,5},{9,13},{17,21},{25,29},{2,6},{10,14}..., dimensions={0}, use_global_device_ids=true | all-gather | bytes 270336 | tf_op jit(solution)/shard_map/all_gather | solution.py:367
  65.1 1.3 %collective-permute-start.9 = (f32[10,16,128]{2,1,0:T(8,128)S(1)}, f32[10,16,128]{2,1,0:T(8,128)S(1)}, u32[]{:S(2)}, u32[]{:S(2)}) collective-permute-start(f32[10,16,128]{2,1,0:T(8,128)S(1)} %get-tuple-element.57.behind), channel_id=1, source_target_pairs={{0,32},{32,64},{64,96},{96,128},{128,160},{160,192},{192,224},{224... | collective-permute-start | bytes 245768 | tf_op jit(solution)/shard_map/ppermute | solution.py:377
  66.4 1.3 %collective-permute-start.10 = (f32[2,16,128]{2,1,0:T(8,128)S(1)}, f32[2,16,128]{2,1,0:T(8,128)S(1)}, u32[]{:S(2)}, u32[]{:S(2)}) collective-permute-start(f32[2,16,128]{2,1,0:T(8,128)S(1)} %get-tuple-element.61), channel_id=1, source_target_pairs={{0,1},{1,2},{2,3},{5,4},{6,5},{7,6},{8,9},{9,10},{10,11},{13,12},{... | collective-permute-start | bytes 49160 | tf_op jit(solution)/shard_map/ppermute | solution.py:378
  67.7 8.4 %collective-permute-start.11 = (f32[5,16,128]{2,1,0:T(8,128)S(1)}, f32[5,16,128]{2,1,0:T(8,128)S(1)}, u32[]{:S(2)}, u32[]{:S(2)}) collective-permute-start(f32[5,16,128]{2,1,0:T(8,128)S(1)} %get-tuple-element.62), channel_id=1, source_target_pairs={{4,8},{12,16},{20,24},{8,4},{16,12},{24,20},{5,9},{13,17},{21,25},... | collective-permute-start | bytes 122888 | tf_op jit(solution)/shard_map/ppermute | solution.py:379
  76.1 0.8 shard_map.136
  76.9 1.9 %all_gather.31.refs_0_ = f32[24,16,128]{2,1,0:T(8,128)S(1)} all-gather(f32[12,16,128]{2,1,0:T(8,128)S(1)} %shard_map.137), channel_id=1, replica_groups={{0,4},{8,12},{16,20},{24,28},{1,5},{9,13},{17,21},{25,29},{2,6},{10,14}..., dimensions={0}, use_global_device_ids=true | all-gather | bytes 294912 | tf_op jit(solution)/shard_map/all_gather | solution.py:382
  78.8 1.6 %shard_map.138 = (f32[6,16,16,128]{3,2,1,0:T(8,128)}, f32[6,16,16,128]{3,2,1,0:T(8,128)}) custom-call(s32[1]{0:T(128)} %bitcast.core, f32[6,16,16,128]{3,2,1,0:T(8,128)S(1)} %get-tuple-element.59.near, f32[6,16,16,128]{3,2,1,0:T(8,128)S(1)} %get-tuple-element.48.stress, f32[6,16,16,128]{3,2,1,0:T(8,128)S(1)} %get-tuple-element.60.memory, ...), custom_call_target="tpu_custom_call" | custom-call | tf_op jit(solution)/shard_map/pallas_call | solution.py:349
  (48 shorter events, 4.6 us)
Async XLA Ops:
  0.6 1.1 %copy-start = (f32[6,16,16,128]{3,2,1,0:T(8,128)S(1)}, f32[6,16,16,128]{3,2,1,0:T(8,128)}, u32[]{:S(2)}) copy-start(f32[6,16,16,128]{3,2,1,0:T(8,128)} %stress.5) | copy-start | bytes 2359300
  1.8 20.1 %copy-start.1 = (f32[6,16,16,128]{3,2,1,0:T(8,128)S(1)}, f32[6,16,16,128]{3,2,1,0:T(8,128)}, u32[]{:S(2)}) copy-start(f32[6,16,16,128]{3,2,1,0:T(8,128)} %stress.5) | copy-start | bytes 2359300
  2.1 19.8 %copy-start.6 = (f32[3,16,16,128]{3,2,1,0:T(8,128)S(1)}, f32[3,16,16,128]{3,2,1,0:T(8,128)}, u32[]{:S(2)}) copy-start(f32[3,16,16,128]{3,2,1,0:T(8,128)} %velocity.1) | copy-start | bytes 1179652
  10.7 11.2 %copy-start.2 = (f32[16,16,128]{2,1,0:T(8,128)S(1)}, f32[16,16,128]{2,1,0:T(8,128)}, u32[]{:S(2)}) copy-start(f32[16,16,128]{2,1,0:T(8,128)} %buoyancy.7) | copy-start | bytes 393220
  10.7 11.7 %collective-permute-start = (f32[10,16,128]{2,1,0:T(8,128)S(1)}, f32[10,16,128]{2,1,0:T(8,128)S(1)}, u32[]{:S(2)}, u32[]{:S(2)}) collective-permute-start(f32[10,16,128]{2,1,0:T(8,128)S(1)} %get-tuple-element.36.behind), channel_id=1, source_target_pairs={{0,32},{32,64},{64,96},{96,128},{128,160},{160,192},{192,224},{224... | collective-permute-start | bytes 245768 | tf_op jit(solution)/shard_map/ppermute | solution.py:377
  12.2 10.2 %collective-permute-start.1 = (f32[2,16,128]{2,1,0:T(8,128)S(1)}, f32[2,16,128]{2,1,0:T(8,128)S(1)}, u32[]{:S(2)}, u32[]{:S(2)}) collective-permute-start(f32[2,16,128]{2,1,0:T(8,128)S(1)} %get-tuple-element.37), channel_id=1, source_target_pairs={{0,1},{1,2},{2,3},{5,4},{6,5},{7,6},{8,9},{9,10},{10,11},{13,12},{... | collective-permute-start | bytes 49160 | tf_op jit(solution)/shard_map/ppermute | solution.py:378
  13.5 10.9 %collective-permute-start.2 = (f32[5,16,128]{2,1,0:T(8,128)S(1)}, f32[5,16,128]{2,1,0:T(8,128)S(1)}, u32[]{:S(2)}, u32[]{:S(2)}) collective-permute-start(f32[5,16,128]{2,1,0:T(8,128)S(1)} %get-tuple-element.38), channel_id=1, source_target_pairs={{4,8},{12,16},{20,24},{8,4},{16,12},{24,20},{5,9},{13,17},{21,25},... | collective-permute-start | bytes 122888 | tf_op jit(solution)/shard_map/ppermute | solution.py:379
  27.0 2.8 %copy-start.7 = (s32[16,16,128]{2,1,0:T(8,128)S(1)}, s32[16,16,128]{2,1,0:T(8,128)}, u32[]{:S(2)}) copy-start(s32[16,16,128]{2,1,0:T(8,128)} %mech.1) | copy-start | bytes 393220
  27.0 2.8 %copy-start.8 = (f32[16,16,128]{2,1,0:T(8,128)S(1)}, f32[16,16,128]{2,1,0:T(8,128)}, u32[]{:S(2)}) copy-start(f32[16,16,128]{2,1,0:T(8,128)} %weight.1) | copy-start | bytes 393220
  27.0 2.8 %copy-start.9 = (s32[16,16]{1,0:T(8,128)S(1)}, s32[16,16]{1,0:T(8,128)}, u32[]{:S(2)}) copy-start(s32[16,16]{1,0:T(8,128)} %top.1) | copy-start | bytes 3076
  27.0 16.3 %collective-permute-start.3 = (f32[10,16,128]{2,1,0:T(8,128)S(1)}, f32[10,16,128]{2,1,0:T(8,128)S(1)}, u32[]{:S(2)}, u32[]{:S(2)}) collective-permute-start(f32[10,16,128]{2,1,0:T(8,128)S(1)} %get-tuple-element.42.behind), channel_id=1, source_target_pairs={{0,32},{32,64},{64,96},{96,128},{128,160},{160,192},{192,224},{224... | collective-permute-start | bytes 245768 | tf_op jit(solution)/shard_map/ppermute | solution.py:377
  28.5 14.9 %collective-permute-start.4 = (f32[2,16,128]{2,1,0:T(8,128)S(1)}, f32[2,16,128]{2,1,0:T(8,128)S(1)}, u32[]{:S(2)}, u32[]{:S(2)}) collective-permute-start(f32[2,16,128]{2,1,0:T(8,128)S(1)} %get-tuple-element.46), channel_id=1, source_target_pairs={{0,1},{1,2},{2,3},{5,4},{6,5},{7,6},{8,9},{9,10},{10,11},{13,12},{... | collective-permute-start | bytes 49160 | tf_op jit(solution)/shard_map/ppermute | solution.py:378
  29.8 0.7 copy-start.10
  31.0 14.5 %collective-permute-start.5 = (f32[5,16,128]{2,1,0:T(8,128)S(1)}, f32[5,16,128]{2,1,0:T(8,128)S(1)}, u32[]{:S(2)}, u32[]{:S(2)}) collective-permute-start(f32[5,16,128]{2,1,0:T(8,128)S(1)} %get-tuple-element.47), channel_id=1, source_target_pairs={{4,8},{12,16},{20,24},{8,4},{16,12},{24,20},{5,9},{13,17},{21,25},... | collective-permute-start | bytes 122888 | tf_op jit(solution)/shard_map/ppermute | solution.py:379
  43.3 2.2 %copy-start.3 = (f32[6,16,16,128]{3,2,1,0:T(8,128)S(1)}, f32[6,16,16,128]{3,2,1,0:T(8,128)}, u32[]{:S(2)}) copy-start(f32[6,16,16,128]{3,2,1,0:T(8,128)} %memory.1) | copy-start | bytes 2359300
  43.4 2.1 %copy-start.4 = (f32[16,16,128]{2,1,0:T(8,128)S(1)}, f32[16,16,128]{2,1,0:T(8,128)}, u32[]{:S(2)}) copy-start(f32[16,16,128]{2,1,0:T(8,128)} %lam.3) | copy-start | bytes 393220
  43.4 2.1 %copy-start.5 = (f32[16,16,128]{2,1,0:T(8,128)S(1)}, f32[16,16,128]{2,1,0:T(8,128)}, u32[]{:S(2)}) copy-start(f32[16,16,128]{2,1,0:T(8,128)} %shear.3) | copy-start | bytes 393220
  48.5 11.9 %collective-permute-start.6 = (f32[10,16,128]{2,1,0:T(8,128)S(1)}, f32[10,16,128]{2,1,0:T(8,128)S(1)}, u32[]{:S(2)}, u32[]{:S(2)}) collective-permute-start(f32[10,16,128]{2,1,0:T(8,128)S(1)} %get-tuple-element.51.behind), channel_id=1, source_target_pairs={{0,32},{32,64},{64,96},{96,128},{128,160},{160,192},{192,224},{224... | collective-permute-start | bytes 245768 | tf_op jit(solution)/shard_map/ppermute | solution.py:377
  49.8 10.6 %collective-permute-start.7 = (f32[2,16,128]{2,1,0:T(8,128)S(1)}, f32[2,16,128]{2,1,0:T(8,128)S(1)}, u32[]{:S(2)}, u32[]{:S(2)}) collective-permute-start(f32[2,16,128]{2,1,0:T(8,128)S(1)} %get-tuple-element.52), channel_id=1, source_target_pairs={{0,1},{1,2},{2,3},{5,4},{6,5},{7,6},{8,9},{9,10},{10,11},{13,12},{... | collective-permute-start | bytes 49160 | tf_op jit(solution)/shard_map/ppermute | solution.py:378
  51.1 11.3 %collective-permute-start.8 = (f32[5,16,128]{2,1,0:T(8,128)S(1)}, f32[5,16,128]{2,1,0:T(8,128)S(1)}, u32[]{:S(2)}, u32[]{:S(2)}) collective-permute-start(f32[5,16,128]{2,1,0:T(8,128)S(1)} %get-tuple-element.53), channel_id=1, source_target_pairs={{4,8},{12,16},{20,24},{8,4},{16,12},{24,20},{5,9},{13,17},{21,25},... | collective-permute-start | bytes 122888 | tf_op jit(solution)/shard_map/ppermute | solution.py:379
  65.1 11.8 %collective-permute-start.9 = (f32[10,16,128]{2,1,0:T(8,128)S(1)}, f32[10,16,128]{2,1,0:T(8,128)S(1)}, u32[]{:S(2)}, u32[]{:S(2)}) collective-permute-start(f32[10,16,128]{2,1,0:T(8,128)S(1)} %get-tuple-element.57.behind), channel_id=1, source_target_pairs={{0,32},{32,64},{64,96},{96,128},{128,160},{160,192},{192,224},{224... | collective-permute-start | bytes 245768 | tf_op jit(solution)/shard_map/ppermute | solution.py:377
  66.4 10.5 %collective-permute-start.10 = (f32[2,16,128]{2,1,0:T(8,128)S(1)}, f32[2,16,128]{2,1,0:T(8,128)S(1)}, u32[]{:S(2)}, u32[]{:S(2)}) collective-permute-start(f32[2,16,128]{2,1,0:T(8,128)S(1)} %get-tuple-element.61), channel_id=1, source_target_pairs={{0,1},{1,2},{2,3},{5,4},{6,5},{7,6},{8,9},{9,10},{10,11},{13,12},{... | collective-permute-start | bytes 49160 | tf_op jit(solution)/shard_map/ppermute | solution.py:378
  67.7 11.2 %collective-permute-start.11 = (f32[5,16,128]{2,1,0:T(8,128)S(1)}, f32[5,16,128]{2,1,0:T(8,128)S(1)}, u32[]{:S(2)}, u32[]{:S(2)}) collective-permute-start(f32[5,16,128]{2,1,0:T(8,128)S(1)} %get-tuple-element.62), channel_id=1, source_target_pairs={{4,8},{12,16},{20,24},{8,4},{16,12},{24,20},{5,9},{13,17},{21,25},... | collective-permute-start | bytes 122888 | tf_op jit(solution)/shard_map/ppermute | solution.py:379
